TPU v7x, 32 devices: a whole 2x2x4 slice. The times are simulated.
32 devices in a mesh: row: 8 (over y, x, core), col: 4 (over z).
Axes of the slice: x: 2, y: 2, z: 4, core: 2. Of those that a mesh axis runs over, the one named last changes fastest.
Arguments:
- support: bfloat16 [8192, 4096], P(('row', 'col')), may hold values from -6 to 6
- targets: bfloat16 [256, 4096], P('col'), may hold values from -6 to 6
- panels: float32 [2, 128, 8192], P(None, None, ('row', 'col')), may hold values from -0.21875 to 0.21875
- diag_inverses: float32 [2, 128, 128], replicated, may hold values from -1 to 1.5, as said below
Outputs:
- solved: float32 [256, 8192], P('col', 'row')
Inputs may be any that keep to these rules, and one draw needn't show every extreme that they name: Each diag_inverses[k] is lower triangular.
All inputs are finite; a program needn't handle non-finite values.
Results may differ from a plain program's by a relative error of at most 0.0003.
Values may be sent and summed in bfloat16 or wider, within the bound.
No kernel may reach another device: no remote copies, remote signals or barrier semaphores. Data moves between devices by JAX's collectives and lax.ppermute only.
A program may use at most 64 MiB of HBM per device.

v0:
```python
import math

import jax
import jax.numpy as jnp
from jax import lax
from jax.sharding import PartitionSpec as P


def spread(value, axis, root):
    mine = lax.axis_index(axis) == root
    return lax.psum(jnp.where(mine, value, jnp.zeros_like(value)), axis)


def solve_head(pivot_cols, inverse):
    return jnp.dot(
        pivot_cols, inverse.T, precision=lax.Precision.HIGHEST, preferred_element_type=jnp.float32
    )


def apply_panel(current, solved_head, panel_cols):
    return current - jnp.dot(
        solved_head, panel_cols, precision=lax.Precision.HIGHEST, preferred_element_type=jnp.float32
    )


def shards(support, targets, panels, diag_inverses):
    feature_width = support.shape[1]
    kernel_scale = 0.5 / math.sqrt(feature_width)
    pivot_width = diag_inverses.shape[1]
    row_pos = lax.axis_index("row")
    products = jnp.einsum(
        "tf,sf->ts",
        lax.all_gather(targets, "col", axis=0, tiled=True),
        support,
        preferred_element_type=jnp.float32,
    )
    strip_tile = jnp.exp(kernel_scale * products)
    grid_tile = lax.all_to_all(strip_tile, "col", split_axis=0, concat_axis=1, tiled=True)
    panel_grid = lax.all_gather(panels, "col", axis=2, tiled=True)
    for panel_num in range(2):
        pivot_cols = grid_tile[:, :pivot_width]
        solved_head = spread(solve_head(pivot_cols, diag_inverses[panel_num]), "row", panel_num)
        updated = apply_panel(grid_tile, solved_head, panel_grid[panel_num])
        new_head = jnp.where(
            row_pos == panel_num,
            solved_head,
            jnp.where(row_pos < panel_num, pivot_cols, updated[:, :pivot_width]),
        )
        grid_tile = updated.at[:, :pivot_width].set(new_head)
    return grid_tile


def solution(mesh):
    in_specs = (P(("row", "col"), None), P("col", None), P(None, None, ("row", "col")), P())
    out_specs = P("col", "row")
    return jax.shard_map(shards, mesh=mesh, in_specs=in_specs, out_specs=out_specs, check_vma=False)
```

profile of v0, /device:TPU:0, one launch (start us, length us, event | category | flops | bytes accessed | tf_op | source)
XLA Modules:
  0.0 138.7 jit_solution(10334743609780325366)
XLA Ops:
  6.5 0.0 copy-start
  6.5 0.0 all-gather.3.cloned.1.call-start
  6.5 0.7 all-gather.3.cloned.1.call-update
  7.3 0.0 all-gather.5.cloned.1.call-start
  7.3 0.7 all-gather.5.cloned.1.call-update
  8.0 0.0 copy-start.1
  8.0 49.6 %all-gather.3.cloned.1.call-done = bf16[256,4096]{1,0:T(8,128)(2,1)} async-done(((bf16[64,4096]{1,0:T(8,128)(2,1)}), bf16[256,4096]{1,0:T(8,128)(2,1)}) %all-gather.3.cloned.1.call-update) | async-done | bytes 2097168 | tf_op jit(solution)/shard_map/all_gather | solution.py:33
  57.6 0.0 copy-done
  57.6 3.0 %fusion = f32[256,256]{1,0:T(8,128)} fusion(bf16[256,4096]{1,0:T(8,128)(2,1)} %all-gather.3.cloned.1.call-done, bf16[256,4096]{1,0:T(8,128)(2,1)S(1)} %copy-done), kind=kOutput, calls=%fused_computation.3 | convolution fusion | flops 536936448 | bytes 4456448 | tf_op jit(solution)/shard_map/tf,sf->ts/dot_general | solution.py:31
  60.6 3.4 %all-to-all-start = ((f32[4,64,256]{2,1,0:T(8,128)}), f32[4,64,256]{2,1,0:T(8,128)S(1)}, u32[]{:S(2)}, u32[]{:S(2)}) async-start(f32[4,64,256]{2,1,0:T(8,128)} %bitcast), calls=%async_computation | async-start | bytes 524288 | tf_op jit(solution)/shard_map/all_to_all | solution.py:38
  64.1 0.7 compare_reduce_fusion
  64.8 14.8 %all-to-all-done = f32[4,64,256]{2,1,0:T(8,128)S(1)} async-done(((f32[4,64,256]{2,1,0:T(8,128)}), f32[4,64,256]{2,1,0:T(8,128)S(1)}, u32[]{:S(2)}, u32[]{:S(2)}) %all-to-all-start) | async-done | bytes 262176 | tf_op jit(solution)/shard_map/all_to_all | solution.py:38
  79.6 0.0 copy-done.1
  79.6 0.2 convolution_select_fusion.1
  79.8 23.2 %psum.14 = f32[64,128]{1,0:T(8,128)S(1)} all-reduce(f32[64,128]{1,0:T(8,128)S(1)} %convolution_select_fusion.1), channel_id=1, replica_groups=mesh['row'=8,'col'=4] {'row'}, use_global_device_ids=true, to_apply=%region_0.1 | all-reduce | flops 8192 | bytes 65536 | tf_op jit(solution)/shard_map/psum | solution.py:11
  103.0 0.0 all-gather.5.cloned.1.call-done
  103.0 1.5 %convolution_subtract_fusion.1 = f32[64,1024]{1,0:T(8,128)S(1)} fusion(f32[64,1024]{1,0:T(8,128)S(1)} %bitcast.22, f32[64,128]{1,0:T(8,128)S(1)} %psum.14, f32[2,128,1024]{2,1,0:T(8,128)} %all-gather.5.cloned.1.call-done), kind=kOutput, calls=%fused_computation.1 | convolution fusion | flops 100728832 | bytes 1081344 | tf_op jit(solution)/shard_map/dot_general | solution.py:21
  104.4 0.6 constant_dynamic-update-slice_fusion
  105.1 0.2 convolution_select_fusion
  105.3 22.4 %psum.15 = f32[64,128]{1,0:T(8,128)S(1)} all-reduce(f32[64,128]{1,0:T(8,128)S(1)} %convolution_select_fusion), channel_id=1, replica_groups=mesh['row'=8,'col'=4] {'row'}, use_global_device_ids=true, to_apply=%region_2.3 | all-reduce | flops 8192 | bytes 65536 | tf_op jit(solution)/shard_map/psum | solution.py:11
  127.7 2.2 %convolution_subtract_fusion = f32[64,1024]{1,0:T(8,128)} fusion(f32[64,1024]{1,0:T(8,128)S(1)} %get-tuple-element.29, f32[64,128]{1,0:T(8,128)S(1)} %psum.15, f32[2,128,1024]{2,1,0:T(8,128)} %all-gather.5.cloned.1.call-done), kind=kOutput, calls=%fused_computation | convolution fusion | flops 100728832 | bytes 1081344 | tf_op jit(solution)/shard_map/dot_general | solution.py:21
  129.9 2.0 %select_dynamic-update-slice_fusion = f32[64,1024]{1,0:T(8,128)} fusion(f32[64,1024]{1,0:T(8,128)} %convolution_subtract_fusion, f32[64,128]{1,0:T(8,128)S(1)} %psum.15, f32[64,128]{1,0:T(8,128)S(1)} %get-tuple-element.30, pred[]{:T(512)S(6)} %lt.7, pred[]{:T(512)S(6)} %eq.9, pred[]{:T(512)} %compare_reduce_fusion), kind=kLoop, calls=%fused_computation.12 | loop fusion | flops 24576 | bytes 131586 | tf_op jit(solution)/shard_map/scatter | solution.py:49
  (1 shorter events, 0.0 us)
Async XLA Ops:
  6.5 51.1 %copy-start = (bf16[256,4096]{1,0:T(8,128)(2,1)S(1)}, bf16[256,4096]{1,0:T(8,128)(2,1)}, u32[]{:S(2)}) copy-start(bf16[256,4096]{1,0:T(8,128)(2,1)} %param.8) | copy-start | bytes 6291460
  6.5 51.1 %all-gather.3.cloned.1.call-start = ((), (), s32[]{:S(2)}) async-start(), calls=%async_computation.1 | async-start | bytes 2621440 | tf_op jit(solution)/shard_map/all_gather | solution.py:33
  7.3 95.7 %all-gather.5.cloned.1.call-start = ((), (), s32[]{:S(2)}) async-start(), calls=%async_computation.2 | async-start | bytes 1310720 | tf_op jit(solution)/shard_map/all_gather | solution.py:39
  8.0 71.5 %copy-start.1 = (f32[2,128,128]{2,1,0:T(8,128)S(1)}, f32[2,128,128]{2,1,0:T(8,128)}, u32[]{:S(2)}) copy-start(f32[2,128,128]{2,1,0:T(8,128)} %param.11) | copy-start | bytes 393220
  60.6 18.9 %all-to-all-start = ((f32[4,64,256]{2,1,0:T(8,128)}), f32[4,64,256]{2,1,0:T(8,128)S(1)}, u32[]{:S(2)}, u32[]{:S(2)}) async-start(f32[4,64,256]{2,1,0:T(8,128)} %bitcast), calls=%async_computation | async-start | bytes 524288 | tf_op jit(solution)/shard_map/all_to_all | solution.py:38
Sparse Core Ops, SparseCore 0:
  8.9 48.6 all-gather.2
  59.2 31.2 all-gather.4
where the time goes:
time: 139 us
  waiting for transfers between devices  65.7 us (47%)
  blocking collectives  45.5 us (33%)
  between operations  13.5 us (10%)
  matrix products  7.16 us (5%)
  starting transfers between devices  3.45 us (2%)
  other arithmetic  3.36 us (2%)
    all_gather x1, waiting for transfers between devices, shards(): lax.all_gather(targets, 'col', axis=0, tiled=True)  49.6 us
    psum x2, blocking collectives, spread(): return lax.psum(jnp.where(mine, value, jnp.zeros_like(value)), axis)  45.5 us
    all_to_all x1, waiting for transfers between devices, shards(): lax.all_to_all(strip_tile, 'col', split_axis=0, concat_axis=1, tiled=True)  14.8 us
    dot_general x2, matrix products, apply_panel(): jnp.dot(solved_head, panel_cols, precision=lax.Precision.HIGHEST, preferr...  3.64 us
    all_to_all x1, starting transfers between devices, shards(): lax.all_to_all(strip_tile, 'col', split_axis=0, concat_axis=1, tiled=True)  3.41 us
    dot_general x1, matrix products, shards(): jnp.einsum('tf,sf->ts', lax.all_gather(targets, 'col', axis=0, tiled=True...  3.04 us
  transfers between devices with their start and end apart: 3, of which 2 were waited for; matrix products, arithmetic and copies ran while one was open for 3% of the time, Pallas kernels for 0%

commit v1 on v0

v1 whole, which is shorter than its diff:
```python
import functools
import math

import jax
import jax.numpy as jnp
from jax import lax
from jax.experimental import pallas as pl
from jax.experimental.pallas import tpu as pltpu
from jax.sharding import PartitionSpec as P

VMEM = pl.BlockSpec(memory_space=pltpu.VMEM)
HBM = pl.BlockSpec(memory_space=pltpu.HBM)
PARAMS = pltpu.CompilerParams(vmem_limit_bytes=60 * 2**20)
LONG = pl.CostEstimate(flops=50_000_000_000, bytes_accessed=0, transcendentals=0)
SHORT = pl.CostEstimate(flops=1_000_000, bytes_accessed=0, transcendentals=0)
PANEL_UNIT = 2.0**17
NT = (((1,), (1,)), ((), ()))
TN = (((0,), (0,)), ((), ()))
NN = (((1,), (0,)), ((), ()))


def dot(a, b, dims):
    return lax.dot_general(a, b, dims, preferred_element_type=jnp.float32)


def halves(a):
    high = a.astype(jnp.bfloat16)
    return high, (a - high.astype(jnp.float32)).astype(jnp.bfloat16)


def dot32(a, b, dims):
    (a_high, a_low), (b_high, b_low) = halves(a), halves(b)
    return dot(a_high, b_high, dims) + (dot(a_low, b_high, dims) + dot(a_high, b_low, dims))


def slice_of(row, n_row):
    return (row % 2) * (n_row // 2) + row // 2


def start_all(pairs, sems):
    copies = [pltpu.make_async_copy(source, target, sems.at[i]) for i, (source, target) in enumerate(pairs)]
    for copy in copies:
        copy.start()
    return copies


def wait_all(copies):
    for copy in copies:
        copy.wait()


def corner_kernel(corner_ref, out_ref):
    out_ref[...] = corner_ref[0]


def tile_kernel(scale, n_row, n_col, *refs):
    own_hbm, support_hbm, sibling_hbm, corner_ref, inverse_ref = refs[:5]
    near, far, refs = refs[5:7], refs[7:7 + n_row], refs[7 + n_row:]
    outs, (targets_ref, support_ref, sems) = refs[:n_col], refs[n_col:]
    (rows, features), (_, width) = own_hbm.shape, far[0].shape
    span, pivot = support_hbm.shape[0], corner_ref.shape[1]
    half = features // 2
    row, col = lax.axis_index("row"), lax.axis_index("col")
    odd = row % 2
    steps = []
    for core in range(2):
        cols = pl.ds(pl.multiple_of((odd ^ core) * half, half), half)
        loads = [
            (own_hbm.at[:, cols], targets_ref.at[pl.ds(0, rows), cols]),
            (support_hbm.at[:, cols], support_ref.at[pl.ds(0, span), cols]),
            (sibling_hbm.at[pl.ds(0, pivot), cols], support_ref.at[pl.ds(span, pivot), cols]),
            (near[core], targets_ref.at[pl.ds(rows, rows), cols]),
        ]
        for step in range(core, n_row, 2):
            inner = pl.ds(pl.multiple_of(slice_of(row ^ step, n_row) * width, width), width)
            loads.append((far[step], targets_ref.at[pl.ds(2 * rows, far[step].shape[0]), inner]))
        steps.append((cols, start_all(loads, sems.at[core])))
    total = 0.0
    for cols, copies in steps:
        wait_all(copies)
        total = total + dot(targets_ref[:, cols], support_ref[:, cols], NT)
    kernel = jnp.exp(scale * total)
    other = jnp.where(odd == 1, kernel[:, span:], 0.0)
    head = kernel[:, :pivot] - dot32(dot32(other, inverse_ref[0], NT), corner_ref[...], NN)
    head = dot32(head, inverse_ref[odd], NT)
    for plane in range(n_col):
        part = slice(plane * rows, (plane + 1) * rows)
        outs[plane][:, :span] = kernel[part, :span]
        outs[plane][:, span:] = head[part]


def solve_kernel(n_col, pivot, *refs):
    tiles, (own_ref, panels_ref, mine_ref, other_ref, out_ref) = refs[:n_col], refs[n_col:]
    span = own_ref.shape[2]
    row, col = lax.axis_index("row"), lax.axis_index("col")
    even = row % 2 == 0
    mine, other = mine_ref[...], other_ref[...]
    first = jnp.where(even, mine, other)
    second = jnp.where(even, other, mine)
    for step in range(n_col):
        plane = col ^ step
        block = own_ref if step == 0 else panels_ref.at[plane]
        value = tiles[step][:, :span] - dot32(first, block[0], NN) - dot32(second, block[1], NN)
        out_ref[:, pl.ds(pl.multiple_of(plane * span, span), span)] = value

    @pl.when(row == 0)
    def _():
        out_ref[:, :pivot] = first

    @pl.when(row == 1)
    def _():
        out_ref[:, :pivot] = second


def exchange(value, axis, size, mask):
    return lax.ppermute(value, axis, [(i, i ^ mask) for i in range(size)])


def together(*values):
    return lax.optimization_barrier(values)


def shards(support, targets, panels, diag_inverses, *, n_row, n_col):
    rows, features = targets.shape
    span = support.shape[0]
    pivot = diag_inverses.shape[1]
    scale = 0.5 / math.sqrt(features)
    row, col = lax.axis_index("row"), lax.axis_index("col")
    width = features // n_row

    half = lax.dynamic_slice(targets, (0, (row % 2) * (features // 2)), (rows, features // 2))
    mine = lax.dynamic_slice(targets, (0, slice_of(row, n_row) * width), (rows, width))
    sibling = exchange(support, "row", n_row, 1)
    near = exchange(half, "col", n_col, 1)
    far = jnp.concatenate([exchange(mine, "col", n_col, j) for j in range(2, n_col)], axis=0)
    small = (jnp.broadcast_to(panels, (n_col, *panels.shape)) * PANEL_UNIT).astype(jnp.float16)
    blocks = lax.all_to_all(small, "col", 0, 0)
    corner = pl.pallas_call(
        corner_kernel,
        grid=(1,),
        out_shape=jax.ShapeDtypeStruct((pivot, pivot), jnp.float32),
        in_specs=[pl.BlockSpec((1, pivot, pivot), lambda i: (0, 0, 0))],
        out_specs=VMEM,
        compiler_params=PARAMS,
        cost_estimate=LONG,
        name="corner_kernel",
    )(panels)
    far, corner = together(far, corner)
    near = [near, exchange(near, "row", n_row, 1)]
    far = [far] + [exchange(far, "row", n_row, i) for i in range(2, n_row, 2)]
    far = [p for own in far for p in (own, exchange(own, "row", n_row, 1))]
    near[0], blocks = together(near[0], blocks)

    made = pl.pallas_call(
        functools.partial(tile_kernel, scale, n_row, n_col),
        out_shape=[jax.ShapeDtypeStruct((rows, span + pivot), jnp.float32)] * n_col,
        in_specs=[HBM] * 3 + [VMEM] * 2 + [HBM] * (n_row + 2),
        out_specs=[VMEM] * n_col,
        scratch_shapes=[
            pltpu.VMEM((n_col * rows, features), jnp.bfloat16),
            pltpu.VMEM((span + pivot, features), jnp.bfloat16),
            pltpu.SemaphoreType.DMA((2, n_row + 4)),
        ],
        compiler_params=PARAMS,
        cost_estimate=SHORT,
        name="tile_kernel",
    )(targets, support, sibling, corner, diag_inverses, *near, *far)

    tiles = [made[0]] + [exchange(made[j], "col", n_col, j) for j in range(1, n_col)]
    head = tiles[0][:, span:]
    for j in range(1, n_col):
        head = jnp.where(col == j, tiles[j][:, span:], head)
    spread = jnp.where(row < 2, head, 0.0)
    for i in range(2, n_row, 2):
        pairs = [(k * n_col + c, (i + k) * n_col + c) for k in range(2) for c in range(n_col)]
        spread = spread + lax.ppermute(head, ("row", "col"), pairs)
    swapped = exchange(spread, "row", n_row, 1)
    blocks = blocks.astype(jnp.float32) * (1 / PANEL_UNIT)

    return pl.pallas_call(
        functools.partial(solve_kernel, n_col, pivot),
        out_shape=jax.ShapeDtypeStruct((rows, span * n_col), jnp.float32),
        in_specs=[VMEM] * (n_col + 4),
        out_specs=VMEM,
        compiler_params=PARAMS,
        name="solve_kernel",
    )(*tiles, panels, blocks, spread, swapped)


def solution(mesh):
    in_specs = (P(("row", "col"), None), P("col", None), P(None, None, ("row", "col")), P())
    body = functools.partial(shards, n_row=mesh.shape["row"], n_col=mesh.shape["col"])
    return jax.shard_map(body, mesh=mesh, in_specs=in_specs, out_specs=P("col", "row"), check_vma=False)
```

time: 139 us -> 61.1 us (0.44)
  waiting for transfers between devices: 65.7 us -> 17.5 us
  blocking collectives: 45.5 us -> 0 us
  starting transfers between devices: 3.45 us -> 25.1 us
  between operations: 13.5 us -> 0.18 us
  Pallas kernels: 0 us -> 10.2 us
  matrix products: 7.16 us -> 0 us
  local copies, waits for them, and re-layouts: 0.03 us -> 4.75 us
    all_gather x2 -> x0, waiting for transfers between devices: 49.6 us -> none  [the longest x1 49.6 us: shards(): lax.all_gather(targets, 'col', axis=0, tiled=True)]
    psum x2 -> x0, blocking collectives: 45.5 us -> none  [spread(): return lax.psum(jnp.where(mine, value, jnp.zeros_like(value)), axis)]
    ppermute x0 -> x19, starting transfers between devices: none -> 20.9 us  [the longest x16 14.9 us: exchange(): return lax.ppermute(value, axis, [(i, i ^ mask) for i in range(size)])]
    ppermute x0 -> x19, waiting for transfers between devices: none -> 16.4 us  [the longest x16 14.8 us: exchange(): return lax.ppermute(value, axis, [(i, i ^ mask) for i in range(size)])]
    all_to_all x1, waiting for transfers between devices: 14.8 us -> 1.13 us  [shards(): blocks = lax.all_to_all(small, 'col', 0, 0)]
    pallas_call x0 -> x3, Pallas kernels: none -> 10.2 us  [the longest x1 6.22 us: shards(): pl.pallas_call(functools.partial(tile_kernel, scale, n_row, n_col), out_s...]
    dot_general x5 -> x0, matrix products: 7.16 us -> none  [the longest x2 3.64 us: apply_panel(): jnp.dot(solved_head, panel_cols, precision=lax.Precision.HIGHEST, preferr...]
    scatter x2 -> x0, other arithmetic: 2.66 us -> none  [shards(): grid_tile = updated.at[:, :pivot_width].set(new_head)]
  transfers between devices with their start and end apart: 3 -> 20, of which waited for: 2 -> 9; matrix products, arithmetic and copies ran while one was open for 3% -> 6% of each run, Pallas kernels for 0% -> 2%
where the time goes in v1:
time: 61.1 us; the launch traced here: 60.6 us
  starting transfers between devices  25.1 us (41%)
  waiting for transfers between devices  17.5 us (29%)
  Pallas kernels  10.2 us (17%)
  local copies, waits for them, and re-layouts  4.75 us (8%)
  other arithmetic  2.86 us (5%)
    ppermute x16, starting transfers between devices, exchange(): return lax.ppermute(value, axis, [(i, i ^ mask) for i in range(size)])  14.9 us
    ppermute x16, waiting for transfers between devices, exchange(): return lax.ppermute(value, axis, [(i, i ^ mask) for i in range(size)])  14.8 us
    pallas_call x1, Pallas kernels, shards(): pl.pallas_call(functools.partial(tile_kernel, scale, n_row, n_col), out_s...  6.22 us
    ppermute x3, starting transfers between devices, shards(): spread = spread + lax.ppermute(head, ('row', 'col'), pairs)  5.98 us
    all_to_all x1, starting transfers between devices, shards(): blocks = lax.all_to_all(small, 'col', 0, 0)  4.19 us
    pallas_call x1, Pallas kernels, shards(): pl.pallas_call(functools.partial(solve_kernel, n_col, pivot), out_shape=j...  2.51 us
    unnamed x24, local copies, waits for them, and re-layouts  1.95 us
    ppermute x3, waiting for transfers between devices, shards(): spread = spread + lax.ppermute(head, ('row', 'col'), pairs)  1.57 us
  transfers between devices with their start and end apart: 20, of which 9 were waited for; matrix products, arithmetic and copies ran while one was open for 6% of the time, Pallas kernels for 2%

profile of v1, /device:TPU:0, one launch (start us, length us, event | category | flops | bytes accessed | tf_op | source)
XLA Modules:
  0.0 60.6 jit_solution(9606076914559088683)
XLA Ops:
  0.0 1.0 %constant_dynamic-slice_fusion.1 = bf16[64,512]{1,0:T(8,128)(2,1)S(1)} fusion(bf16[64,4096]{1,0:T(8,128)(2,1)} %refs_0_.1, s32[]{:T(128)S(6)} %select_n.49), kind=kLoop, calls=%fused_computation.8 | loop fusion | bytes 131076 | tf_op jit(solution)/shard_map/dynamic_slice | solution.py:132
  1.0 4.0 %collective-permute-start.1 = (bf16[64,512]{1,0:T(8,128)(2,1)S(1)}, bf16[64,512]{1,0:T(8,128)(2,1)S(1)}, u32[]{:S(2)}, u32[]{:S(2)}) collective-permute-start(bf16[64,512]{1,0:T(8,128)(2,1)S(1)} %constant_dynamic-slice_fusion.1), channel_id=1, source_target_pairs={{0,2},{1,3},{2,0},{3,1},{4,6},{5,7},{6,4},{7,5},{8,10},{9,11},{10,... | collective-permute-start | bytes 196616 | tf_op jit(solution)/shard_map/ppermute | solution.py:116
  5.0 1.3 %collective-permute-start.2 = (bf16[64,512]{1,0:T(8,128)(2,1)S(1)}, bf16[64,512]{1,0:T(8,128)(2,1)S(1)}, u32[]{:S(2)}, u32[]{:S(2)}) collective-permute-start(bf16[64,512]{1,0:T(8,128)(2,1)S(1)} %constant_dynamic-slice_fusion.1), channel_id=1, source_target_pairs={{0,3},{1,2},{2,1},{3,0},{4,7},{5,6},{6,5},{7,4},{8,11},{9,10},{10,... | collective-permute-start | bytes 196616 | tf_op jit(solution)/shard_map/ppermute | solution.py:116
  6.4 1.0 %constant_dynamic-slice_fusion = bf16[64,2048]{1,0:T(8,128)(2,1)S(1)} fusion(bf16[64,4096]{1,0:T(8,128)(2,1)} %refs_0_.1, s32[]{:T(128)S(6)} %select_n.50), kind=kLoop, calls=%fused_computation.7 | loop fusion | bytes 524292 | tf_op jit(solution)/shard_map/dynamic_slice | solution.py:131
  7.6 1.0 %multiply_convert_fusion = f16[2,128,256]{2,1,0:T(8,128)(2,1)S(1)} fusion(f32[2,128,256]{2,1,0:T(8,128)} %refs_4_.3), kind=kLoop, calls=%fused_computation.1 | loop fusion | flops 131072 | bytes 393216 | tf_op jit(solution)/shard_map/convert_element_type | solution.py:136
  8.6 0.8 %broadcast_in_dim.7 = f16[4,2,128,256]{3,2,1,0:T(8,128)(2,1)} broadcast(f16[2,128,256]{2,1,0:T(8,128)(2,1)S(1)} %multiply_convert_fusion), dimensions={1,2,3} | broadcast | bytes 655360 | tf_op jit(solution)/shard_map/broadcast_in_dim | solution.py:136
  9.5 4.2 %all-to-all-start = ((f16[4,2,128,256]{3,2,1,0:T(8,128)(2,1)}), f16[4,2,128,256]{3,2,1,0:T(8,128)(2,1)S(1)}, u32[]{:S(2)}, u32[]{:S(2)}) async-start(f16[4,2,128,256]{3,2,1,0:T(8,128)(2,1)} %broadcast_in_dim.7), calls=%async_computation | async-start | bytes 1048576 | tf_op jit(solution)/shard_map/all_to_all | solution.py:137
  13.7 1.5 %corner_kernel.1.refs_3_ = f32[128,128]{1,0:T(8,128)} custom-call(f32[2,128,256]{2,1,0:T(8,128)} %refs_4_.3), custom_call_target="tpu_custom_call" | custom-call | flops 49999998976 | tf_op jit(solution)/shard_map/corner_kernel/pallas_call | solution.py:138
  15.2 2.5 %collective-permute-start.10 = (bf16[128,512]{1,0:T(8,128)(2,1)S(1)}, bf16[128,512]{1,0:T(8,128)(2,1)S(1)}, u32[]{:S(2)}, u32[]{:S(2)}) collective-permute-start(bf16[128,512]{1,0:T(8,128)(2,1)S(1)} %pad_maximum_fusion.refs_7_), channel_id=1, source_target_pairs={{0,24},{4,28},{8,16},{12,20},{16,8},{20,12},{24,0},{28,4},{1,25},{... | collective-permute-start | bytes 393224 | tf_op jit(solution)/shard_map/ppermute | solution.py:116
  17.7 0.5 collective-permute-start.6
  18.2 0.5 collective-permute-start.8
  18.7 3.7 %collective-permute-done.10.refs_13_ = bf16[128,512]{1,0:T(8,128)(2,1)S(1)} collective-permute-done((bf16[128,512]{1,0:T(8,128)(2,1)S(1)}, bf16[128,512]{1,0:T(8,128)(2,1)S(1)}, u32[]{:S(2)}, u32[]{:S(2)}) %collective-permute-start.10) | collective-permute-done | bytes 131104 | tf_op jit(solution)/shard_map/ppermute | solution.py:116
  22.4 0.5 collective-permute-start.4
  22.9 2.0 %collective-permute-done.6.refs_9_ = bf16[128,512]{1,0:T(8,128)(2,1)S(1)} collective-permute-done((bf16[128,512]{1,0:T(8,128)(2,1)S(1)}, bf16[128,512]{1,0:T(8,128)(2,1)S(1)}, u32[]{:S(2)}, u32[]{:S(2)}) %collective-permute-start.6) | collective-permute-done | bytes 131104 | tf_op jit(solution)/shard_map/ppermute | solution.py:116
  25.0 0.5 collective-permute-start.7
  25.5 0.6 %copy-done.10 = bf16[128,512]{1,0:T(8,128)(2,1)} copy-done((bf16[128,512]{1,0:T(8,128)(2,1)}, bf16[128,512]{1,0:T(8,128)(2,1)S(1)}, u32[]{:S(2)}) %copy-start.10) | copy-done | bytes 131096
  26.2 1.1 %all-to-all-done = f16[4,2,128,256]{3,2,1,0:T(8,128)(2,1)S(1)} async-done(((f16[4,2,128,256]{3,2,1,0:T(8,128)(2,1)}), f16[4,2,128,256]{3,2,1,0:T(8,128)(2,1)S(1)}, u32[]{:S(2)}, u32[]{:S(2)}) %all-to-all-start) | async-done | bytes 524320 | tf_op jit(solution)/shard_map/all_to_all | solution.py:137
  27.3 0.5 collective-permute-done.9.refs_12_
  27.9 0.7 %copy-done.3 = bf16[64,2048]{1,0:T(8,128)(2,1)} copy-done((bf16[64,2048]{1,0:T(8,128)(2,1)}, bf16[64,2048]{1,0:T(8,128)(2,1)S(1)}, u32[]{:S(2)}) %copy-start.3) | copy-done | bytes 262168
  28.5 6.2 %tile_kernel.1 = (f32[64,384]{1,0:T(8,128)}, f32[64,384]{1,0:T(8,128)}, f32[64,384]{1,0:T(8,128)}, f32[64,384]{1,0:T(8,128)}) custom-call(bf16[64,4096]{1,0:T(8,128)(2,1)} %refs_0_.1, bf16[256,4096]{1,0:T(8,128)(2,1)} %refs_1_.1, bf16[256,4096]{1,0:T(8,128)(2,1)} %collective-permute-done.refs_2_, f32[128,128]{1,0:T(8,128)} %corner_kernel.1.refs_3_, ...), custom_call_target="tpu_custom_call" | custom-call | flops 1000000 | tf_op jit(solution)/shard_map/tile_kernel/pallas_call | solution.py:154
  34.7 2.1 %collective-permute-start.12 = (f32[64,384]{1,0:T(8,128)}, f32[64,384]{1,0:T(8,128)S(1)}, u32[]{:S(2)}, u32[]{:S(2)}) collective-permute-start(f32[64,384]{1,0:T(8,128)} %get-tuple-element.17), channel_id=1, source_target_pairs={{0,1},{1,0},{2,3},{3,2},{4,5},{5,4},{6,7},{7,6},{8,9},{9,8},{10,11... | collective-permute-start | bytes 294920 | tf_op jit(solution)/shard_map/ppermute | solution.py:116
  36.8 2.4 %collective-permute-start.13 = (f32[64,384]{1,0:T(8,128)}, f32[64,384]{1,0:T(8,128)S(1)}, u32[]{:S(2)}, u32[]{:S(2)}) collective-permute-start(f32[64,384]{1,0:T(8,128)} %get-tuple-element.18), channel_id=1, source_target_pairs={{0,2},{1,3},{2,0},{3,1},{4,6},{5,7},{6,4},{7,5},{8,10},{9,11},{10,... | collective-permute-start | bytes 294920 | tf_op jit(solution)/shard_map/ppermute | solution.py:116
  39.3 0.9 %collective-permute-done.12.refs_1_ = f32[64,384]{1,0:T(8,128)S(1)} collective-permute-done((f32[64,384]{1,0:T(8,128)}, f32[64,384]{1,0:T(8,128)S(1)}, u32[]{:S(2)}, u32[]{:S(2)}) %collective-permute-start.12) | collective-permute-done | bytes 98336 | tf_op jit(solution)/shard_map/ppermute | solution.py:116
  40.2 7.6 %collective-permute-done.13.refs_2_ = f32[64,384]{1,0:T(8,128)S(1)} collective-permute-done((f32[64,384]{1,0:T(8,128)}, f32[64,384]{1,0:T(8,128)S(1)}, u32[]{:S(2)}, u32[]{:S(2)}) %collective-permute-start.13) | collective-permute-done | bytes 98336 | tf_op jit(solution)/shard_map/ppermute | solution.py:116
  47.8 0.8 %fusion.1 = f32[64,128]{1,0:T(8,128)S(1)} fusion(f32[64,384]{1,0:T(8,128)S(1)} %collective-permute-done.12.refs_1_, f32[64,384]{1,0:T(8,128)S(1)} %collective-permute-done.13.refs_2_, f32[64,384]{1,0:T(8,128)S(1)} %collective-permute-done.14.refs_3_, f32[64,384]{1,0:T(8,128)} %get-tuple-element.16.refs_0_, pred[]{:T(512)S(6)} %eq.14, pred[]{:T(512)S(6)} %eq.13, ...), kind=kLoop, calls=%fused_computation.5 | loop fusion | flops 24576 | bytes 163843 | tf_op jit(solution)/shard_map/jit(_where)/select_n | solution.py:172
  48.6 3.4 %collective-permute-start.15 = (f32[64,128]{1,0:T(8,128)S(1)}, f32[64,128]{1,0:T(8,128)S(1)}, u32[]{:S(2)}, u32[]{:S(2)}) collective-permute-start(f32[64,128]{1,0:T(8,128)S(1)} %fusion.1), channel_id=1, source_target_pairs={{0,8},{1,9},{2,10},{3,11},{4,12},{5,13},{6,14},{7,15}} | collective-permute-start | bytes 98312 | tf_op jit(solution)/shard_map/ppermute | solution.py:176
  52.0 1.3 %collective-permute-start.16 = (f32[64,128]{1,0:T(8,128)S(1)}, f32[64,128]{1,0:T(8,128)S(1)}, u32[]{:S(2)}, u32[]{:S(2)}) collective-permute-start(f32[64,128]{1,0:T(8,128)S(1)} %fusion.1), channel_id=1, source_target_pairs={{0,16},{1,17},{2,18},{3,19},{4,20},{5,21},{6,22},{7,23}} | collective-permute-start | bytes 98312 | tf_op jit(solution)/shard_map/ppermute | solution.py:176
  53.3 1.3 %collective-permute-start.17 = (f32[64,128]{1,0:T(8,128)S(1)}, f32[64,128]{1,0:T(8,128)S(1)}, u32[]{:S(2)}, u32[]{:S(2)}) collective-permute-start(f32[64,128]{1,0:T(8,128)S(1)} %fusion.1), channel_id=1, source_target_pairs={{0,24},{1,25},{2,26},{3,27},{4,28},{5,29},{6,30},{7,31}} | collective-permute-start | bytes 98312 | tf_op jit(solution)/shard_map/ppermute | solution.py:176
  54.8 1.3 %collective-permute-done.17 = f32[64,128]{1,0:T(8,128)S(1)} collective-permute-done((f32[64,128]{1,0:T(8,128)S(1)}, f32[64,128]{1,0:T(8,128)S(1)}, u32[]{:S(2)}, u32[]{:S(2)}) %collective-permute-start.17) | collective-permute-done | bytes 32800 | tf_op jit(solution)/shard_map/ppermute | solution.py:176
  56.2 1.1 %convert_multiply_fusion.refs_5_ = f32[4,2,128,256]{3,2,1,0:T(8,128)} fusion(f16[4,2,128,256]{3,2,1,0:T(8,128)(2,1)S(1)} %all-to-all-done), kind=kLoop, calls=%fused_computation | loop fusion | flops 524288 | bytes 1572864 | tf_op jit(solution)/shard_map/mul | solution.py:178
  57.5 0.6 copy-done.11
  58.1 2.5 %solve_kernel.1 = f32[64,1024]{1,0:T(8,128)} custom-call(f32[64,384]{1,0:T(8,128)} %get-tuple-element.16.refs_0_, f32[64,384]{1,0:T(8,128)} %copy-done.4, f32[64,384]{1,0:T(8,128)} %copy-done.5, f32[64,384]{1,0:T(8,128)} %copy-done.6, f32[2,128,256]{2,1,0:T(8,128)} %refs_4_.3, f32[4,2,128,256]{3,2,1,0:T(8,128)} %convert_multiply_fusion.refs_5_, ...), custom_call_target="tpu_custom_call" | custom-call | tf_op jit(solution)/shard_map/solve_kernel/pallas_call | solution.py:180
  (43 shorter events, 1.0 us)
Async XLA Ops:
  0.0 13.7 %copy-start = (bf16[256,4096]{1,0:T(8,128)(2,1)S(1)}, bf16[256,4096]{1,0:T(8,128)(2,1)}, u32[]{:S(2)}) copy-start(bf16[256,4096]{1,0:T(8,128)(2,1)} %refs_1_.1) | copy-start | bytes 6291460
  1.0 14.1 %collective-permute-start.1 = (bf16[64,512]{1,0:T(8,128)(2,1)S(1)}, bf16[64,512]{1,0:T(8,128)(2,1)S(1)}, u32[]{:S(2)}, u32[]{:S(2)}) collective-permute-start(bf16[64,512]{1,0:T(8,128)(2,1)S(1)} %constant_dynamic-slice_fusion.1), channel_id=1, source_target_pairs={{0,2},{1,3},{2,0},{3,1},{4,6},{5,7},{6,4},{7,5},{8,10},{9,11},{10,... | collective-permute-start | bytes 196616 | tf_op jit(solution)/shard_map/ppermute | solution.py:116
  5.0 10.1 %collective-permute-start.2 = (bf16[64,512]{1,0:T(8,128)(2,1)S(1)}, bf16[64,512]{1,0:T(8,128)(2,1)S(1)}, u32[]{:S(2)}, u32[]{:S(2)}) collective-permute-start(bf16[64,512]{1,0:T(8,128)(2,1)S(1)} %constant_dynamic-slice_fusion.1), channel_id=1, source_target_pairs={{0,3},{1,2},{2,1},{3,0},{4,7},{5,6},{6,5},{7,4},{8,11},{9,10},{10,... | collective-permute-start | bytes 196616 | tf_op jit(solution)/shard_map/ppermute | solution.py:116
  7.4 15.1 %collective-permute-start.3 = (bf16[64,2048]{1,0:T(8,128)(2,1)S(1)}, bf16[64,2048]{1,0:T(8,128)(2,1)S(1)}, u32[]{:S(2)}, u32[]{:S(2)}) collective-permute-start(bf16[64,2048]{1,0:T(8,128)(2,1)S(1)} %constant_dynamic-slice_fusion), channel_id=1, source_target_pairs={{0,1},{1,0},{2,3},{3,2},{4,5},{5,4},{6,7},{7,6},{8,9},{9,8},{10,11... | collective-permute-start | bytes 786440 | tf_op jit(solution)/shard_map/ppermute | solution.py:116
  9.5 17.8 %all-to-all-start = ((f16[4,2,128,256]{3,2,1,0:T(8,128)(2,1)}), f16[4,2,128,256]{3,2,1,0:T(8,128)(2,1)S(1)}, u32[]{:S(2)}, u32[]{:S(2)}) async-start(f16[4,2,128,256]{3,2,1,0:T(8,128)(2,1)} %broadcast_in_dim.7), calls=%async_computation | async-start | bytes 1048576 | tf_op jit(solution)/shard_map/all_to_all | solution.py:137
  13.7 14.1 %collective-permute-start = (bf16[256,4096]{1,0:T(8,128)(2,1)S(1)}, bf16[256,4096]{1,0:T(8,128)(2,1)}, u32[]{:S(2)}, u32[]{:S(2)}) collective-permute-start(bf16[256,4096]{1,0:T(8,128)(2,1)S(1)} %copy-done), channel_id=1, source_target_pairs={{0,4},{4,0},{8,12},{12,8},{16,20},{20,16},{24,28},{28,24},{1,5},{5... | collective-permute-start | bytes 6291464 | tf_op jit(solution)/shard_map/ppermute | solution.py:116
  15.2 12.7 %copy-start.1 = (bf16[128,512]{1,0:T(8,128)(2,1)}, bf16[128,512]{1,0:T(8,128)(2,1)S(1)}, u32[]{:S(2)}) copy-start(bf16[128,512]{1,0:T(8,128)(2,1)S(1)} %pad_maximum_fusion.refs_7_) | copy-start | bytes 393220
  15.2 7.3 %collective-permute-start.10 = (bf16[128,512]{1,0:T(8,128)(2,1)S(1)}, bf16[128,512]{1,0:T(8,128)(2,1)S(1)}, u32[]{:S(2)}, u32[]{:S(2)}) collective-permute-start(bf16[128,512]{1,0:T(8,128)(2,1)S(1)} %pad_maximum_fusion.refs_7_), channel_id=1, source_target_pairs={{0,24},{4,28},{8,16},{12,20},{16,8},{20,12},{24,0},{28,4},{1,25},{... | collective-permute-start | bytes 393224 | tf_op jit(solution)/shard_map/ppermute | solution.py:116
  17.7 7.3 %collective-permute-start.6 = (bf16[128,512]{1,0:T(8,128)(2,1)S(1)}, bf16[128,512]{1,0:T(8,128)(2,1)S(1)}, u32[]{:S(2)}, u32[]{:S(2)}) collective-permute-start(bf16[128,512]{1,0:T(8,128)(2,1)S(1)} %pad_maximum_fusion.refs_7_), channel_id=1, source_target_pairs={{0,8},{4,12},{8,0},{12,4},{16,24},{20,28},{24,16},{28,20},{1,9},{5... | collective-permute-start | bytes 393224 | tf_op jit(solution)/shard_map/ppermute | solution.py:116
  18.2 6.7 %collective-permute-start.8 = (bf16[128,512]{1,0:T(8,128)(2,1)S(1)}, bf16[128,512]{1,0:T(8,128)(2,1)}, u32[]{:S(2)}, u32[]{:S(2)}) collective-permute-start(bf16[128,512]{1,0:T(8,128)(2,1)S(1)} %pad_maximum_fusion.refs_7_), channel_id=1, source_target_pairs={{0,16},{4,20},{8,24},{12,28},{16,0},{20,4},{24,8},{28,12},{1,17},{... | collective-permute-start | bytes 393224 | tf_op jit(solution)/shard_map/ppermute | solution.py:116
  22.4 5.4 %copy-start.8 = (bf16[128,512]{1,0:T(8,128)(2,1)}, bf16[128,512]{1,0:T(8,128)(2,1)S(1)}, u32[]{:S(2)}) copy-start(bf16[128,512]{1,0:T(8,128)(2,1)S(1)} %collective-permute-done.10.refs_13_) | copy-start | bytes 393220
  22.4 3.0 %collective-permute-start.5 = (bf16[128,512]{1,0:T(8,128)(2,1)S(1)}, bf16[128,512]{1,0:T(8,128)(2,1)S(1)}, u32[]{:S(2)}, u32[]{:S(2)}) collective-permute-start(bf16[128,512]{1,0:T(8,128)(2,1)S(1)} %pad_maximum_fusion.refs_7_), channel_id=1, source_target_pairs={{0,4},{4,0},{8,12},{12,8},{16,20},{20,16},{24,28},{28,24},{1,5},{5... | collective-permute-start | bytes 393224 | tf_op jit(solution)/shard_map/ppermute | solution.py:116
  22.4 5.4 %copy-start.2 = (bf16[64,2048]{1,0:T(8,128)(2,1)}, bf16[64,2048]{1,0:T(8,128)(2,1)S(1)}, u32[]{:S(2)}) copy-start(bf16[64,2048]{1,0:T(8,128)(2,1)S(1)} %collective-permute-done.3.refs_5_) | copy-start | bytes 786436
  22.4 5.4 %collective-permute-start.4 = (bf16[64,2048]{1,0:T(8,128)(2,1)S(1)}, bf16[64,2048]{1,0:T(8,128)(2,1)S(1)}, u32[]{:S(2)}, u32[]{:S(2)}) collective-permute-start(bf16[64,2048]{1,0:T(8,128)(2,1)S(1)} %collective-permute-done.3.refs_5_), channel_id=1, source_target_pairs={{0,4},{4,0},{8,12},{12,8},{16,20},{20,16},{24,28},{28,24},{1,5},{5... | collective-permute-start | bytes 786440 | tf_op jit(solution)/shard_map/ppermute | solution.py:116
  24.9 2.9 %copy-start.9 = (bf16[128,512]{1,0:T(8,128)(2,1)}, bf16[128,512]{1,0:T(8,128)(2,1)S(1)}, u32[]{:S(2)}) copy-start(bf16[128,512]{1,0:T(8,128)(2,1)S(1)} %collective-permute-done.6.refs_9_) | copy-start | bytes 393220
  24.9 2.4 %collective-permute-start.11 = (bf16[128,512]{1,0:T(8,128)(2,1)S(1)}, bf16[128,512]{1,0:T(8,128)(2,1)}, u32[]{:S(2)}, u32[]{:S(2)}) collective-permute-start(bf16[128,512]{1,0:T(8,128)(2,1)S(1)} %collective-permute-done.10.refs_13_), channel_id=1, source_target_pairs={{0,4},{4,0},{8,12},{12,8},{16,20},{20,16},{24,28},{28,24},{1,5},{5... | collective-permute-start | bytes 393224 | tf_op jit(solution)/shard_map/ppermute | solution.py:116
  25.0 2.4 %collective-permute-start.7 = (bf16[128,512]{1,0:T(8,128)(2,1)S(1)}, bf16[128,512]{1,0:T(8,128)(2,1)}, u32[]{:S(2)}, u32[]{:S(2)}) collective-permute-start(bf16[128,512]{1,0:T(8,128)(2,1)S(1)} %collective-permute-done.6.refs_9_), channel_id=1, source_target_pairs={{0,4},{4,0},{8,12},{12,8},{16,20},{20,16},{24,28},{28,24},{1,5},{5... | collective-permute-start | bytes 393224 | tf_op jit(solution)/shard_map/ppermute | solution.py:116
  25.5 0.7 %copy-start.10 = (bf16[128,512]{1,0:T(8,128)(2,1)}, bf16[128,512]{1,0:T(8,128)(2,1)S(1)}, u32[]{:S(2)}) copy-start(bf16[128,512]{1,0:T(8,128)(2,1)S(1)} %collective-permute-done.5.refs_8_) | copy-start | bytes 393220
  26.1 1.7 %collective-permute-start.9 = (bf16[128,512]{1,0:T(8,128)(2,1)}, bf16[128,512]{1,0:T(8,128)(2,1)}, u32[]{:S(2)}, u32[]{:S(2)}) collective-permute-start(bf16[128,512]{1,0:T(8,128)(2,1)} %collective-permute-done.8.refs_11_), channel_id=1, source_target_pairs={{0,4},{4,0},{8,12},{12,8},{16,20},{20,16},{24,28},{28,24},{1,5},{5... | collective-permute-start | bytes 393224 | tf_op jit(solution)/shard_map/ppermute | solution.py:116
  27.8 0.7 %copy-start.3 = (bf16[64,2048]{1,0:T(8,128)(2,1)}, bf16[64,2048]{1,0:T(8,128)(2,1)S(1)}, u32[]{:S(2)}) copy-start(bf16[64,2048]{1,0:T(8,128)(2,1)S(1)} %collective-permute-done.4.refs_6_) | copy-start | bytes 786436
  34.7 5.4 %collective-permute-start.12 = (f32[64,384]{1,0:T(8,128)}, f32[64,384]{1,0:T(8,128)S(1)}, u32[]{:S(2)}, u32[]{:S(2)}) collective-permute-start(f32[64,384]{1,0:T(8,128)} %get-tuple-element.17), channel_id=1, source_target_pairs={{0,1},{1,0},{2,3},{3,2},{4,5},{5,4},{6,7},{7,6},{8,9},{9,8},{10,11... | collective-permute-start | bytes 294920 | tf_op jit(solution)/shard_map/ppermute | solution.py:116
  36.8 10.9 %collective-permute-start.13 = (f32[64,384]{1,0:T(8,128)}, f32[64,384]{1,0:T(8,128)S(1)}, u32[]{:S(2)}, u32[]{:S(2)}) collective-permute-start(f32[64,384]{1,0:T(8,128)} %get-tuple-element.18), channel_id=1, source_target_pairs={{0,2},{1,3},{2,0},{3,1},{4,6},{5,7},{6,4},{7,5},{8,10},{9,11},{10,... | collective-permute-start | bytes 294920 | tf_op jit(solution)/shard_map/ppermute | solution.py:116
  39.2 8.6 %collective-permute-start.14 = (f32[64,384]{1,0:T(8,128)}, f32[64,384]{1,0:T(8,128)S(1)}, u32[]{:S(2)}, u32[]{:S(2)}) collective-permute-start(f32[64,384]{1,0:T(8,128)} %get-tuple-element.19), channel_id=1, source_target_pairs={{0,3},{1,2},{2,1},{3,0},{4,7},{5,6},{6,5},{7,4},{8,11},{9,10},{10,... | collective-permute-start | bytes 294920 | tf_op jit(solution)/shard_map/ppermute | solution.py:116
  40.2 17.3 %copy-start.4 = (f32[64,384]{1,0:T(8,128)}, f32[64,384]{1,0:T(8,128)S(1)}, u32[]{:S(2)}) copy-start(f32[64,384]{1,0:T(8,128)S(1)} %collective-permute-done.12.refs_1_) | copy-start | bytes 294916
  47.7 9.7 %copy-start.5 = (f32[64,384]{1,0:T(8,128)}, f32[64,384]{1,0:T(8,128)S(1)}, u32[]{:S(2)}) copy-start(f32[64,384]{1,0:T(8,128)S(1)} %collective-permute-done.13.refs_2_) | copy-start | bytes 294916
  47.8 9.7 %copy-start.6 = (f32[64,384]{1,0:T(8,128)}, f32[64,384]{1,0:T(8,128)S(1)}, u32[]{:S(2)}) copy-start(f32[64,384]{1,0:T(8,128)S(1)} %collective-permute-done.14.refs_3_) | copy-start | bytes 294916
  48.6 6.0 %collective-permute-start.15 = (f32[64,128]{1,0:T(8,128)S(1)}, f32[64,128]{1,0:T(8,128)S(1)}, u32[]{:S(2)}, u32[]{:S(2)}) collective-permute-start(f32[64,128]{1,0:T(8,128)S(1)} %fusion.1), channel_id=1, source_target_pairs={{0,8},{1,9},{2,10},{3,11},{4,12},{5,13},{6,14},{7,15}} | collective-permute-start | bytes 98312 | tf_op jit(solution)/shard_map/ppermute | solution.py:176
  52.0 2.9 %collective-permute-start.16 = (f32[64,128]{1,0:T(8,128)S(1)}, f32[64,128]{1,0:T(8,128)S(1)}, u32[]{:S(2)}, u32[]{:S(2)}) collective-permute-start(f32[64,128]{1,0:T(8,128)S(1)} %fusion.1), channel_id=1, source_target_pairs={{0,16},{1,17},{2,18},{3,19},{4,20},{5,21},{6,22},{7,23}} | collective-permute-start | bytes 98312 | tf_op jit(solution)/shard_map/ppermute | solution.py:176
  53.3 2.9 %collective-permute-start.17 = (f32[64,128]{1,0:T(8,128)S(1)}, f32[64,128]{1,0:T(8,128)S(1)}, u32[]{:S(2)}, u32[]{:S(2)}) collective-permute-start(f32[64,128]{1,0:T(8,128)S(1)} %fusion.1), channel_id=1, source_target_pairs={{0,24},{1,25},{2,26},{3,27},{4,28},{5,29},{6,30},{7,31}} | collective-permute-start | bytes 98312 | tf_op jit(solution)/shard_map/ppermute | solution.py:176
  56.1 1.3 %copy-start.7 = (f32[64,128]{1,0:T(8,128)}, f32[64,128]{1,0:T(8,128)S(1)}, u32[]{:S(2)}) copy-start(f32[64,128]{1,0:T(8,128)S(1)} %add_add_fusion.refs_6_) | copy-start | bytes 98308
  56.2 1.3 %collective-permute-start.18 = (f32[64,128]{1,0:T(8,128)S(1)}, f32[64,128]{1,0:T(8,128)S(1)}, u32[]{:S(2)}, u32[]{:S(2)}) collective-permute-start(f32[64,128]{1,0:T(8,128)S(1)} %add_add_fusion.refs_6_), channel_id=1, source_target_pairs={{0,4},{4,0},{8,12},{12,8},{16,20},{20,16},{24,28},{28,24},{1,5},{5... | collective-permute-start | bytes 98312 | tf_op jit(solution)/shard_map/ppermute | solution.py:116
  57.4 0.6 copy-start.11

commit v2 on v1

--- a/solution.py
+++ b/solution.py
@@ -10,7 +10,8 @@
 
 VMEM = pl.BlockSpec(memory_space=pltpu.VMEM)
 HBM = pl.BlockSpec(memory_space=pltpu.HBM)
-PARAMS = pltpu.CompilerParams(vmem_limit_bytes=60 * 2**20)
+TILE_PARAMS = pltpu.CompilerParams(vmem_limit_bytes=32 * 2**20)
+SOLVE_PARAMS = pltpu.CompilerParams(vmem_limit_bytes=32 * 2**20)
 LONG = pl.CostEstimate(flops=50_000_000_000, bytes_accessed=0, transcendentals=0)
 SHORT = pl.CostEstimate(flops=1_000_000, bytes_accessed=0, transcendentals=0)
 PANEL_UNIT = 2.0**17
@@ -49,26 +50,24 @@
         copy.wait()
 
 
-def corner_kernel(corner_ref, out_ref):
-    out_ref[...] = corner_ref[0]
-
-
-def tile_kernel(scale, n_row, n_col, *refs):
-    own_hbm, support_hbm, sibling_hbm, corner_ref, inverse_ref = refs[:5]
-    near, far, refs = refs[5:7], refs[7:7 + n_row], refs[7 + n_row:]
+def mark_kernel(value_ref, token_ref, out_ref):
+    del token_ref
+    out_ref[...] = value_ref[0, :8, :128]
+
+
+def tile_kernel(scale, n_row, n_col, own_hbm, support_hbm, _, *refs):
+    near, far, refs = refs[:2], refs[2:2 + n_row], refs[2 + n_row:]
     outs, (targets_ref, support_ref, sems) = refs[:n_col], refs[n_col:]
     (rows, features), (_, width) = own_hbm.shape, far[0].shape
-    span, pivot = support_hbm.shape[0], corner_ref.shape[1]
     half = features // 2
-    row, col = lax.axis_index("row"), lax.axis_index("col")
+    row = lax.axis_index("row")
     odd = row % 2
     steps = []
     for core in range(2):
         cols = pl.ds(pl.multiple_of((odd ^ core) * half, half), half)
         loads = [
             (own_hbm.at[:, cols], targets_ref.at[pl.ds(0, rows), cols]),
-            (support_hbm.at[:, cols], support_ref.at[pl.ds(0, span), cols]),
-            (sibling_hbm.at[pl.ds(0, pivot), cols], support_ref.at[pl.ds(span, pivot), cols]),
+            (support_hbm.at[:, cols], support_ref.at[:, cols]),
             (near[core], targets_ref.at[pl.ds(rows, rows), cols]),
         ]
         for step in range(core, n_row, 2):
@@ -79,14 +78,15 @@
     for cols, copies in steps:
         wait_all(copies)
         total = total + dot(targets_ref[:, cols], support_ref[:, cols], NT)
-    kernel = jnp.exp(scale * total)
-    other = jnp.where(odd == 1, kernel[:, span:], 0.0)
-    head = kernel[:, :pivot] - dot32(dot32(other, inverse_ref[0], NT), corner_ref[...], NN)
-    head = dot32(head, inverse_ref[odd], NT)
     for plane in range(n_col):
-        part = slice(plane * rows, (plane + 1) * rows)
-        outs[plane][:, :span] = kernel[part, :span]
-        outs[plane][:, span:] = head[part]
+        outs[plane][...] = jnp.exp(scale * total[plane * rows:(plane + 1) * rows])
+
+
+def head_kernel(mine_ref, other_ref, corner_ref, inverse_ref, out_ref):
+    odd = lax.axis_index("row") % 2
+    other = jnp.where(odd == 1, other_ref[...], 0.0)
+    head = mine_ref[...] - dot32(dot32(other, inverse_ref[0], NT), corner_ref[...], NN)
+    out_ref[...] = dot32(head, inverse_ref[odd], NT)
 
 
 def solve_kernel(n_col, pivot, *refs):
@@ -100,7 +100,7 @@
     for step in range(n_col):
         plane = col ^ step
         block = own_ref if step == 0 else panels_ref.at[plane]
-        value = tiles[step][:, :span] - dot32(first, block[0], NN) - dot32(second, block[1], NN)
+        value = tiles[step][...] - dot32(first, block[0], NN) - dot32(second, block[1], NN)
         out_ref[:, pl.ds(pl.multiple_of(plane * span, span), span)] = value
 
     @pl.when(row == 0)
@@ -130,50 +130,62 @@
 
     half = lax.dynamic_slice(targets, (0, (row % 2) * (features // 2)), (rows, features // 2))
     mine = lax.dynamic_slice(targets, (0, slice_of(row, n_row) * width), (rows, width))
-    sibling = exchange(support, "row", n_row, 1)
     near = exchange(half, "col", n_col, 1)
     far = jnp.concatenate([exchange(mine, "col", n_col, j) for j in range(2, n_col)], axis=0)
-    small = (jnp.broadcast_to(panels, (n_col, *panels.shape)) * PANEL_UNIT).astype(jnp.float16)
+    small = jnp.concatenate([panels * PANEL_UNIT] * n_col, axis=0).astype(jnp.float16)
+    small = small.reshape(n_col, *panels.shape)
+    far, small, marked = together(far, small, diag_inverses)
+    token = exchange(far[:16, :128], "row", n_row, 1)
+    small, token = together(small, token)
     blocks = lax.all_to_all(small, "col", 0, 0)
-    corner = pl.pallas_call(
-        corner_kernel,
+    mark = pl.pallas_call(
+        mark_kernel,
         grid=(1,),
-        out_shape=jax.ShapeDtypeStruct((pivot, pivot), jnp.float32),
-        in_specs=[pl.BlockSpec((1, pivot, pivot), lambda i: (0, 0, 0))],
+        out_shape=jax.ShapeDtypeStruct((8, 128), jnp.float32),
+        in_specs=[pl.BlockSpec((1, 8, 128), lambda i: (0, 0, 0)), VMEM],
         out_specs=VMEM,
-        compiler_params=PARAMS,
+        compiler_params=SOLVE_PARAMS,
         cost_estimate=LONG,
-        name="corner_kernel",
-    )(panels)
-    far, corner = together(far, corner)
+        name="mark_kernel",
+    )(marked, token)
     near = [near, exchange(near, "row", n_row, 1)]
     far = [far] + [exchange(far, "row", n_row, i) for i in range(2, n_row, 2)]
+    far[1], mark = together(far[1], mark)
     far = [p for own in far for p in (own, exchange(own, "row", n_row, 1))]
-    near[0], blocks = together(near[0], blocks)
 
     made = pl.pallas_call(
         functools.partial(tile_kernel, scale, n_row, n_col),
-        out_shape=[jax.ShapeDtypeStruct((rows, span + pivot), jnp.float32)] * n_col,
-        in_specs=[HBM] * 3 + [VMEM] * 2 + [HBM] * (n_row + 2),
+        out_shape=[jax.ShapeDtypeStruct((rows, span), jnp.float32)] * n_col,
+        in_specs=[HBM] * (n_row + 5),
         out_specs=[VMEM] * n_col,
         scratch_shapes=[
             pltpu.VMEM((n_col * rows, features), jnp.bfloat16),
-            pltpu.VMEM((span + pivot, features), jnp.bfloat16),
+            pltpu.VMEM((span, features), jnp.bfloat16),
             pltpu.SemaphoreType.DMA((2, n_row + 4)),
         ],
-        compiler_params=PARAMS,
+        compiler_params=TILE_PARAMS,
         cost_estimate=SHORT,
         name="tile_kernel",
-    )(targets, support, sibling, corner, diag_inverses, *near, *far)
+    )(targets, support, mark, *near, *far)
 
     tiles = [made[0]] + [exchange(made[j], "col", n_col, j) for j in range(1, n_col)]
-    head = tiles[0][:, span:]
+    tiles, blocks = together(tiles, blocks)
+    corner = blocks[0, 0, :, :pivot].astype(jnp.float32) * (1 / PANEL_UNIT)
+    head = tiles[0][:, :pivot]
     for j in range(1, n_col):
-        head = jnp.where(col == j, tiles[j][:, span:], head)
-    spread = jnp.where(row < 2, head, 0.0)
+        head = jnp.where(col == j, tiles[j][:, :pivot], head)
+    head = pl.pallas_call(
+        head_kernel,
+        out_shape=jax.ShapeDtypeStruct((rows, pivot), jnp.float32),
+        in_specs=[VMEM] * 4,
+        out_specs=VMEM,
+        compiler_params=SOLVE_PARAMS,
+        cost_estimate=SHORT,
+        name="head_kernel",
+    )(head, exchange(head, "row", n_row, 1), corner, diag_inverses)
+    spread = head
     for i in range(2, n_row, 2):
-        pairs = [(k * n_col + c, (i + k) * n_col + c) for k in range(2) for c in range(n_col)]
-        spread = spread + lax.ppermute(head, ("row", "col"), pairs)
+        spread = jnp.where(row // 2 == i // 2, exchange(head, "row", n_row, i), spread)
     swapped = exchange(spread, "row", n_row, 1)
     blocks = blocks.astype(jnp.float32) * (1 / PANEL_UNIT)
 
@@ -182,7 +194,7 @@
         out_shape=jax.ShapeDtypeStruct((rows, span * n_col), jnp.float32),
         in_specs=[VMEM] * (n_col + 4),
         out_specs=VMEM,
-        compiler_params=PARAMS,
+        compiler_params=SOLVE_PARAMS,
         name="solve_kernel",
     )(*tiles, panels, blocks, spread, swapped)
 

time: 61.1 us -> 50.2 us (0.82)
  Pallas kernels: 10.2 us -> 3.2 us
  waiting for transfers between devices: 17.5 us -> 21.2 us
  starting transfers between devices: 25.1 us -> 21.6 us
  local copies, waits for them, and re-layouts: 4.75 us -> 1.87 us
  other arithmetic: 2.86 us -> 2.03 us
    ppermute x16 -> x20, waiting for transfers between devices: 14.8 us -> 21.2 us  [exchange(): return lax.ppermute(value, axis, [(i, i ^ mask) for i in range(size)])]
    ppermute x3 -> x0, starting transfers between devices: 5.98 us -> none  [shards(): spread = spread + lax.ppermute(head, ('row', 'col'), pairs)]
    pallas_call x1, Pallas kernels: 6.22 us -> 1.6 us  [shards(): pl.pallas_call(functools.partial(tile_kernel, scale, n_row, n_col), out_s...]
    ppermute x16 -> x20, starting transfers between devices: 14.9 us -> 18.1 us  [exchange(): return lax.ppermute(value, axis, [(i, i ^ mask) for i in range(size)])]
    unnamed x24 -> x8, local copies, waits for them, and re-layouts: 1.95 us -> 0.02 us
    ppermute x3 -> x0, waiting for transfers between devices: 1.57 us -> none  [shards(): spread = spread + lax.ppermute(head, ('row', 'col'), pairs)]
    pallas_call x1, Pallas kernels: 2.51 us -> 1.08 us  [shards(): pl.pallas_call(functools.partial(solve_kernel, n_col, pivot), out_shape=j...]
    all_to_all x1, waiting for transfers between devices: 1.13 us -> 0.01 us  [shards(): blocks = lax.all_to_all(small, 'col', 0, 0)]
  transfers between devices with their start and end apart: 20 -> 21, of which waited for: 9 -> 11; matrix products, arithmetic and copies ran while one was open for 6% -> 6% of each run, Pallas kernels for 2% -> 3%
where the time goes in v2:
time: 50.2 us; the launch traced here: 50 us
  starting transfers between devices  21.6 us (43%)
  waiting for transfers between devices  21.2 us (42%)
  Pallas kernels  3.2 us (6%)
  other arithmetic  2.03 us (4%)
  local copies, waits for them, and re-layouts  1.87 us (4%)
    ppermute x20, waiting for transfers between devices, exchange(): return lax.ppermute(value, axis, [(i, i ^ mask) for i in range(size)])  21.2 us
    ppermute x20, starting transfers between devices, exchange(): return lax.ppermute(value, axis, [(i, i ^ mask) for i in range(size)])  18.1 us
    all_to_all x1, starting transfers between devices, shards(): blocks = lax.all_to_all(small, 'col', 0, 0)  3.51 us
    pallas_call x1, Pallas kernels, shards(): pl.pallas_call(functools.partial(tile_kernel, scale, n_row, n_col), out_s...  1.6 us
    pallas_call x1, Pallas kernels, shards(): pl.pallas_call(functools.partial(solve_kernel, n_col, pivot), out_shape=j...  1.08 us
  transfers between devices with their start and end apart: 21, of which 11 were waited for; matrix products, arithmetic and copies ran while one was open for 6% of the time, Pallas kernels for 3%

profile of v2, /device:TPU:0, one launch (start us, length us, event | category | flops | bytes accessed | tf_op | source)
XLA Modules:
  0.0 50.0 jit_solution(2431145228942623791)
XLA Ops:
  0.0 0.9 %constant_dynamic-slice_fusion.1 = bf16[64,512]{1,0:T(8,128)(2,1)S(1)} fusion(bf16[64,4096]{1,0:T(8,128)(2,1)} %own_hbm.1, s32[]{:T(128)S(6)} %select_n.62), kind=kLoop, calls=%fused_computation.8 | loop fusion | bytes 131076 | tf_op jit(solution)/shard_map/dynamic_slice | solution.py:132
  0.9 4.0 %collective-permute-start = (bf16[64,512]{1,0:T(8,128)(2,1)S(1)}, bf16[64,512]{1,0:T(8,128)(2,1)S(1)}, u32[]{:S(2)}, u32[]{:S(2)}) collective-permute-start(bf16[64,512]{1,0:T(8,128)(2,1)S(1)} %constant_dynamic-slice_fusion.1), channel_id=1, source_target_pairs={{0,2},{1,3},{2,0},{3,1},{4,6},{5,7},{6,4},{7,5},{8,10},{9,11},{10,... | collective-permute-start | bytes 196616 | tf_op jit(solution)/shard_map/ppermute | solution.py:116
  4.9 1.3 %collective-permute-start.1 = (bf16[64,512]{1,0:T(8,128)(2,1)S(1)}, bf16[64,512]{1,0:T(8,128)(2,1)S(1)}, u32[]{:S(2)}, u32[]{:S(2)}) collective-permute-start(bf16[64,512]{1,0:T(8,128)(2,1)S(1)} %constant_dynamic-slice_fusion.1), channel_id=1, source_target_pairs={{0,3},{1,2},{2,1},{3,0},{4,7},{5,6},{6,5},{7,4},{8,11},{9,10},{10,... | collective-permute-start | bytes 196616 | tf_op jit(solution)/shard_map/ppermute | solution.py:116
  6.3 1.0 %constant_dynamic-slice_fusion = bf16[64,2048]{1,0:T(8,128)(2,1)S(1)} fusion(bf16[64,4096]{1,0:T(8,128)(2,1)} %own_hbm.1, s32[]{:T(128)S(6)} %select_n.63), kind=kLoop, calls=%fused_computation.7 | loop fusion | bytes 524292 | tf_op jit(solution)/shard_map/dynamic_slice | solution.py:131
  7.2 0.3 collective-permute-start.4
  7.5 1.0 %multiply_convert_fusion = f16[2,128,256]{2,1,0:T(8,128)(2,1)S(1)} fusion(f32[2,128,256]{2,1,0:T(8,128)} %refs_4_.1), kind=kLoop, calls=%fused_computation.2 | loop fusion | flops 131072 | bytes 393216 | tf_op jit(solution)/shard_map/convert
  8.5 0.9 %pad_maximum_fusion = f16[8,128,256]{2,1,0:T(8,128)(2,1)} fusion(f16[2,128,256]{2,1,0:T(8,128)(2,1)S(1)} %multiply_convert_fusion), kind=kLoop, calls=%fused_computation.1 | loop fusion | flops 786432 | bytes 655360 | tf_op jit(solution)/shard_map/concatenate | solution.py:135
  9.4 2.2 %collective-permute-done.1 = bf16[64,512]{1,0:T(8,128)(2,1)S(1)} collective-permute-done((bf16[64,512]{1,0:T(8,128)(2,1)S(1)}, bf16[64,512]{1,0:T(8,128)(2,1)S(1)}, u32[]{:S(2)}, u32[]{:S(2)}) %collective-permute-start.1) | collective-permute-done | bytes 65568 | tf_op jit(solution)/shard_map/ppermute | solution.py:116
  11.8 1.6 %collective-permute-start.2 = (bf16[128,512]{1,0:T(8,128)(2,1)S(1)}, bf16[128,512]{1,0:T(8,128)(2,1)S(1)}, u32[]{:S(2)}, u32[]{:S(2)}) collective-permute-start(bf16[128,512]{1,0:T(8,128)(2,1)S(1)} %pad_maximum_fusion.1.refs_2_), channel_id=1, source_target_pairs={{0,8},{4,12},{8,0},{12,4},{16,24},{20,28},{24,16},{28,20},{1,9},{5... | collective-permute-start | bytes 393224 | tf_op jit(solution)/shard_map/ppermute | solution.py:116
  13.3 1.5 %collective-permute-start.10 = (bf16[128,512]{1,0:T(8,128)(2,1)S(1)}, bf16[128,512]{1,0:T(8,128)(2,1)S(1)}, u32[]{:S(2)}, u32[]{:S(2)}) collective-permute-start(bf16[128,512]{1,0:T(8,128)(2,1)S(1)} %pad_maximum_fusion.1.refs_2_), channel_id=1, source_target_pairs={{0,24},{4,28},{8,16},{12,20},{16,8},{20,12},{24,0},{28,4},{1,25},{... | collective-permute-start | bytes 393224 | tf_op jit(solution)/shard_map/ppermute | solution.py:116
  14.8 0.5 %collective-permute-start.8 = (bf16[128,512]{1,0:T(8,128)(2,1)S(1)}, bf16[128,512]{1,0:T(8,128)(2,1)S(1)}, u32[]{:S(2)}, u32[]{:S(2)}) collective-permute-start(bf16[128,512]{1,0:T(8,128)(2,1)S(1)} %pad_maximum_fusion.1.refs_2_), channel_id=1, source_target_pairs={{0,16},{4,20},{8,24},{12,28},{16,0},{20,4},{24,8},{28,12},{1,17},{... | collective-permute-start | bytes 393224 | tf_op jit(solution)/shard_map/ppermute | solution.py:116
  15.3 3.5 %all-to-all-start = ((f16[4,2,128,256]{3,2,1,0:T(8,128)(2,1)}), f16[4,2,128,256]{3,2,1,0:T(8,128)(2,1)S(1)}, u32[]{:S(2)}, u32[]{:S(2)}) async-start(f16[4,2,128,256]{3,2,1,0:T(8,128)(2,1)} %bitcast), calls=%async_computation | async-start | bytes 1048576 | tf_op jit(solution)/shard_map/all_to_all | solution.py:140
  18.9 0.6 %collective-permute-start.5 = (bf16[64,2048]{1,0:T(8,128)(2,1)S(1)}, bf16[64,2048]{1,0:T(8,128)(2,1)S(1)}, u32[]{:S(2)}, u32[]{:S(2)}) collective-permute-start(bf16[64,2048]{1,0:T(8,128)(2,1)S(1)} %collective-permute-done.4.refs_0_), channel_id=1, source_target_pairs={{0,4},{4,0},{8,12},{12,8},{16,20},{20,16},{24,28},{28,24},{1,5},{5... | collective-permute-start | bytes 786440 | tf_op jit(solution)/shard_map/ppermute | solution.py:116
  19.5 2.0 %collective-permute-done.10.refs_8_ = bf16[128,512]{1,0:T(8,128)(2,1)S(1)} collective-permute-done((bf16[128,512]{1,0:T(8,128)(2,1)S(1)}, bf16[128,512]{1,0:T(8,128)(2,1)S(1)}, u32[]{:S(2)}, u32[]{:S(2)}) %collective-permute-start.10) | collective-permute-done | bytes 131104 | tf_op jit(solution)/shard_map/ppermute | solution.py:116
  21.6 1.4 %collective-permute-done.8.refs_6_ = bf16[128,512]{1,0:T(8,128)(2,1)S(1)} collective-permute-done((bf16[128,512]{1,0:T(8,128)(2,1)S(1)}, bf16[128,512]{1,0:T(8,128)(2,1)S(1)}, u32[]{:S(2)}, u32[]{:S(2)}) %collective-permute-start.8) | collective-permute-done | bytes 131104 | tf_op jit(solution)/shard_map/ppermute | solution.py:116
  22.9 1.3 %collective-permute-done.9.refs_7_ = bf16[128,512]{1,0:T(8,128)(2,1)S(1)} collective-permute-done((bf16[128,512]{1,0:T(8,128)(2,1)S(1)}, bf16[128,512]{1,0:T(8,128)(2,1)S(1)}, u32[]{:S(2)}, u32[]{:S(2)}) %collective-permute-start.9) | collective-permute-done | bytes 131104 | tf_op jit(solution)/shard_map/ppermute | solution.py:116
  24.3 1.6 %tile_kernel.1 = (f32[64,256]{1,0:T(8,128)S(1)}, f32[64,256]{1,0:T(8,128)S(1)}, f32[64,256]{1,0:T(8,128)S(1)}, f32[64,256]{1,0:T(8,128)S(1)}) custom-call(bf16[64,4096]{1,0:T(8,128)(2,1)S(1)} %copy-done.1, bf16[256,4096]{1,0:T(8,128)(2,1)S(1)} %copy-done, f32[8,128]{1,0:T(8,128)S(1)} %mark_kernel.1._, bf16[64,2048]{1,0:T(8,128)(2,1)S(1)} %collective-permute-done.4.refs_0_, ...), custom_call_target="tpu_custom_call" | custom-call | flops 1000000 | tf_op jit(solution)/shard_map/tile_kernel/pallas_call | solution.py:156
  25.9 0.5 collective-permute-start.12
  26.3 2.3 %collective-permute-start.13 = (f32[64,256]{1,0:T(8,128)S(1)}, f32[64,256]{1,0:T(8,128)S(1)}, u32[]{:S(2)}, u32[]{:S(2)}) collective-permute-start(f32[64,256]{1,0:T(8,128)S(1)} %get-tuple-element.29), channel_id=1, source_target_pairs={{0,2},{1,3},{2,0},{3,1},{4,6},{5,7},{6,4},{7,5},{8,10},{9,11},{10,... | collective-permute-start | bytes 196616 | tf_op jit(solution)/shard_map/ppermute | solution.py:116
  28.6 1.7 %collective-permute-start.14 = (f32[64,256]{1,0:T(8,128)S(1)}, f32[64,256]{1,0:T(8,128)S(1)}, u32[]{:S(2)}, u32[]{:S(2)}) collective-permute-start(f32[64,256]{1,0:T(8,128)S(1)} %get-tuple-element.30), channel_id=1, source_target_pairs={{0,3},{1,2},{2,1},{3,0},{4,7},{5,6},{6,5},{7,4},{8,11},{9,10},{10,... | collective-permute-start | bytes 196616 | tf_op jit(solution)/shard_map/ppermute | solution.py:116
  30.3 0.5 %collective-permute-done.12.refs_1_ = f32[64,256]{1,0:T(8,128)S(1)} collective-permute-done((f32[64,256]{1,0:T(8,128)S(1)}, f32[64,256]{1,0:T(8,128)S(1)}, u32[]{:S(2)}, u32[]{:S(2)}) %collective-permute-start.12) | collective-permute-done | bytes 65568 | tf_op jit(solution)/shard_map/ppermute | solution.py:116
  30.9 8.0 %collective-permute-done.13.refs_2_ = f32[64,256]{1,0:T(8,128)S(1)} collective-permute-done((f32[64,256]{1,0:T(8,128)S(1)}, f32[64,256]{1,0:T(8,128)S(1)}, u32[]{:S(2)}, u32[]{:S(2)}) %collective-permute-start.13) | collective-permute-done | bytes 65568 | tf_op jit(solution)/shard_map/ppermute | solution.py:116
  39.0 1.2 %collective-permute-done.15.other_ref = f32[64,128]{1,0:T(8,128)S(1)} collective-permute-done((f32[64,128]{1,0:T(8,128)S(1)}, f32[64,128]{1,0:T(8,128)S(1)}, u32[]{:S(2)}, u32[]{:S(2)}) %collective-permute-start.15) | collective-permute-done | bytes 32800 | tf_op jit(solution)/shard_map/ppermute | solution.py:116
  40.2 0.5 %head_kernel.1 = f32[64,128]{1,0:T(8,128)S(1)} custom-call(f32[64,128]{1,0:T(8,128)S(1)} %select_select_fusion.1.mine_ref, f32[64,128]{1,0:T(8,128)S(1)} %collective-permute-done.15.other_ref, f32[128,128]{1,0:T(8,128)S(1)} %multiply_bitcast_fusion.corner_ref, f32[2,128,128]{2,1,0:T(8,128)S(1)} %copy-done.3), custom_call_target="tpu_custom_call" | custom-call | flops 1000000 | tf_op jit(solution)/shard_map/head_kernel/pallas_call | solution.py:177
  40.7 2.5 %collective-permute-start.16 = (f32[64,128]{1,0:T(8,128)S(1)}, f32[64,128]{1,0:T(8,128)S(1)}, u32[]{:S(2)}, u32[]{:S(2)}) collective-permute-start(f32[64,128]{1,0:T(8,128)S(1)} %head_kernel.1), channel_id=1, source_target_pairs={{0,24},{4,28},{8,16},{12,20},{16,8},{20,12},{24,0},{28,4},{1,25},{... | collective-permute-start | bytes 98312 | tf_op jit(solution)/shard_map/ppermute | solution.py:116
  43.2 0.5 %collective-permute-start.17 = (f32[64,128]{1,0:T(8,128)S(1)}, f32[64,128]{1,0:T(8,128)S(1)}, u32[]{:S(2)}, u32[]{:S(2)}) collective-permute-start(f32[64,128]{1,0:T(8,128)S(1)} %head_kernel.1), channel_id=1, source_target_pairs={{0,16},{4,20},{8,24},{12,28},{16,0},{20,4},{24,8},{28,12},{1,17},{... | collective-permute-start | bytes 98312 | tf_op jit(solution)/shard_map/ppermute | solution.py:116
  43.7 0.5 %collective-permute-start.18 = (f32[64,128]{1,0:T(8,128)S(1)}, f32[64,128]{1,0:T(8,128)S(1)}, u32[]{:S(2)}, u32[]{:S(2)}) collective-permute-start(f32[64,128]{1,0:T(8,128)S(1)} %head_kernel.1), channel_id=1, source_target_pairs={{0,8},{4,12},{8,0},{12,4},{16,24},{20,28},{24,16},{28,20},{1,9},{5... | collective-permute-start | bytes 98312 | tf_op jit(solution)/shard_map/ppermute | solution.py:116
  44.2 1.3 %collective-permute-done.16 = f32[64,128]{1,0:T(8,128)S(1)} collective-permute-done((f32[64,128]{1,0:T(8,128)S(1)}, f32[64,128]{1,0:T(8,128)S(1)}, u32[]{:S(2)}, u32[]{:S(2)}) %collective-permute-start.16) | collective-permute-done | bytes 32800 | tf_op jit(solution)/shard_map/ppermute | solution.py:116
  45.6 1.5 %collective-permute-done.17 = f32[64,128]{1,0:T(8,128)S(1)} collective-permute-done((f32[64,128]{1,0:T(8,128)S(1)}, f32[64,128]{1,0:T(8,128)S(1)}, u32[]{:S(2)}, u32[]{:S(2)}) %collective-permute-start.17) | collective-permute-done | bytes 32800 | tf_op jit(solution)/shard_map/ppermute | solution.py:116
  47.1 0.5 %collective-permute-done.18 = f32[64,128]{1,0:T(8,128)S(1)} collective-permute-done((f32[64,128]{1,0:T(8,128)S(1)}, f32[64,128]{1,0:T(8,128)S(1)}, u32[]{:S(2)}, u32[]{:S(2)}) %collective-permute-start.18) | collective-permute-done | bytes 32800 | tf_op jit(solution)/shard_map/ppermute | solution.py:116
  47.8 1.1 %collective-permute-done.19.refs_7_ = f32[64,128]{1,0:T(8,128)S(1)} collective-permute-done((f32[64,128]{1,0:T(8,128)S(1)}, f32[64,128]{1,0:T(8,128)S(1)}, u32[]{:S(2)}, u32[]{:S(2)}) %collective-permute-start.19) | collective-permute-done | bytes 32800 | tf_op jit(solution)/shard_map/ppermute | solution.py:116
  48.9 1.1 %solve_kernel.1 = f32[64,1024]{1,0:T(8,128)} custom-call(f32[64,256]{1,0:T(8,128)S(1)} %get-tuple-element.32.refs_0_, f32[64,256]{1,0:T(8,128)S(1)} %collective-permute-done.12.refs_1_, f32[64,256]{1,0:T(8,128)S(1)} %collective-permute-done.13.refs_2_, f32[64,256]{1,0:T(8,128)S(1)} %collective-permute-done.14.refs_3_, f32[2,128,256]{2,1,0:T(8,128)S(1)} %copy-done.2, ...), custom_call_target="tpu_custom_call" | custom-call | tf_op jit(solution)/shard_map/solve_kernel/pallas_call | solution.py:192
  (32 shorter events, 0.5 us)
Async XLA Ops:
  0.0 19.4 %copy-start.3 = (f32[2,128,128]{2,1,0:T(8,128)S(1)}, f32[2,128,128]{2,1,0:T(8,128)}, u32[]{:S(2)}) copy-start(f32[2,128,128]{2,1,0:T(8,128)} %inverse_ref.1) | copy-start | bytes 393220
  0.9 8.5 %collective-permute-start = (bf16[64,512]{1,0:T(8,128)(2,1)S(1)}, bf16[64,512]{1,0:T(8,128)(2,1)S(1)}, u32[]{:S(2)}, u32[]{:S(2)}) collective-permute-start(bf16[64,512]{1,0:T(8,128)(2,1)S(1)} %constant_dynamic-slice_fusion.1), channel_id=1, source_target_pairs={{0,2},{1,3},{2,0},{3,1},{4,6},{5,7},{6,4},{7,5},{8,10},{9,11},{10,... | collective-permute-start | bytes 196616 | tf_op jit(solution)/shard_map/ppermute | solution.py:116
  4.9 6.7 %collective-permute-start.1 = (bf16[64,512]{1,0:T(8,128)(2,1)S(1)}, bf16[64,512]{1,0:T(8,128)(2,1)S(1)}, u32[]{:S(2)}, u32[]{:S(2)}) collective-permute-start(bf16[64,512]{1,0:T(8,128)(2,1)S(1)} %constant_dynamic-slice_fusion.1), channel_id=1, source_target_pairs={{0,3},{1,2},{2,1},{3,0},{4,7},{5,6},{6,5},{7,4},{8,11},{9,10},{10,... | collective-permute-start | bytes 196616 | tf_op jit(solution)/shard_map/ppermute | solution.py:116
  7.2 11.6 %collective-permute-start.4 = (bf16[64,2048]{1,0:T(8,128)(2,1)S(1)}, bf16[64,2048]{1,0:T(8,128)(2,1)S(1)}, u32[]{:S(2)}, u32[]{:S(2)}) collective-permute-start(bf16[64,2048]{1,0:T(8,128)(2,1)S(1)} %constant_dynamic-slice_fusion), channel_id=1, source_target_pairs={{0,1},{1,0},{2,3},{3,2},{4,5},{5,4},{6,7},{7,6},{8,9},{9,8},{10,11... | collective-permute-start | bytes 786440 | tf_op jit(solution)/shard_map/ppermute | solution.py:116
  11.7 3.6 %collective-permute-start.3 = (bf16[16,128]{1,0:T(8,128)(2,1)S(1)}, bf16[16,128]{1,0:T(8,128)(2,1)S(1)}, u32[]{:S(2)}, u32[]{:S(2)}) collective-permute-start(bf16[16,128]{1,0:T(8,128)(2,1)S(1)} %slice.18), channel_id=1, source_target_pairs={{0,4},{4,0},{8,12},{12,8},{16,20},{20,16},{24,28},{28,24},{1,5},{5... | collective-permute-start | bytes 12296 | tf_op jit(solution)/shard_map/ppermute | solution.py:116
  11.8 7.7 %collective-permute-start.2 = (bf16[128,512]{1,0:T(8,128)(2,1)S(1)}, bf16[128,512]{1,0:T(8,128)(2,1)S(1)}, u32[]{:S(2)}, u32[]{:S(2)}) collective-permute-start(bf16[128,512]{1,0:T(8,128)(2,1)S(1)} %pad_maximum_fusion.1.refs_2_), channel_id=1, source_target_pairs={{0,8},{4,12},{8,0},{12,4},{16,24},{20,28},{24,16},{28,20},{1,9},{5... | collective-permute-start | bytes 393224 | tf_op jit(solution)/shard_map/ppermute | solution.py:116
  13.3 8.2 %collective-permute-start.10 = (bf16[128,512]{1,0:T(8,128)(2,1)S(1)}, bf16[128,512]{1,0:T(8,128)(2,1)S(1)}, u32[]{:S(2)}, u32[]{:S(2)}) collective-permute-start(bf16[128,512]{1,0:T(8,128)(2,1)S(1)} %pad_maximum_fusion.1.refs_2_), channel_id=1, source_target_pairs={{0,24},{4,28},{8,16},{12,20},{16,8},{20,12},{24,0},{28,4},{1,25},{... | collective-permute-start | bytes 393224 | tf_op jit(solution)/shard_map/ppermute | solution.py:116
  14.8 8.1 %collective-permute-start.8 = (bf16[128,512]{1,0:T(8,128)(2,1)S(1)}, bf16[128,512]{1,0:T(8,128)(2,1)S(1)}, u32[]{:S(2)}, u32[]{:S(2)}) collective-permute-start(bf16[128,512]{1,0:T(8,128)(2,1)S(1)} %pad_maximum_fusion.1.refs_2_), channel_id=1, source_target_pairs={{0,16},{4,20},{8,24},{12,28},{16,0},{20,4},{24,8},{28,12},{1,17},{... | collective-permute-start | bytes 393224 | tf_op jit(solution)/shard_map/ppermute | solution.py:116
  15.3 7.6 %collective-permute-start.6 = (bf16[128,512]{1,0:T(8,128)(2,1)S(1)}, bf16[128,512]{1,0:T(8,128)(2,1)S(1)}, u32[]{:S(2)}, u32[]{:S(2)}) collective-permute-start(bf16[128,512]{1,0:T(8,128)(2,1)S(1)} %pad_maximum_fusion.1.refs_2_), channel_id=1, source_target_pairs={{0,4},{4,0},{8,12},{12,8},{16,20},{20,16},{24,28},{28,24},{1,5},{5... | collective-permute-start | bytes 393224 | tf_op jit(solution)/shard_map/ppermute | solution.py:116
  15.3 23.6 %all-to-all-start = ((f16[4,2,128,256]{3,2,1,0:T(8,128)(2,1)}), f16[4,2,128,256]{3,2,1,0:T(8,128)(2,1)S(1)}, u32[]{:S(2)}, u32[]{:S(2)}) async-start(f16[4,2,128,256]{3,2,1,0:T(8,128)(2,1)} %bitcast), calls=%async_computation | async-start | bytes 1048576 | tf_op jit(solution)/shard_map/all_to_all | solution.py:140
  18.8 5.4 %copy-start = (bf16[256,4096]{1,0:T(8,128)(2,1)S(1)}, bf16[256,4096]{1,0:T(8,128)(2,1)}, u32[]{:S(2)}) copy-start(bf16[256,4096]{1,0:T(8,128)(2,1)} %support_hbm.1) | copy-start | bytes 6291460
  18.8 5.4 %copy-start.1 = (bf16[64,4096]{1,0:T(8,128)(2,1)S(1)}, bf16[64,4096]{1,0:T(8,128)(2,1)}, u32[]{:S(2)}) copy-start(bf16[64,4096]{1,0:T(8,128)(2,1)} %own_hbm.1) | copy-start | bytes 1572868
  18.9 5.4 %collective-permute-start.5 = (bf16[64,2048]{1,0:T(8,128)(2,1)S(1)}, bf16[64,2048]{1,0:T(8,128)(2,1)S(1)}, u32[]{:S(2)}, u32[]{:S(2)}) collective-permute-start(bf16[64,2048]{1,0:T(8,128)(2,1)S(1)} %collective-permute-done.4.refs_0_), channel_id=1, source_target_pairs={{0,4},{4,0},{8,12},{12,8},{16,20},{20,16},{24,28},{28,24},{1,5},{5... | collective-permute-start | bytes 786440 | tf_op jit(solution)/shard_map/ppermute | solution.py:116
  19.4 3.5 %collective-permute-start.7 = (bf16[128,512]{1,0:T(8,128)(2,1)S(1)}, bf16[128,512]{1,0:T(8,128)(2,1)S(1)}, u32[]{:S(2)}, u32[]{:S(2)}) collective-permute-start(bf16[128,512]{1,0:T(8,128)(2,1)S(1)} %collective-permute-done.2.refs_4_), channel_id=1, source_target_pairs={{0,4},{4,0},{8,12},{12,8},{16,20},{20,16},{24,28},{28,24},{1,5},{5... | collective-permute-start | bytes 393224 | tf_op jit(solution)/shard_map/ppermute | solution.py:116
  21.6 1.4 %collective-permute-start.11 = (bf16[128,512]{1,0:T(8,128)(2,1)S(1)}, bf16[128,512]{1,0:T(8,128)(2,1)S(1)}, u32[]{:S(2)}, u32[]{:S(2)}) collective-permute-start(bf16[128,512]{1,0:T(8,128)(2,1)S(1)} %collective-permute-done.10.refs_8_), channel_id=1, source_target_pairs={{0,4},{4,0},{8,12},{12,8},{16,20},{20,16},{24,28},{28,24},{1,5},{5... | collective-permute-start | bytes 393224 | tf_op jit(solution)/shard_map/ppermute | solution.py:116
  22.9 1.3 %collective-permute-start.9 = (bf16[128,512]{1,0:T(8,128)(2,1)S(1)}, bf16[128,512]{1,0:T(8,128)(2,1)S(1)}, u32[]{:S(2)}, u32[]{:S(2)}) collective-permute-start(bf16[128,512]{1,0:T(8,128)(2,1)S(1)} %collective-permute-done.8.refs_6_), channel_id=1, source_target_pairs={{0,4},{4,0},{8,12},{12,8},{16,20},{20,16},{24,28},{28,24},{1,5},{5... | collective-permute-start | bytes 393224 | tf_op jit(solution)/shard_map/ppermute | solution.py:116
  25.9 23.0 %copy-start.2 = (f32[2,128,256]{2,1,0:T(8,128)S(1)}, f32[2,128,256]{2,1,0:T(8,128)}, u32[]{:S(2)}) copy-start(f32[2,128,256]{2,1,0:T(8,128)} %refs_4_.1) | copy-start | bytes 786436
  25.9 5.0 %collective-permute-start.12 = (f32[64,256]{1,0:T(8,128)S(1)}, f32[64,256]{1,0:T(8,128)S(1)}, u32[]{:S(2)}, u32[]{:S(2)}) collective-permute-start(f32[64,256]{1,0:T(8,128)S(1)} %get-tuple-element.28), channel_id=1, source_target_pairs={{0,1},{1,0},{2,3},{3,2},{4,5},{5,4},{6,7},{7,6},{8,9},{9,8},{10,11... | collective-permute-start | bytes 196616 | tf_op jit(solution)/shard_map/ppermute | solution.py:116
  26.3 12.5 %collective-permute-start.13 = (f32[64,256]{1,0:T(8,128)S(1)}, f32[64,256]{1,0:T(8,128)S(1)}, u32[]{:S(2)}, u32[]{:S(2)}) collective-permute-start(f32[64,256]{1,0:T(8,128)S(1)} %get-tuple-element.29), channel_id=1, source_target_pairs={{0,2},{1,3},{2,0},{3,1},{4,6},{5,7},{6,4},{7,5},{8,10},{9,11},{10,... | collective-permute-start | bytes 196616 | tf_op jit(solution)/shard_map/ppermute | solution.py:116
  28.6 10.3 %collective-permute-start.14 = (f32[64,256]{1,0:T(8,128)S(1)}, f32[64,256]{1,0:T(8,128)S(1)}, u32[]{:S(2)}, u32[]{:S(2)}) collective-permute-start(f32[64,256]{1,0:T(8,128)S(1)} %get-tuple-element.30), channel_id=1, source_target_pairs={{0,3},{1,2},{2,1},{3,0},{4,7},{5,6},{6,5},{7,4},{8,11},{9,10},{10,... | collective-permute-start | bytes 196616 | tf_op jit(solution)/shard_map/ppermute | solution.py:116
  38.9 1.3 %collective-permute-start.15 = (f32[64,128]{1,0:T(8,128)S(1)}, f32[64,128]{1,0:T(8,128)S(1)}, u32[]{:S(2)}, u32[]{:S(2)}) collective-permute-start(f32[64,128]{1,0:T(8,128)S(1)} %select_select_fusion.1.mine_ref), channel_id=1, source_target_pairs={{0,4},{4,0},{8,12},{12,8},{16,20},{20,16},{24,28},{28,24},{1,5},{5... | collective-permute-start | bytes 98312 | tf_op jit(solution)/shard_map/ppermute | solution.py:116
  40.7 4.8 %collective-permute-start.16 = (f32[64,128]{1,0:T(8,128)S(1)}, f32[64,128]{1,0:T(8,128)S(1)}, u32[]{:S(2)}, u32[]{:S(2)}) collective-permute-start(f32[64,128]{1,0:T(8,128)S(1)} %head_kernel.1), channel_id=1, source_target_pairs={{0,24},{4,28},{8,16},{12,20},{16,8},{20,12},{24,0},{28,4},{1,25},{... | collective-permute-start | bytes 98312 | tf_op jit(solution)/shard_map/ppermute | solution.py:116
  43.2 3.9 %collective-permute-start.17 = (f32[64,128]{1,0:T(8,128)S(1)}, f32[64,128]{1,0:T(8,128)S(1)}, u32[]{:S(2)}, u32[]{:S(2)}) collective-permute-start(f32[64,128]{1,0:T(8,128)S(1)} %head_kernel.1), channel_id=1, source_target_pairs={{0,16},{4,20},{8,24},{12,28},{16,0},{20,4},{24,8},{28,12},{1,17},{... | collective-permute-start | bytes 98312 | tf_op jit(solution)/shard_map/ppermute | solution.py:116
  43.7 3.9 %collective-permute-start.18 = (f32[64,128]{1,0:T(8,128)S(1)}, f32[64,128]{1,0:T(8,128)S(1)}, u32[]{:S(2)}, u32[]{:S(2)}) collective-permute-start(f32[64,128]{1,0:T(8,128)S(1)} %head_kernel.1), channel_id=1, source_target_pairs={{0,8},{4,12},{8,0},{12,4},{16,24},{20,28},{24,16},{28,20},{1,9},{5... | collective-permute-start | bytes 98312 | tf_op jit(solution)/shard_map/ppermute | solution.py:116
  47.6 1.3 %collective-permute-start.19 = (f32[64,128]{1,0:T(8,128)S(1)}, f32[64,128]{1,0:T(8,128)S(1)}, u32[]{:S(2)}, u32[]{:S(2)}) collective-permute-start(f32[64,128]{1,0:T(8,128)S(1)} %select_select_fusion.refs_6_), channel_id=1, source_target_pairs={{0,4},{4,0},{8,12},{12,8},{16,20},{20,16},{24,28},{28,24},{1,5},{5... | collective-permute-start | bytes 98312 | tf_op jit(solution)/shard_map/ppermute | solution.py:116

commit v3 on v2

--- a/solution.py
+++ b/solution.py
@@ -50,8 +50,7 @@
         copy.wait()
 
 
-def mark_kernel(value_ref, token_ref, out_ref):
-    del token_ref
+def mark_kernel(value_ref, out_ref):
     out_ref[...] = value_ref[0, :8, :128]
 
 
@@ -134,23 +133,20 @@
     far = jnp.concatenate([exchange(mine, "col", n_col, j) for j in range(2, n_col)], axis=0)
     small = jnp.concatenate([panels * PANEL_UNIT] * n_col, axis=0).astype(jnp.float16)
     small = small.reshape(n_col, *panels.shape)
-    far, small, marked = together(far, small, diag_inverses)
-    token = exchange(far[:16, :128], "row", n_row, 1)
-    small, token = together(small, token)
     blocks = lax.all_to_all(small, "col", 0, 0)
     mark = pl.pallas_call(
         mark_kernel,
         grid=(1,),
         out_shape=jax.ShapeDtypeStruct((8, 128), jnp.float32),
-        in_specs=[pl.BlockSpec((1, 8, 128), lambda i: (0, 0, 0)), VMEM],
+        in_specs=[pl.BlockSpec((1, 8, 128), lambda i: (0, 0, 0))],
         out_specs=VMEM,
         compiler_params=SOLVE_PARAMS,
         cost_estimate=LONG,
         name="mark_kernel",
-    )(marked, token)
+    )(diag_inverses)
+    far, mark = together(far, mark)
     near = [near, exchange(near, "row", n_row, 1)]
     far = [far] + [exchange(far, "row", n_row, i) for i in range(2, n_row, 2)]
-    far[1], mark = together(far[1], mark)
     far = [p for own in far for p in (own, exchange(own, "row", n_row, 1))]
 
     made = pl.pallas_call(

time: 50.2 us -> 46.6 us (0.928)
  waiting for transfers between devices: 21.2 us -> 16.7 us
  starting transfers between devices: 21.6 us -> 22.5 us
    ppermute x20 -> x19, waiting for transfers between devices: 21.2 us -> 16.7 us  [exchange(): return lax.ppermute(value, axis, [(i, i ^ mask) for i in range(size)])]
    all_to_all x1, starting transfers between devices: 3.51 us -> 4.19 us  [shards(): blocks = lax.all_to_all(small, 'col', 0, 0)]
    ppermute x20 -> x19, starting transfers between devices: 18.1 us -> 18.3 us  [exchange(): return lax.ppermute(value, axis, [(i, i ^ mask) for i in range(size)])]
  transfers between devices with their start and end apart: 21 -> 20, of which waited for: 11 -> 12; matrix products, arithmetic and copies ran while one was open for 6% -> 6% of each run, Pallas kernels for 3% -> 3%
where the time goes in v3:
time: 46.6 us; the launch traced here: 46.4 us
  starting transfers between devices  22.5 us (48%)
  waiting for transfers between devices  16.7 us (36%)
  Pallas kernels  3.2 us (7%)
  other arithmetic  2.03 us (4%)
  local copies, waits for them, and re-layouts  1.86 us (4%)
    ppermute x19, starting transfers between devices, exchange(): return lax.ppermute(value, axis, [(i, i ^ mask) for i in range(size)])  18.3 us
    ppermute x19, waiting for transfers between devices, exchange(): return lax.ppermute(value, axis, [(i, i ^ mask) for i in range(size)])  16.7 us
    all_to_all x1, starting transfers between devices, shards(): blocks = lax.all_to_all(small, 'col', 0, 0)  4.19 us
    pallas_call x1, Pallas kernels, shards(): pl.pallas_call(functools.partial(tile_kernel, scale, n_row, n_col), out_s...  1.59 us
    pallas_call x1, Pallas kernels, shards(): pl.pallas_call(functools.partial(solve_kernel, n_col, pivot), out_shape=j...  1.08 us
    another operation x1, other arithmetic  0.97 us
    dynamic_slice x1, local copies, waits for them, and re-layouts, shards(): lax.dynamic_slice(targets, (0, row % 2 * (features // 2)), (rows, feature...  0.97 us
  transfers between devices with their start and end apart: 20, of which 12 were waited for; matrix products, arithmetic and copies ran while one was open for 6% of the time, Pallas kernels for 3%

profile of v3, /device:TPU:0, one launch (start us, length us, event | category | flops | bytes accessed | tf_op | source)
XLA Modules:
  0.0 46.4 jit_solution(11872552020293213414)
XLA Ops:
  0.0 0.9 %constant_dynamic-slice_fusion.1 = bf16[64,512]{1,0:T(8,128)(2,1)S(1)} fusion(bf16[64,4096]{1,0:T(8,128)(2,1)} %own_hbm.1, s32[]{:T(128)S(6)} %select_n.62), kind=kLoop, calls=%fused_computation.8 | loop fusion | bytes 131076 | tf_op jit(solution)/shard_map/dynamic_slice | solution.py:131
  0.9 4.0 %collective-permute-start = (bf16[64,512]{1,0:T(8,128)(2,1)S(1)}, bf16[64,512]{1,0:T(8,128)(2,1)S(1)}, u32[]{:S(2)}, u32[]{:S(2)}) collective-permute-start(bf16[64,512]{1,0:T(8,128)(2,1)S(1)} %constant_dynamic-slice_fusion.1), channel_id=1, source_target_pairs={{0,2},{1,3},{2,0},{3,1},{4,6},{5,7},{6,4},{7,5},{8,10},{9,11},{10,... | collective-permute-start | bytes 196616 | tf_op jit(solution)/shard_map/ppermute | solution.py:115
  4.9 1.3 %collective-permute-start.1 = (bf16[64,512]{1,0:T(8,128)(2,1)S(1)}, bf16[64,512]{1,0:T(8,128)(2,1)S(1)}, u32[]{:S(2)}, u32[]{:S(2)}) collective-permute-start(bf16[64,512]{1,0:T(8,128)(2,1)S(1)} %constant_dynamic-slice_fusion.1), channel_id=1, source_target_pairs={{0,3},{1,2},{2,1},{3,0},{4,7},{5,6},{6,5},{7,4},{8,11},{9,10},{10,... | collective-permute-start | bytes 196616 | tf_op jit(solution)/shard_map/ppermute | solution.py:115
  6.3 1.0 %constant_dynamic-slice_fusion = bf16[64,2048]{1,0:T(8,128)(2,1)S(1)} fusion(bf16[64,4096]{1,0:T(8,128)(2,1)} %own_hbm.1, s32[]{:T(128)S(6)} %select_n.63), kind=kLoop, calls=%fused_computation.7 | loop fusion | bytes 524292 | tf_op jit(solution)/shard_map/dynamic_slice | solution.py:130
  7.2 0.3 collective-permute-start.2
  7.5 1.0 %multiply_convert_fusion = f16[2,128,256]{2,1,0:T(8,128)(2,1)S(1)} fusion(f32[2,128,256]{2,1,0:T(8,128)} %refs_4_.1), kind=kLoop, calls=%fused_computation.2 | loop fusion | flops 131072 | bytes 393216 | tf_op jit(solution)/shard_map/convert
  8.5 0.9 %pad_maximum_fusion = f16[8,128,256]{2,1,0:T(8,128)(2,1)} fusion(f16[2,128,256]{2,1,0:T(8,128)(2,1)S(1)} %multiply_convert_fusion), kind=kLoop, calls=%fused_computation.1 | loop fusion | flops 786432 | bytes 655360 | tf_op jit(solution)/shard_map/concatenate | solution.py:134
  9.4 4.2 %all-to-all-start = ((f16[4,2,128,256]{3,2,1,0:T(8,128)(2,1)}), f16[4,2,128,256]{3,2,1,0:T(8,128)(2,1)S(1)}, u32[]{:S(2)}, u32[]{:S(2)}) async-start(f16[4,2,128,256]{3,2,1,0:T(8,128)(2,1)} %bitcast), calls=%async_computation | async-start | bytes 1048576 | tf_op jit(solution)/shard_map/all_to_all | solution.py:136
  13.7 2.5 %collective-permute-start.9 = (bf16[128,512]{1,0:T(8,128)(2,1)S(1)}, bf16[128,512]{1,0:T(8,128)(2,1)S(1)}, u32[]{:S(2)}, u32[]{:S(2)}) collective-permute-start(bf16[128,512]{1,0:T(8,128)(2,1)S(1)} %pad_maximum_fusion.1.refs_2_), channel_id=1, source_target_pairs={{0,24},{4,28},{8,16},{12,20},{16,8},{20,12},{24,0},{28,4},{1,25},{... | collective-permute-start | bytes 393224 | tf_op jit(solution)/shard_map/ppermute | solution.py:115
  16.2 0.5 %collective-permute-start.5 = (bf16[128,512]{1,0:T(8,128)(2,1)S(1)}, bf16[128,512]{1,0:T(8,128)(2,1)S(1)}, u32[]{:S(2)}, u32[]{:S(2)}) collective-permute-start(bf16[128,512]{1,0:T(8,128)(2,1)S(1)} %pad_maximum_fusion.1.refs_2_), channel_id=1, source_target_pairs={{0,8},{4,12},{8,0},{12,4},{16,24},{20,28},{24,16},{28,20},{1,9},{5... | collective-permute-start | bytes 393224 | tf_op jit(solution)/shard_map/ppermute | solution.py:115
  16.7 0.5 %collective-permute-start.7 = (bf16[128,512]{1,0:T(8,128)(2,1)S(1)}, bf16[128,512]{1,0:T(8,128)(2,1)S(1)}, u32[]{:S(2)}, u32[]{:S(2)}) collective-permute-start(bf16[128,512]{1,0:T(8,128)(2,1)S(1)} %pad_maximum_fusion.1.refs_2_), channel_id=1, source_target_pairs={{0,16},{4,20},{8,24},{12,28},{16,0},{20,4},{24,8},{28,12},{1,17},{... | collective-permute-start | bytes 393224 | tf_op jit(solution)/shard_map/ppermute | solution.py:115
  17.2 0.5 %collective-permute-start.4 = (bf16[128,512]{1,0:T(8,128)(2,1)S(1)}, bf16[128,512]{1,0:T(8,128)(2,1)S(1)}, u32[]{:S(2)}, u32[]{:S(2)}) collective-permute-start(bf16[128,512]{1,0:T(8,128)(2,1)S(1)} %pad_maximum_fusion.1.refs_2_), channel_id=1, source_target_pairs={{0,4},{4,0},{8,12},{12,8},{16,20},{20,16},{24,28},{28,24},{1,5},{5... | collective-permute-start | bytes 393224 | tf_op jit(solution)/shard_map/ppermute | solution.py:115
  17.8 2.5 %collective-permute-done.9.refs_8_ = bf16[128,512]{1,0:T(8,128)(2,1)S(1)} collective-permute-done((bf16[128,512]{1,0:T(8,128)(2,1)S(1)}, bf16[128,512]{1,0:T(8,128)(2,1)S(1)}, u32[]{:S(2)}, u32[]{:S(2)}) %collective-permute-start.9) | collective-permute-done | bytes 131104 | tf_op jit(solution)/shard_map/ppermute | solution.py:115
  20.3 1.3 %collective-permute-done.5.refs_4_ = bf16[128,512]{1,0:T(8,128)(2,1)S(1)} collective-permute-done((bf16[128,512]{1,0:T(8,128)(2,1)S(1)}, bf16[128,512]{1,0:T(8,128)(2,1)S(1)}, u32[]{:S(2)}, u32[]{:S(2)}) %collective-permute-start.5) | collective-permute-done | bytes 131104 | tf_op jit(solution)/shard_map/ppermute | solution.py:115
  21.7 0.4 collective-permute-start.8
  22.2 0.8 %collective-permute-done.6.refs_5_ = bf16[128,512]{1,0:T(8,128)(2,1)S(1)} collective-permute-done((bf16[128,512]{1,0:T(8,128)(2,1)S(1)}, bf16[128,512]{1,0:T(8,128)(2,1)S(1)}, u32[]{:S(2)}, u32[]{:S(2)}) %collective-permute-start.6) | collective-permute-done | bytes 131104 | tf_op jit(solution)/shard_map/ppermute | solution.py:115
  23.0 0.2 collective-permute-done.8.refs_7_
  23.2 1.6 %tile_kernel.1 = (f32[64,256]{1,0:T(8,128)S(1)}, f32[64,256]{1,0:T(8,128)S(1)}, f32[64,256]{1,0:T(8,128)S(1)}, f32[64,256]{1,0:T(8,128)S(1)}) custom-call(bf16[64,4096]{1,0:T(8,128)(2,1)S(1)} %copy-done.1, bf16[256,4096]{1,0:T(8,128)(2,1)S(1)} %copy-done, f32[8,128]{1,0:T(8,128)S(1)} %mark_kernel.1._, bf16[64,2048]{1,0:T(8,128)(2,1)S(1)} %collective-permute-done.2.refs_0_, ...), custom_call_target="tpu_custom_call" | custom-call | flops 1000000 | tf_op jit(solution)/shard_map/tile_kernel/pallas_call | solution.py:152
  24.8 2.0 %collective-permute-start.11 = (f32[64,256]{1,0:T(8,128)S(1)}, f32[64,256]{1,0:T(8,128)S(1)}, u32[]{:S(2)}, u32[]{:S(2)}) collective-permute-start(f32[64,256]{1,0:T(8,128)S(1)} %get-tuple-element.19), channel_id=1, source_target_pairs={{0,1},{1,0},{2,3},{3,2},{4,5},{5,4},{6,7},{7,6},{8,9},{9,8},{10,11... | collective-permute-start | bytes 196616 | tf_op jit(solution)/shard_map/ppermute | solution.py:115
  26.8 2.4 %collective-permute-start.12 = (f32[64,256]{1,0:T(8,128)S(1)}, f32[64,256]{1,0:T(8,128)S(1)}, u32[]{:S(2)}, u32[]{:S(2)}) collective-permute-start(f32[64,256]{1,0:T(8,128)S(1)} %get-tuple-element.20), channel_id=1, source_target_pairs={{0,2},{1,3},{2,0},{3,1},{4,6},{5,7},{6,4},{7,5},{8,10},{9,11},{10,... | collective-permute-start | bytes 196616 | tf_op jit(solution)/shard_map/ppermute | solution.py:115
  29.2 5.1 %collective-permute-done.12.refs_2_ = f32[64,256]{1,0:T(8,128)S(1)} collective-permute-done((f32[64,256]{1,0:T(8,128)S(1)}, f32[64,256]{1,0:T(8,128)S(1)}, u32[]{:S(2)}, u32[]{:S(2)}) %collective-permute-start.12) | collective-permute-done | bytes 65568 | tf_op jit(solution)/shard_map/ppermute | solution.py:115
  34.3 1.0 %collective-permute-done.13.refs_3_ = f32[64,256]{1,0:T(8,128)S(1)} collective-permute-done((f32[64,256]{1,0:T(8,128)S(1)}, f32[64,256]{1,0:T(8,128)S(1)}, u32[]{:S(2)}, u32[]{:S(2)}) %collective-permute-start.13) | collective-permute-done | bytes 65568 | tf_op jit(solution)/shard_map/ppermute | solution.py:115
  35.4 1.2 %collective-permute-done.14.other_ref = f32[64,128]{1,0:T(8,128)S(1)} collective-permute-done((f32[64,128]{1,0:T(8,128)S(1)}, f32[64,128]{1,0:T(8,128)S(1)}, u32[]{:S(2)}, u32[]{:S(2)}) %collective-permute-start.14) | collective-permute-done | bytes 32800 | tf_op jit(solution)/shard_map/ppermute | solution.py:115
  36.6 0.5 %head_kernel.1 = f32[64,128]{1,0:T(8,128)S(1)} custom-call(f32[64,128]{1,0:T(8,128)S(1)} %select_select_fusion.1.mine_ref, f32[64,128]{1,0:T(8,128)S(1)} %collective-permute-done.14.other_ref, f32[128,128]{1,0:T(8,128)S(1)} %multiply_bitcast_fusion.corner_ref, f32[2,128,128]{2,1,0:T(8,128)S(1)} %copy-done.3), custom_call_target="tpu_custom_call" | custom-call | flops 1000000 | tf_op jit(solution)/shard_map/head_kernel/pallas_call | solution.py:173
  37.1 2.1 %collective-permute-start.15 = (f32[64,128]{1,0:T(8,128)S(1)}, f32[64,128]{1,0:T(8,128)S(1)}, u32[]{:S(2)}, u32[]{:S(2)}) collective-permute-start(f32[64,128]{1,0:T(8,128)S(1)} %head_kernel.1), channel_id=1, source_target_pairs={{0,24},{4,28},{8,16},{12,20},{16,8},{20,12},{24,0},{28,4},{1,25},{... | collective-permute-start | bytes 98312 | tf_op jit(solution)/shard_map/ppermute | solution.py:115
  39.2 0.9 %collective-permute-start.16 = (f32[64,128]{1,0:T(8,128)S(1)}, f32[64,128]{1,0:T(8,128)S(1)}, u32[]{:S(2)}, u32[]{:S(2)}) collective-permute-start(f32[64,128]{1,0:T(8,128)S(1)} %head_kernel.1), channel_id=1, source_target_pairs={{0,16},{4,20},{8,24},{12,28},{16,0},{20,4},{24,8},{28,12},{1,17},{... | collective-permute-start | bytes 98312 | tf_op jit(solution)/shard_map/ppermute | solution.py:115
  40.1 0.5 %collective-permute-start.17 = (f32[64,128]{1,0:T(8,128)S(1)}, f32[64,128]{1,0:T(8,128)S(1)}, u32[]{:S(2)}, u32[]{:S(2)}) collective-permute-start(f32[64,128]{1,0:T(8,128)S(1)} %head_kernel.1), channel_id=1, source_target_pairs={{0,8},{4,12},{8,0},{12,4},{16,24},{20,28},{24,16},{28,20},{1,9},{5... | collective-permute-start | bytes 98312 | tf_op jit(solution)/shard_map/ppermute | solution.py:115
  40.6 1.4 %collective-permute-done.15 = f32[64,128]{1,0:T(8,128)S(1)} collective-permute-done((f32[64,128]{1,0:T(8,128)S(1)}, f32[64,128]{1,0:T(8,128)S(1)}, u32[]{:S(2)}, u32[]{:S(2)}) %collective-permute-start.15) | collective-permute-done | bytes 32800 | tf_op jit(solution)/shard_map/ppermute | solution.py:115
  42.0 1.1 %collective-permute-done.16 = f32[64,128]{1,0:T(8,128)S(1)} collective-permute-done((f32[64,128]{1,0:T(8,128)S(1)}, f32[64,128]{1,0:T(8,128)S(1)}, u32[]{:S(2)}, u32[]{:S(2)}) %collective-permute-start.16) | collective-permute-done | bytes 32800 | tf_op jit(solution)/shard_map/ppermute | solution.py:115
  43.1 0.9 %collective-permute-done.17 = f32[64,128]{1,0:T(8,128)S(1)} collective-permute-done((f32[64,128]{1,0:T(8,128)S(1)}, f32[64,128]{1,0:T(8,128)S(1)}, u32[]{:S(2)}, u32[]{:S(2)}) %collective-permute-start.17) | collective-permute-done | bytes 32800 | tf_op jit(solution)/shard_map/ppermute | solution.py:115
  44.2 1.1 %collective-permute-done.18.refs_7_ = f32[64,128]{1,0:T(8,128)S(1)} collective-permute-done((f32[64,128]{1,0:T(8,128)S(1)}, f32[64,128]{1,0:T(8,128)S(1)}, u32[]{:S(2)}, u32[]{:S(2)}) %collective-permute-start.18) | collective-permute-done | bytes 32800 | tf_op jit(solution)/shard_map/ppermute | solution.py:115
  45.3 1.1 %solve_kernel.1 = f32[64,1024]{1,0:T(8,128)} custom-call(f32[64,256]{1,0:T(8,128)S(1)} %get-tuple-element.22.refs_0_, f32[64,256]{1,0:T(8,128)S(1)} %collective-permute-done.11.refs_1_, f32[64,256]{1,0:T(8,128)S(1)} %collective-permute-done.12.refs_2_, f32[64,256]{1,0:T(8,128)S(1)} %collective-permute-done.13.refs_3_, f32[2,128,256]{2,1,0:T(8,128)S(1)} %copy-done.2, ...), custom_call_target="tpu_custom_call" | custom-call | tf_op jit(solution)/shard_map/solve_kernel/pallas_call | solution.py:188
  (29 shorter events, 0.5 us)
Async XLA Ops:
  0.0 13.6 %copy-start.3 = (f32[2,128,128]{2,1,0:T(8,128)S(1)}, f32[2,128,128]{2,1,0:T(8,128)}, u32[]{:S(2)}) copy-start(f32[2,128,128]{2,1,0:T(8,128)} %inverse_ref.1) | copy-start | bytes 393220
  0.9 12.8 %collective-permute-start = (bf16[64,512]{1,0:T(8,128)(2,1)S(1)}, bf16[64,512]{1,0:T(8,128)(2,1)S(1)}, u32[]{:S(2)}, u32[]{:S(2)}) collective-permute-start(bf16[64,512]{1,0:T(8,128)(2,1)S(1)} %constant_dynamic-slice_fusion.1), channel_id=1, source_target_pairs={{0,2},{1,3},{2,0},{3,1},{4,6},{5,7},{6,4},{7,5},{8,10},{9,11},{10,... | collective-permute-start | bytes 196616 | tf_op jit(solution)/shard_map/ppermute | solution.py:115
  4.9 8.7 %collective-permute-start.1 = (bf16[64,512]{1,0:T(8,128)(2,1)S(1)}, bf16[64,512]{1,0:T(8,128)(2,1)S(1)}, u32[]{:S(2)}, u32[]{:S(2)}) collective-permute-start(bf16[64,512]{1,0:T(8,128)(2,1)S(1)} %constant_dynamic-slice_fusion.1), channel_id=1, source_target_pairs={{0,3},{1,2},{2,1},{3,0},{4,7},{5,6},{6,5},{7,4},{8,11},{9,10},{10,... | collective-permute-start | bytes 196616 | tf_op jit(solution)/shard_map/ppermute | solution.py:115
  7.2 10.0 %collective-permute-start.2 = (bf16[64,2048]{1,0:T(8,128)(2,1)S(1)}, bf16[64,2048]{1,0:T(8,128)(2,1)S(1)}, u32[]{:S(2)}, u32[]{:S(2)}) collective-permute-start(bf16[64,2048]{1,0:T(8,128)(2,1)S(1)} %constant_dynamic-slice_fusion), channel_id=1, source_target_pairs={{0,1},{1,0},{2,3},{3,2},{4,5},{5,4},{6,7},{7,6},{8,9},{9,8},{10,11... | collective-permute-start | bytes 786440 | tf_op jit(solution)/shard_map/ppermute | solution.py:115
  9.4 25.9 %all-to-all-start = ((f16[4,2,128,256]{3,2,1,0:T(8,128)(2,1)}), f16[4,2,128,256]{3,2,1,0:T(8,128)(2,1)S(1)}, u32[]{:S(2)}, u32[]{:S(2)}) async-start(f16[4,2,128,256]{3,2,1,0:T(8,128)(2,1)} %bitcast), calls=%async_computation | async-start | bytes 1048576 | tf_op jit(solution)/shard_map/all_to_all | solution.py:136
  13.6 9.5 %copy-start = (bf16[256,4096]{1,0:T(8,128)(2,1)S(1)}, bf16[256,4096]{1,0:T(8,128)(2,1)}, u32[]{:S(2)}) copy-start(bf16[256,4096]{1,0:T(8,128)(2,1)} %support_hbm.1) | copy-start | bytes 6291460
  13.6 9.6 %copy-start.1 = (bf16[64,4096]{1,0:T(8,128)(2,1)S(1)}, bf16[64,4096]{1,0:T(8,128)(2,1)}, u32[]{:S(2)}) copy-start(bf16[64,4096]{1,0:T(8,128)(2,1)} %own_hbm.1) | copy-start | bytes 1572868
  13.7 6.6 %collective-permute-start.9 = (bf16[128,512]{1,0:T(8,128)(2,1)S(1)}, bf16[128,512]{1,0:T(8,128)(2,1)S(1)}, u32[]{:S(2)}, u32[]{:S(2)}) collective-permute-start(bf16[128,512]{1,0:T(8,128)(2,1)S(1)} %pad_maximum_fusion.1.refs_2_), channel_id=1, source_target_pairs={{0,24},{4,28},{8,16},{12,20},{16,8},{20,12},{24,0},{28,4},{1,25},{... | collective-permute-start | bytes 393224 | tf_op jit(solution)/shard_map/ppermute | solution.py:115
  16.2 5.4 %collective-permute-start.5 = (bf16[128,512]{1,0:T(8,128)(2,1)S(1)}, bf16[128,512]{1,0:T(8,128)(2,1)S(1)}, u32[]{:S(2)}, u32[]{:S(2)}) collective-permute-start(bf16[128,512]{1,0:T(8,128)(2,1)S(1)} %pad_maximum_fusion.1.refs_2_), channel_id=1, source_target_pairs={{0,8},{4,12},{8,0},{12,4},{16,24},{20,28},{24,16},{28,20},{1,9},{5... | collective-permute-start | bytes 393224 | tf_op jit(solution)/shard_map/ppermute | solution.py:115
  16.7 5.0 %collective-permute-start.7 = (bf16[128,512]{1,0:T(8,128)(2,1)S(1)}, bf16[128,512]{1,0:T(8,128)(2,1)S(1)}, u32[]{:S(2)}, u32[]{:S(2)}) collective-permute-start(bf16[128,512]{1,0:T(8,128)(2,1)S(1)} %pad_maximum_fusion.1.refs_2_), channel_id=1, source_target_pairs={{0,16},{4,20},{8,24},{12,28},{16,0},{20,4},{24,8},{28,12},{1,17},{... | collective-permute-start | bytes 393224 | tf_op jit(solution)/shard_map/ppermute | solution.py:115
  17.2 5.9 %collective-permute-start.3 = (bf16[64,2048]{1,0:T(8,128)(2,1)S(1)}, bf16[64,2048]{1,0:T(8,128)(2,1)S(1)}, u32[]{:S(2)}, u32[]{:S(2)}) collective-permute-start(bf16[64,2048]{1,0:T(8,128)(2,1)S(1)} %collective-permute-done.2.refs_0_), channel_id=1, source_target_pairs={{0,4},{4,0},{8,12},{12,8},{16,20},{20,16},{24,28},{28,24},{1,5},{5... | collective-permute-start | bytes 786440 | tf_op jit(solution)/shard_map/ppermute | solution.py:115
  17.2 4.9 %collective-permute-start.4 = (bf16[128,512]{1,0:T(8,128)(2,1)S(1)}, bf16[128,512]{1,0:T(8,128)(2,1)S(1)}, u32[]{:S(2)}, u32[]{:S(2)}) collective-permute-start(bf16[128,512]{1,0:T(8,128)(2,1)S(1)} %pad_maximum_fusion.1.refs_2_), channel_id=1, source_target_pairs={{0,4},{4,0},{8,12},{12,8},{16,20},{20,16},{24,28},{28,24},{1,5},{5... | collective-permute-start | bytes 393224 | tf_op jit(solution)/shard_map/ppermute | solution.py:115
  20.3 1.9 %collective-permute-start.10 = (bf16[128,512]{1,0:T(8,128)(2,1)S(1)}, bf16[128,512]{1,0:T(8,128)(2,1)S(1)}, u32[]{:S(2)}, u32[]{:S(2)}) collective-permute-start(bf16[128,512]{1,0:T(8,128)(2,1)S(1)} %collective-permute-done.9.refs_8_), channel_id=1, source_target_pairs={{0,4},{4,0},{8,12},{12,8},{16,20},{20,16},{24,28},{28,24},{1,5},{5... | collective-permute-start | bytes 393224 | tf_op jit(solution)/shard_map/ppermute | solution.py:115
  21.6 1.3 %collective-permute-start.6 = (bf16[128,512]{1,0:T(8,128)(2,1)S(1)}, bf16[128,512]{1,0:T(8,128)(2,1)S(1)}, u32[]{:S(2)}, u32[]{:S(2)}) collective-permute-start(bf16[128,512]{1,0:T(8,128)(2,1)S(1)} %collective-permute-done.5.refs_4_), channel_id=1, source_target_pairs={{0,4},{4,0},{8,12},{12,8},{16,20},{20,16},{24,28},{28,24},{1,5},{5... | collective-permute-start | bytes 393224 | tf_op jit(solution)/shard_map/ppermute | solution.py:115
  21.7 1.5 %collective-permute-start.8 = (bf16[128,512]{1,0:T(8,128)(2,1)S(1)}, bf16[128,512]{1,0:T(8,128)(2,1)S(1)}, u32[]{:S(2)}, u32[]{:S(2)}) collective-permute-start(bf16[128,512]{1,0:T(8,128)(2,1)S(1)} %collective-permute-done.7.refs_6_), channel_id=1, source_target_pairs={{0,4},{4,0},{8,12},{12,8},{16,20},{20,16},{24,28},{28,24},{1,5},{5... | collective-permute-start | bytes 393224 | tf_op jit(solution)/shard_map/ppermute | solution.py:115
  24.8 20.5 %copy-start.2 = (f32[2,128,256]{2,1,0:T(8,128)S(1)}, f32[2,128,256]{2,1,0:T(8,128)}, u32[]{:S(2)}) copy-start(f32[2,128,256]{2,1,0:T(8,128)} %refs_4_.1) | copy-start | bytes 786436
  24.8 4.5 %collective-permute-start.11 = (f32[64,256]{1,0:T(8,128)S(1)}, f32[64,256]{1,0:T(8,128)S(1)}, u32[]{:S(2)}, u32[]{:S(2)}) collective-permute-start(f32[64,256]{1,0:T(8,128)S(1)} %get-tuple-element.19), channel_id=1, source_target_pairs={{0,1},{1,0},{2,3},{3,2},{4,5},{5,4},{6,7},{7,6},{8,9},{9,8},{10,11... | collective-permute-start | bytes 196616 | tf_op jit(solution)/shard_map/ppermute | solution.py:115
  26.8 7.6 %collective-permute-start.12 = (f32[64,256]{1,0:T(8,128)S(1)}, f32[64,256]{1,0:T(8,128)S(1)}, u32[]{:S(2)}, u32[]{:S(2)}) collective-permute-start(f32[64,256]{1,0:T(8,128)S(1)} %get-tuple-element.20), channel_id=1, source_target_pairs={{0,2},{1,3},{2,0},{3,1},{4,6},{5,7},{6,4},{7,5},{8,10},{9,11},{10,... | collective-permute-start | bytes 196616 | tf_op jit(solution)/shard_map/ppermute | solution.py:115
  29.1 6.2 %collective-permute-start.13 = (f32[64,256]{1,0:T(8,128)S(1)}, f32[64,256]{1,0:T(8,128)S(1)}, u32[]{:S(2)}, u32[]{:S(2)}) collective-permute-start(f32[64,256]{1,0:T(8,128)S(1)} %get-tuple-element.21), channel_id=1, source_target_pairs={{0,3},{1,2},{2,1},{3,0},{4,7},{5,6},{6,5},{7,4},{8,11},{9,10},{10,... | collective-permute-start | bytes 196616 | tf_op jit(solution)/shard_map/ppermute | solution.py:115
  35.3 1.3 %collective-permute-start.14 = (f32[64,128]{1,0:T(8,128)S(1)}, f32[64,128]{1,0:T(8,128)S(1)}, u32[]{:S(2)}, u32[]{:S(2)}) collective-permute-start(f32[64,128]{1,0:T(8,128)S(1)} %select_select_fusion.1.mine_ref), channel_id=1, source_target_pairs={{0,4},{4,0},{8,12},{12,8},{16,20},{20,16},{24,28},{28,24},{1,5},{5... | collective-permute-start | bytes 98312 | tf_op jit(solution)/shard_map/ppermute | solution.py:115
  37.1 4.9 %collective-permute-start.15 = (f32[64,128]{1,0:T(8,128)S(1)}, f32[64,128]{1,0:T(8,128)S(1)}, u32[]{:S(2)}, u32[]{:S(2)}) collective-permute-start(f32[64,128]{1,0:T(8,128)S(1)} %head_kernel.1), channel_id=1, source_target_pairs={{0,24},{4,28},{8,16},{12,20},{16,8},{20,12},{24,0},{28,4},{1,25},{... | collective-permute-start | bytes 98312 | tf_op jit(solution)/shard_map/ppermute | solution.py:115
  39.2 3.9 %collective-permute-start.16 = (f32[64,128]{1,0:T(8,128)S(1)}, f32[64,128]{1,0:T(8,128)S(1)}, u32[]{:S(2)}, u32[]{:S(2)}) collective-permute-start(f32[64,128]{1,0:T(8,128)S(1)} %head_kernel.1), channel_id=1, source_target_pairs={{0,16},{4,20},{8,24},{12,28},{16,0},{20,4},{24,8},{28,12},{1,17},{... | collective-permute-start | bytes 98312 | tf_op jit(solution)/shard_map/ppermute | solution.py:115
  40.1 3.9 %collective-permute-start.17 = (f32[64,128]{1,0:T(8,128)S(1)}, f32[64,128]{1,0:T(8,128)S(1)}, u32[]{:S(2)}, u32[]{:S(2)}) collective-permute-start(f32[64,128]{1,0:T(8,128)S(1)} %head_kernel.1), channel_id=1, source_target_pairs={{0,8},{4,12},{8,0},{12,4},{16,24},{20,28},{24,16},{28,20},{1,9},{5... | collective-permute-start | bytes 98312 | tf_op jit(solution)/shard_map/ppermute | solution.py:115
  44.0 1.3 %collective-permute-start.18 = (f32[64,128]{1,0:T(8,128)S(1)}, f32[64,128]{1,0:T(8,128)S(1)}, u32[]{:S(2)}, u32[]{:S(2)}) collective-permute-start(f32[64,128]{1,0:T(8,128)S(1)} %select_select_fusion.refs_6_), channel_id=1, source_target_pairs={{0,4},{4,0},{8,12},{12,8},{16,20},{20,16},{24,28},{28,24},{1,5},{5... | collective-permute-start | bytes 98312 | tf_op jit(solution)/shard_map/ppermute | solution.py:115

commit v4 on v3

--- a/solution.py
+++ b/solution.py
@@ -34,10 +34,6 @@
     return dot(a_high, b_high, dims) + (dot(a_low, b_high, dims) + dot(a_high, b_low, dims))
 
 
-def slice_of(row, n_row):
-    return (row % 2) * (n_row // 2) + row // 2
-
-
 def start_all(pairs, sems):
     copies = [pltpu.make_async_copy(source, target, sems.at[i]) for i, (source, target) in enumerate(pairs)]
     for copy in copies:
@@ -50,29 +46,44 @@
         copy.wait()
 
 
+def cut_kernel(n_row, targets_hbm, mine_ref, half_ref, sems):
+    row = lax.axis_index("row")
+    (_, width), (_, half) = mine_ref.shape, half_ref.shape
+    mine = pl.ds(pl.multiple_of((row // 2) * width, width), width)
+    core = pl.ds(pl.multiple_of((row % 2) * half, half), half)
+    wait_all(start_all([(targets_hbm.at[:, mine], mine_ref), (targets_hbm.at[:, core], half_ref)], sems))
+
+
 def mark_kernel(value_ref, out_ref):
     out_ref[...] = value_ref[0, :8, :128]
 
 
 def tile_kernel(scale, n_row, n_col, own_hbm, support_hbm, _, *refs):
-    near, far, refs = refs[:2], refs[2:2 + n_row], refs[2 + n_row:]
+    near, far, refs = refs[:2], refs[2:2 + n_row * (n_col // 2 - 1)], refs[2 + n_row * (n_col // 2 - 1):]
     outs, (targets_ref, support_ref, sems) = refs[:n_col], refs[n_col:]
-    (rows, features), (_, width) = own_hbm.shape, far[0].shape
-    half = features // 2
+    rows, features = own_hbm.shape
     row = lax.axis_index("row")
-    odd = row % 2
+    chip, core = row // 2, row % 2
+    half, width = features // 2, 2 * features // n_row
     steps = []
-    for core in range(2):
-        cols = pl.ds(pl.multiple_of((odd ^ core) * half, half), half)
+    for part in range(2):
+        side = core ^ part
+        cols = pl.ds(pl.multiple_of(side * half, half), half)
         loads = [
             (own_hbm.at[:, cols], targets_ref.at[pl.ds(0, rows), cols]),
             (support_hbm.at[:, cols], support_ref.at[:, cols]),
-            (near[core], targets_ref.at[pl.ds(rows, rows), cols]),
+            (near[part], targets_ref.at[pl.ds(rows, rows), cols]),
         ]
-        for step in range(core, n_row, 2):
-            inner = pl.ds(pl.multiple_of(slice_of(row ^ step, n_row) * width, width), width)
-            loads.append((far[step], targets_ref.at[pl.ds(2 * rows, far[step].shape[0]), inner]))
-        steps.append((cols, start_all(loads, sems.at[core])))
+        steps.append((cols, loads))
+    loads = []
+    for pair in range(n_col // 2 - 1):
+        for step in range(n_row):
+            plane = 2 * pair + 2 + (core ^ (step % 2))
+            cols = pl.ds(pl.multiple_of((chip ^ (step // 2)) * width, width), width)
+            spot = targets_ref.at[pl.ds(pl.multiple_of(plane * rows, rows), rows), cols]
+            loads.append((far[pair * n_row + step], spot))
+    steps[0][1].extend(loads)
+    steps = [(cols, start_all(loads, sems.at[i])) for i, (cols, loads) in enumerate(steps)]
     total = 0.0
     for cols, copies in steps:
         wait_all(copies)
@@ -125,12 +136,28 @@
     pivot = diag_inverses.shape[1]
     scale = 0.5 / math.sqrt(features)
     row, col = lax.axis_index("row"), lax.axis_index("col")
-    width = features // n_row
-
-    half = lax.dynamic_slice(targets, (0, (row % 2) * (features // 2)), (rows, features // 2))
-    mine = lax.dynamic_slice(targets, (0, slice_of(row, n_row) * width), (rows, width))
+    width = 2 * features // n_row
+
+    mine, half = pl.pallas_call(
+        functools.partial(cut_kernel, n_row),
+        out_shape=[
+            jax.ShapeDtypeStruct((rows, width), targets.dtype),
+            jax.ShapeDtypeStruct((rows, features // 2), targets.dtype),
+        ],
+        in_specs=[HBM],
+        out_specs=[VMEM] * 2,
+        scratch_shapes=[pltpu.SemaphoreType.DMA((2,))],
+        compiler_params=SOLVE_PARAMS,
+        cost_estimate=SHORT,
+        name="cut_kernel",
+    )(targets)
     near = exchange(half, "col", n_col, 1)
-    far = jnp.concatenate([exchange(mine, "col", n_col, j) for j in range(2, n_col)], axis=0)
+    far = [
+        lax.ppermute(mine, ("row", "col"), [
+            (r * n_col + c, r * n_col + (c ^ (j + r % 2))) for r in range(n_row) for c in range(n_col)
+        ])
+        for j in range(2, n_col, 2)
+    ]
     small = jnp.concatenate([panels * PANEL_UNIT] * n_col, axis=0).astype(jnp.float16)
     small = small.reshape(n_col, *panels.shape)
     blocks = lax.all_to_all(small, "col", 0, 0)
@@ -146,23 +173,25 @@
     )(diag_inverses)
     far, mark = together(far, mark)
     near = [near, exchange(near, "row", n_row, 1)]
-    far = [far] + [exchange(far, "row", n_row, i) for i in range(2, n_row, 2)]
-    far = [p for own in far for p in (own, exchange(own, "row", n_row, 1))]
+    pieces = []
+    for own in far:
+        for piece in [own] + [exchange(own, "row", n_row, i) for i in range(2, n_row, 2)]:
+            pieces += [piece, exchange(piece, "row", n_row, 1)]
 
     made = pl.pallas_call(
         functools.partial(tile_kernel, scale, n_row, n_col),
         out_shape=[jax.ShapeDtypeStruct((rows, span), jnp.float32)] * n_col,
-        in_specs=[HBM] * (n_row + 5),
+        in_specs=[HBM] * (len(pieces) + 5),
         out_specs=[VMEM] * n_col,
         scratch_shapes=[
             pltpu.VMEM((n_col * rows, features), jnp.bfloat16),
             pltpu.VMEM((span, features), jnp.bfloat16),
-            pltpu.SemaphoreType.DMA((2, n_row + 4)),
+            pltpu.SemaphoreType.DMA((2, len(pieces) + 3)),
         ],
         compiler_params=TILE_PARAMS,
         cost_estimate=SHORT,
         name="tile_kernel",
-    )(targets, support, mark, *near, *far)
+    )(targets, support, mark, *near, *pieces)
 
     tiles = [made[0]] + [exchange(made[j], "col", n_col, j) for j in range(1, n_col)]
     tiles, blocks = together(tiles, blocks)

time: 46.6 us -> 45.1 us (0.968)
  local copies, waits for them, and re-layouts: 1.86 us -> 1.06 us
  starting transfers between devices: 22.5 us -> 21.8 us
    ppermute x0 -> x1, starting transfers between devices: none -> 4.1 us  [shards(): lax.ppermute(mine, ('row', 'col'), [(r * n_col + c, r * n_col + (c ^ j +...]
    ppermute x19 -> x17, starting transfers between devices: 18.3 us -> 14.3 us  [exchange(): return lax.ppermute(value, axis, [(i, i ^ mask) for i in range(size)])]
    dynamic_slice x2 -> x0, local copies, waits for them, and re-layouts: 1.85 us -> none  [the longest x1 0.97 us: shards(): lax.dynamic_slice(targets, (0, row % 2 * (features // 2)), (rows, feature...]
    unnamed x8 -> x10, local copies, waits for them, and re-layouts: 0.02 us -> 1.06 us
    all_to_all x1, starting transfers between devices: 4.19 us -> 3.47 us  [shards(): blocks = lax.all_to_all(small, 'col', 0, 0)]
    ppermute x19 -> x17, waiting for transfers between devices: 16.7 us -> 16.5 us  [exchange(): return lax.ppermute(value, axis, [(i, i ^ mask) for i in range(size)])]
  transfers between devices with their start and end apart: 20 -> 19, of which waited for: 12 -> 11; matrix products, arithmetic and copies ran while one was open for 6% -> 4% of each run, Pallas kernels for 3% -> 4%
where the time goes in v4:
time: 45.1 us; the launch traced here: 44.8 us
  starting transfers between devices  21.8 us (48%)
  waiting for transfers between devices  16.5 us (37%)
  Pallas kernels  3.28 us (7%)
  other arithmetic  2.02 us (4%)
  local copies, waits for them, and re-layouts  1.06 us (2%)
    ppermute x17, waiting for transfers between devices, exchange(): return lax.ppermute(value, axis, [(i, i ^ mask) for i in range(size)])  16.5 us
    ppermute x17, starting transfers between devices, exchange(): return lax.ppermute(value, axis, [(i, i ^ mask) for i in range(size)])  14.3 us
    ppermute x1, starting transfers between devices, shards(): lax.ppermute(mine, ('row', 'col'), [(r * n_col + c, r * n_col + (c ^ j +...  4.1 us
    all_to_all x1, starting transfers between devices, shards(): blocks = lax.all_to_all(small, 'col', 0, 0)  3.47 us
    pallas_call x1, Pallas kernels, shards(): pl.pallas_call(functools.partial(tile_kernel, scale, n_row, n_col), out_s...  1.61 us
    pallas_call x1, Pallas kernels, shards(): pl.pallas_call(functools.partial(solve_kernel, n_col, pivot), out_shape=j...  1.08 us
    unnamed x10, local copies, waits for them, and re-layouts  1.06 us
    another operation x1, other arithmetic  0.97 us
  transfers between devices with their start and end apart: 19, of which 11 were waited for; matrix products, arithmetic and copies ran while one was open for 4% of the time, Pallas kernels for 4%

profile of v4, /device:TPU:0, one launch (start us, length us, event | category | flops | bytes accessed | tf_op | source)
XLA Modules:
  0.0 44.8 jit_solution(12306575488922941957)
XLA Ops:
  0.0 1.0 %copy-done.1 = bf16[64,4096]{1,0:T(8,128)(2,1)S(1)} copy-done((bf16[64,4096]{1,0:T(8,128)(2,1)S(1)}, bf16[64,4096]{1,0:T(8,128)(2,1)}, u32[]{:S(2)}) %copy-start.1) | copy-done | bytes 524312
  1.1 4.1 %collective-permute-start = (bf16[64,1024]{1,0:T(8,128)(2,1)S(1)}, bf16[64,1024]{1,0:T(8,128)(2,1)S(1)}, u32[]{:S(2)}, u32[]{:S(2)}) collective-permute-start(bf16[64,1024]{1,0:T(8,128)(2,1)S(1)} %get-tuple-element.18), channel_id=1, source_target_pairs={{0,2},{1,3},{2,0},{3,1},{4,7},{5,6},{6,5},{7,4},{8,10},{9,11},{10,... | collective-permute-start | bytes 393224 | tf_op jit(solution)/shard_map/ppermute | solution.py:156
  5.2 1.6 %collective-permute-start.1 = (bf16[64,2048]{1,0:T(8,128)(2,1)S(1)}, bf16[64,2048]{1,0:T(8,128)(2,1)S(1)}, u32[]{:S(2)}, u32[]{:S(2)}) collective-permute-start(bf16[64,2048]{1,0:T(8,128)(2,1)S(1)} %get-tuple-element.20), channel_id=1, source_target_pairs={{0,1},{1,0},{2,3},{3,2},{4,5},{5,4},{6,7},{7,6},{8,9},{9,8},{10,11... | collective-permute-start | bytes 786440 | tf_op jit(solution)/shard_map/ppermute | solution.py:126
  6.8 1.0 %multiply_convert_fusion = f16[2,128,256]{2,1,0:T(8,128)(2,1)S(1)} fusion(f32[2,128,256]{2,1,0:T(8,128)} %refs_4_.1), kind=kLoop, calls=%fused_computation.2 | loop fusion | flops 131072 | bytes 393216 | tf_op jit(solution)/shard_map/convert
  7.8 0.9 %pad_maximum_fusion = f16[8,128,256]{2,1,0:T(8,128)(2,1)} fusion(f16[2,128,256]{2,1,0:T(8,128)(2,1)S(1)} %multiply_convert_fusion), kind=kLoop, calls=%fused_computation.1 | loop fusion | flops 786432 | bytes 655360 | tf_op jit(solution)/shard_map/concatenate | solution.py:161
  8.7 3.5 %all-to-all-start = ((f16[4,2,128,256]{3,2,1,0:T(8,128)(2,1)}), f16[4,2,128,256]{3,2,1,0:T(8,128)(2,1)S(1)}, u32[]{:S(2)}, u32[]{:S(2)}) async-start(f16[4,2,128,256]{3,2,1,0:T(8,128)(2,1)} %bitcast), calls=%async_computation | async-start | bytes 1048576 | tf_op jit(solution)/shard_map/all_to_all | solution.py:163
  12.2 1.6 %collective-permute-start.4 = (bf16[64,1024]{1,0:T(8,128)(2,1)S(1)}, bf16[64,1024]{1,0:T(8,128)(2,1)S(1)}, u32[]{:S(2)}, u32[]{:S(2)}) collective-permute-start(bf16[64,1024]{1,0:T(8,128)(2,1)S(1)} %collective-permute-done.refs_2_), channel_id=1, source_target_pairs={{0,8},{4,12},{8,0},{12,4},{16,24},{20,28},{24,16},{28,20},{1,9},{5... | collective-permute-start | bytes 393224 | tf_op jit(solution)/shard_map/ppermute | solution.py:126
  13.8 1.5 %collective-permute-start.6 = (bf16[64,1024]{1,0:T(8,128)(2,1)S(1)}, bf16[64,1024]{1,0:T(8,128)(2,1)S(1)}, u32[]{:S(2)}, u32[]{:S(2)}) collective-permute-start(bf16[64,1024]{1,0:T(8,128)(2,1)S(1)} %collective-permute-done.refs_2_), channel_id=1, source_target_pairs={{0,16},{4,20},{8,24},{12,28},{16,0},{20,4},{24,8},{28,12},{1,17},{... | collective-permute-start | bytes 393224 | tf_op jit(solution)/shard_map/ppermute | solution.py:126
  15.3 0.5 %collective-permute-start.8 = (bf16[64,1024]{1,0:T(8,128)(2,1)S(1)}, bf16[64,1024]{1,0:T(8,128)(2,1)S(1)}, u32[]{:S(2)}, u32[]{:S(2)}) collective-permute-start(bf16[64,1024]{1,0:T(8,128)(2,1)S(1)} %collective-permute-done.refs_2_), channel_id=1, source_target_pairs={{0,24},{4,28},{8,16},{12,20},{16,8},{20,12},{24,0},{28,4},{1,25},{... | collective-permute-start | bytes 393224 | tf_op jit(solution)/shard_map/ppermute | solution.py:126
  15.8 0.5 %collective-permute-start.3 = (bf16[64,1024]{1,0:T(8,128)(2,1)S(1)}, bf16[64,1024]{1,0:T(8,128)(2,1)S(1)}, u32[]{:S(2)}, u32[]{:S(2)}) collective-permute-start(bf16[64,1024]{1,0:T(8,128)(2,1)S(1)} %collective-permute-done.refs_2_), channel_id=1, source_target_pairs={{0,4},{4,0},{8,12},{12,8},{16,20},{20,16},{24,28},{28,24},{1,5},{5... | collective-permute-start | bytes 393224 | tf_op jit(solution)/shard_map/ppermute | solution.py:126
  16.3 2.0 %collective-permute-done.4.refs_4_ = bf16[64,1024]{1,0:T(8,128)(2,1)S(1)} collective-permute-done((bf16[64,1024]{1,0:T(8,128)(2,1)S(1)}, bf16[64,1024]{1,0:T(8,128)(2,1)S(1)}, u32[]{:S(2)}, u32[]{:S(2)}) %collective-permute-start.4) | collective-permute-done | bytes 131104 | tf_op jit(solution)/shard_map/ppermute | solution.py:126
  18.3 3.1 %collective-permute-done.6.refs_6_ = bf16[64,1024]{1,0:T(8,128)(2,1)S(1)} collective-permute-done((bf16[64,1024]{1,0:T(8,128)(2,1)S(1)}, bf16[64,1024]{1,0:T(8,128)(2,1)S(1)}, u32[]{:S(2)}, u32[]{:S(2)}) %collective-permute-start.6) | collective-permute-done | bytes 131104 | tf_op jit(solution)/shard_map/ppermute | solution.py:126
  21.5 0.5 %collective-permute-start.9 = (bf16[64,1024]{1,0:T(8,128)(2,1)S(1)}, bf16[64,1024]{1,0:T(8,128)(2,1)S(1)}, u32[]{:S(2)}, u32[]{:S(2)}) collective-permute-start(bf16[64,1024]{1,0:T(8,128)(2,1)S(1)} %collective-permute-done.8.refs_8_), channel_id=1, source_target_pairs={{0,4},{4,0},{8,12},{12,8},{16,20},{20,16},{24,28},{28,24},{1,5},{5... | collective-permute-start | bytes 393224 | tf_op jit(solution)/shard_map/ppermute | solution.py:126
  22.0 0.8 %collective-permute-done.7.refs_7_ = bf16[64,1024]{1,0:T(8,128)(2,1)S(1)} collective-permute-done((bf16[64,1024]{1,0:T(8,128)(2,1)S(1)}, bf16[64,1024]{1,0:T(8,128)(2,1)S(1)}, u32[]{:S(2)}, u32[]{:S(2)}) %collective-permute-start.7) | collective-permute-done | bytes 131104 | tf_op jit(solution)/shard_map/ppermute | solution.py:126
  22.8 0.2 collective-permute-done.9.refs_9_
  23.0 1.6 %tile_kernel.1 = (f32[64,256]{1,0:T(8,128)S(1)}, f32[64,256]{1,0:T(8,128)S(1)}, f32[64,256]{1,0:T(8,128)S(1)}, f32[64,256]{1,0:T(8,128)S(1)}) custom-call(bf16[64,4096]{1,0:T(8,128)(2,1)S(1)} %copy-done.2, bf16[256,4096]{1,0:T(8,128)(2,1)S(1)} %copy-done, f32[8,128]{1,0:T(8,128)S(1)} %mark_kernel.1._, bf16[64,2048]{1,0:T(8,128)(2,1)S(1)} %collective-permute-done.1.refs_0_, ...), custom_call_target="tpu_custom_call" | custom-call | flops 1000000 | tf_op jit(solution)/shard_map/tile_kernel/pallas_call | solution.py:181
  24.6 1.9 %collective-permute-start.10 = (f32[64,256]{1,0:T(8,128)S(1)}, f32[64,256]{1,0:T(8,128)S(1)}, u32[]{:S(2)}, u32[]{:S(2)}) collective-permute-start(f32[64,256]{1,0:T(8,128)S(1)} %get-tuple-element.23), channel_id=1, source_target_pairs={{0,1},{1,0},{2,3},{3,2},{4,5},{5,4},{6,7},{7,6},{8,9},{9,8},{10,11... | collective-permute-start | bytes 196616 | tf_op jit(solution)/shard_map/ppermute | solution.py:126
  26.6 2.3 %collective-permute-start.11 = (f32[64,256]{1,0:T(8,128)S(1)}, f32[64,256]{1,0:T(8,128)S(1)}, u32[]{:S(2)}, u32[]{:S(2)}) collective-permute-start(f32[64,256]{1,0:T(8,128)S(1)} %get-tuple-element.24), channel_id=1, source_target_pairs={{0,2},{1,3},{2,0},{3,1},{4,6},{5,7},{6,4},{7,5},{8,10},{9,11},{10,... | collective-permute-start | bytes 196616 | tf_op jit(solution)/shard_map/ppermute | solution.py:126
  28.9 0.2 collective-permute-start.12
  29.1 0.1 collective-permute-done.10.refs_1_
  29.2 5.1 %collective-permute-done.11.refs_2_ = f32[64,256]{1,0:T(8,128)S(1)} collective-permute-done((f32[64,256]{1,0:T(8,128)S(1)}, f32[64,256]{1,0:T(8,128)S(1)}, u32[]{:S(2)}, u32[]{:S(2)}) %collective-permute-start.11) | collective-permute-done | bytes 65568 | tf_op jit(solution)/shard_map/ppermute | solution.py:126
  34.2 0.9 %collective-permute-done.12.refs_3_ = f32[64,256]{1,0:T(8,128)S(1)} collective-permute-done((f32[64,256]{1,0:T(8,128)S(1)}, f32[64,256]{1,0:T(8,128)S(1)}, u32[]{:S(2)}, u32[]{:S(2)}) %collective-permute-start.12) | collective-permute-done | bytes 65568 | tf_op jit(solution)/shard_map/ppermute | solution.py:126
  35.2 1.2 %collective-permute-done.13.other_ref = f32[64,128]{1,0:T(8,128)S(1)} collective-permute-done((f32[64,128]{1,0:T(8,128)S(1)}, f32[64,128]{1,0:T(8,128)S(1)}, u32[]{:S(2)}, u32[]{:S(2)}) %collective-permute-start.13) | collective-permute-done | bytes 32800 | tf_op jit(solution)/shard_map/ppermute | solution.py:126
  36.4 0.5 %head_kernel.1 = f32[64,128]{1,0:T(8,128)S(1)} custom-call(f32[64,128]{1,0:T(8,128)S(1)} %select_select_fusion.1.mine_ref, f32[64,128]{1,0:T(8,128)S(1)} %collective-permute-done.13.other_ref, f32[128,128]{1,0:T(8,128)S(1)} %multiply_bitcast_fusion.corner_ref, f32[2,128,128]{2,1,0:T(8,128)S(1)} %copy-done.4), custom_call_target="tpu_custom_call" | custom-call | flops 1000000 | tf_op jit(solution)/shard_map/head_kernel/pallas_call | solution.py:202
  36.9 0.6 %collective-permute-start.14 = (f32[64,128]{1,0:T(8,128)S(1)}, f32[64,128]{1,0:T(8,128)S(1)}, u32[]{:S(2)}, u32[]{:S(2)}) collective-permute-start(f32[64,128]{1,0:T(8,128)S(1)} %head_kernel.1), channel_id=1, source_target_pairs={{0,24},{4,28},{8,16},{12,20},{16,8},{20,12},{24,0},{28,4},{1,25},{... | collective-permute-start | bytes 98312 | tf_op jit(solution)/shard_map/ppermute | solution.py:126
  37.5 1.0 %collective-permute-start.15 = (f32[64,128]{1,0:T(8,128)S(1)}, f32[64,128]{1,0:T(8,128)S(1)}, u32[]{:S(2)}, u32[]{:S(2)}) collective-permute-start(f32[64,128]{1,0:T(8,128)S(1)} %head_kernel.1), channel_id=1, source_target_pairs={{0,16},{4,20},{8,24},{12,28},{16,0},{20,4},{24,8},{28,12},{1,17},{... | collective-permute-start | bytes 98312 | tf_op jit(solution)/shard_map/ppermute | solution.py:126
  38.6 1.9 %collective-permute-start.16 = (f32[64,128]{1,0:T(8,128)S(1)}, f32[64,128]{1,0:T(8,128)S(1)}, u32[]{:S(2)}, u32[]{:S(2)}) collective-permute-start(f32[64,128]{1,0:T(8,128)S(1)} %head_kernel.1), channel_id=1, source_target_pairs={{0,8},{4,12},{8,0},{12,4},{16,24},{20,28},{24,16},{28,20},{1,9},{5... | collective-permute-start | bytes 98312 | tf_op jit(solution)/shard_map/ppermute | solution.py:126
  40.4 1.6 %collective-permute-done.14 = f32[64,128]{1,0:T(8,128)S(1)} collective-permute-done((f32[64,128]{1,0:T(8,128)S(1)}, f32[64,128]{1,0:T(8,128)S(1)}, u32[]{:S(2)}, u32[]{:S(2)}) %collective-permute-start.14) | collective-permute-done | bytes 32800 | tf_op jit(solution)/shard_map/ppermute | solution.py:126
  42.0 0.4 collective-permute-done.16
  42.6 0.1 convert_multiply_fusion.refs_5_
  42.7 1.1 %collective-permute-done.17.refs_7_ = f32[64,128]{1,0:T(8,128)S(1)} collective-permute-done((f32[64,128]{1,0:T(8,128)S(1)}, f32[64,128]{1,0:T(8,128)S(1)}, u32[]{:S(2)}, u32[]{:S(2)}) %collective-permute-start.17) | collective-permute-done | bytes 32800 | tf_op jit(solution)/shard_map/ppermute | solution.py:126
  43.8 1.1 %solve_kernel.1 = f32[64,1024]{1,0:T(8,128)} custom-call(f32[64,256]{1,0:T(8,128)S(1)} %get-tuple-element.26.refs_0_, f32[64,256]{1,0:T(8,128)S(1)} %collective-permute-done.10.refs_1_, f32[64,256]{1,0:T(8,128)S(1)} %collective-permute-done.11.refs_2_, f32[64,256]{1,0:T(8,128)S(1)} %collective-permute-done.12.refs_3_, f32[2,128,256]{2,1,0:T(8,128)S(1)} %copy-done.3, ...), custom_call_target="tpu_custom_call" | custom-call | tf_op jit(solution)/shard_map/solve_kernel/pallas_call | solution.py:217
  (27 shorter events, 0.3 us)
Async XLA Ops:
  0.0 1.0 %copy-start.1 = (bf16[64,4096]{1,0:T(8,128)(2,1)S(1)}, bf16[64,4096]{1,0:T(8,128)(2,1)}, u32[]{:S(2)}) copy-start(bf16[64,4096]{1,0:T(8,128)(2,1)} %own_hbm.1) | copy-start | bytes 1572868
  1.0 11.1 %copy-start.4 = (f32[2,128,128]{2,1,0:T(8,128)S(1)}, f32[2,128,128]{2,1,0:T(8,128)}, u32[]{:S(2)}) copy-start(f32[2,128,128]{2,1,0:T(8,128)} %inverse_ref.1) | copy-start | bytes 393220
  1.1 11.1 %collective-permute-start = (bf16[64,1024]{1,0:T(8,128)(2,1)S(1)}, bf16[64,1024]{1,0:T(8,128)(2,1)S(1)}, u32[]{:S(2)}, u32[]{:S(2)}) collective-permute-start(bf16[64,1024]{1,0:T(8,128)(2,1)S(1)} %get-tuple-element.18), channel_id=1, source_target_pairs={{0,2},{1,3},{2,0},{3,1},{4,7},{5,6},{6,5},{7,4},{8,10},{9,11},{10,... | collective-permute-start | bytes 393224 | tf_op jit(solution)/shard_map/ppermute | solution.py:156
  5.2 10.6 %collective-permute-start.1 = (bf16[64,2048]{1,0:T(8,128)(2,1)S(1)}, bf16[64,2048]{1,0:T(8,128)(2,1)S(1)}, u32[]{:S(2)}, u32[]{:S(2)}) collective-permute-start(bf16[64,2048]{1,0:T(8,128)(2,1)S(1)} %get-tuple-element.20), channel_id=1, source_target_pairs={{0,1},{1,0},{2,3},{3,2},{4,5},{5,4},{6,7},{7,6},{8,9},{9,8},{10,11... | collective-permute-start | bytes 786440 | tf_op jit(solution)/shard_map/ppermute | solution.py:126
  8.7 26.4 %all-to-all-start = ((f16[4,2,128,256]{3,2,1,0:T(8,128)(2,1)}), f16[4,2,128,256]{3,2,1,0:T(8,128)(2,1)S(1)}, u32[]{:S(2)}, u32[]{:S(2)}) async-start(f16[4,2,128,256]{3,2,1,0:T(8,128)(2,1)} %bitcast), calls=%async_computation | async-start | bytes 1048576 | tf_op jit(solution)/shard_map/all_to_all | solution.py:163
  12.2 10.8 %copy-start = (bf16[256,4096]{1,0:T(8,128)(2,1)S(1)}, bf16[256,4096]{1,0:T(8,128)(2,1)}, u32[]{:S(2)}) copy-start(bf16[256,4096]{1,0:T(8,128)(2,1)} %support_hbm.1) | copy-start | bytes 6291460
  12.2 10.8 %copy-start.2 = (bf16[64,4096]{1,0:T(8,128)(2,1)S(1)}, bf16[64,4096]{1,0:T(8,128)(2,1)}, u32[]{:S(2)}) copy-start(bf16[64,4096]{1,0:T(8,128)(2,1)} %own_hbm.1) | copy-start | bytes 1572868
  12.2 6.1 %collective-permute-start.4 = (bf16[64,1024]{1,0:T(8,128)(2,1)S(1)}, bf16[64,1024]{1,0:T(8,128)(2,1)S(1)}, u32[]{:S(2)}, u32[]{:S(2)}) collective-permute-start(bf16[64,1024]{1,0:T(8,128)(2,1)S(1)} %collective-permute-done.refs_2_), channel_id=1, source_target_pairs={{0,8},{4,12},{8,0},{12,4},{16,24},{20,28},{24,16},{28,20},{1,9},{5... | collective-permute-start | bytes 393224 | tf_op jit(solution)/shard_map/ppermute | solution.py:126
  13.8 7.7 %collective-permute-start.6 = (bf16[64,1024]{1,0:T(8,128)(2,1)S(1)}, bf16[64,1024]{1,0:T(8,128)(2,1)S(1)}, u32[]{:S(2)}, u32[]{:S(2)}) collective-permute-start(bf16[64,1024]{1,0:T(8,128)(2,1)S(1)} %collective-permute-done.refs_2_), channel_id=1, source_target_pairs={{0,16},{4,20},{8,24},{12,28},{16,0},{20,4},{24,8},{28,12},{1,17},{... | collective-permute-start | bytes 393224 | tf_op jit(solution)/shard_map/ppermute | solution.py:126
  15.3 6.2 %collective-permute-start.8 = (bf16[64,1024]{1,0:T(8,128)(2,1)S(1)}, bf16[64,1024]{1,0:T(8,128)(2,1)S(1)}, u32[]{:S(2)}, u32[]{:S(2)}) collective-permute-start(bf16[64,1024]{1,0:T(8,128)(2,1)S(1)} %collective-permute-done.refs_2_), channel_id=1, source_target_pairs={{0,24},{4,28},{8,16},{12,20},{16,8},{20,12},{24,0},{28,4},{1,25},{... | collective-permute-start | bytes 393224 | tf_op jit(solution)/shard_map/ppermute | solution.py:126
  15.8 7.2 %collective-permute-start.2 = (bf16[64,2048]{1,0:T(8,128)(2,1)S(1)}, bf16[64,2048]{1,0:T(8,128)(2,1)S(1)}, u32[]{:S(2)}, u32[]{:S(2)}) collective-permute-start(bf16[64,2048]{1,0:T(8,128)(2,1)S(1)} %collective-permute-done.1.refs_0_), channel_id=1, source_target_pairs={{0,4},{4,0},{8,12},{12,8},{16,20},{20,16},{24,28},{28,24},{1,5},{5... | collective-permute-start | bytes 786440 | tf_op jit(solution)/shard_map/ppermute | solution.py:126
  15.8 6.2 %collective-permute-start.3 = (bf16[64,1024]{1,0:T(8,128)(2,1)S(1)}, bf16[64,1024]{1,0:T(8,128)(2,1)S(1)}, u32[]{:S(2)}, u32[]{:S(2)}) collective-permute-start(bf16[64,1024]{1,0:T(8,128)(2,1)S(1)} %collective-permute-done.refs_2_), channel_id=1, source_target_pairs={{0,4},{4,0},{8,12},{12,8},{16,20},{20,16},{24,28},{28,24},{1,5},{5... | collective-permute-start | bytes 393224 | tf_op jit(solution)/shard_map/ppermute | solution.py:126
  18.3 3.7 %collective-permute-start.5 = (bf16[64,1024]{1,0:T(8,128)(2,1)S(1)}, bf16[64,1024]{1,0:T(8,128)(2,1)S(1)}, u32[]{:S(2)}, u32[]{:S(2)}) collective-permute-start(bf16[64,1024]{1,0:T(8,128)(2,1)S(1)} %collective-permute-done.4.refs_4_), channel_id=1, source_target_pairs={{0,4},{4,0},{8,12},{12,8},{16,20},{20,16},{24,28},{28,24},{1,5},{5... | collective-permute-start | bytes 393224 | tf_op jit(solution)/shard_map/ppermute | solution.py:126
  21.4 1.3 %collective-permute-start.7 = (bf16[64,1024]{1,0:T(8,128)(2,1)S(1)}, bf16[64,1024]{1,0:T(8,128)(2,1)S(1)}, u32[]{:S(2)}, u32[]{:S(2)}) collective-permute-start(bf16[64,1024]{1,0:T(8,128)(2,1)S(1)} %collective-permute-done.6.refs_6_), channel_id=1, source_target_pairs={{0,4},{4,0},{8,12},{12,8},{16,20},{20,16},{24,28},{28,24},{1,5},{5... | collective-permute-start | bytes 393224 | tf_op jit(solution)/shard_map/ppermute | solution.py:126
  21.5 1.5 %collective-permute-start.9 = (bf16[64,1024]{1,0:T(8,128)(2,1)S(1)}, bf16[64,1024]{1,0:T(8,128)(2,1)S(1)}, u32[]{:S(2)}, u32[]{:S(2)}) collective-permute-start(bf16[64,1024]{1,0:T(8,128)(2,1)S(1)} %collective-permute-done.8.refs_8_), channel_id=1, source_target_pairs={{0,4},{4,0},{8,12},{12,8},{16,20},{20,16},{24,28},{28,24},{1,5},{5... | collective-permute-start | bytes 393224 | tf_op jit(solution)/shard_map/ppermute | solution.py:126
  24.6 19.1 %copy-start.3 = (f32[2,128,256]{2,1,0:T(8,128)S(1)}, f32[2,128,256]{2,1,0:T(8,128)}, u32[]{:S(2)}) copy-start(f32[2,128,256]{2,1,0:T(8,128)} %refs_4_.1) | copy-start | bytes 786436
  24.6 4.5 %collective-permute-start.10 = (f32[64,256]{1,0:T(8,128)S(1)}, f32[64,256]{1,0:T(8,128)S(1)}, u32[]{:S(2)}, u32[]{:S(2)}) collective-permute-start(f32[64,256]{1,0:T(8,128)S(1)} %get-tuple-element.23), channel_id=1, source_target_pairs={{0,1},{1,0},{2,3},{3,2},{4,5},{5,4},{6,7},{7,6},{8,9},{9,8},{10,11... | collective-permute-start | bytes 196616 | tf_op jit(solution)/shard_map/ppermute | solution.py:126
  26.6 7.6 %collective-permute-start.11 = (f32[64,256]{1,0:T(8,128)S(1)}, f32[64,256]{1,0:T(8,128)S(1)}, u32[]{:S(2)}, u32[]{:S(2)}) collective-permute-start(f32[64,256]{1,0:T(8,128)S(1)} %get-tuple-element.24), channel_id=1, source_target_pairs={{0,2},{1,3},{2,0},{3,1},{4,6},{5,7},{6,4},{7,5},{8,10},{9,11},{10,... | collective-permute-start | bytes 196616 | tf_op jit(solution)/shard_map/ppermute | solution.py:126
  28.9 6.2 %collective-permute-start.12 = (f32[64,256]{1,0:T(8,128)S(1)}, f32[64,256]{1,0:T(8,128)S(1)}, u32[]{:S(2)}, u32[]{:S(2)}) collective-permute-start(f32[64,256]{1,0:T(8,128)S(1)} %get-tuple-element.25), channel_id=1, source_target_pairs={{0,3},{1,2},{2,1},{3,0},{4,7},{5,6},{6,5},{7,4},{8,11},{9,10},{10,... | collective-permute-start | bytes 196616 | tf_op jit(solution)/shard_map/ppermute | solution.py:126
  35.1 1.3 %collective-permute-start.13 = (f32[64,128]{1,0:T(8,128)S(1)}, f32[64,128]{1,0:T(8,128)S(1)}, u32[]{:S(2)}, u32[]{:S(2)}) collective-permute-start(f32[64,128]{1,0:T(8,128)S(1)} %select_select_fusion.1.mine_ref), channel_id=1, source_target_pairs={{0,4},{4,0},{8,12},{12,8},{16,20},{20,16},{24,28},{28,24},{1,5},{5... | collective-permute-start | bytes 98312 | tf_op jit(solution)/shard_map/ppermute | solution.py:126
  36.9 5.1 %collective-permute-start.14 = (f32[64,128]{1,0:T(8,128)S(1)}, f32[64,128]{1,0:T(8,128)S(1)}, u32[]{:S(2)}, u32[]{:S(2)}) collective-permute-start(f32[64,128]{1,0:T(8,128)S(1)} %head_kernel.1), channel_id=1, source_target_pairs={{0,24},{4,28},{8,16},{12,20},{16,8},{20,12},{24,0},{28,4},{1,25},{... | collective-permute-start | bytes 98312 | tf_op jit(solution)/shard_map/ppermute | solution.py:126
  37.5 4.5 %collective-permute-start.15 = (f32[64,128]{1,0:T(8,128)S(1)}, f32[64,128]{1,0:T(8,128)S(1)}, u32[]{:S(2)}, u32[]{:S(2)}) collective-permute-start(f32[64,128]{1,0:T(8,128)S(1)} %head_kernel.1), channel_id=1, source_target_pairs={{0,16},{4,20},{8,24},{12,28},{16,0},{20,4},{24,8},{28,12},{1,17},{... | collective-permute-start | bytes 98312 | tf_op jit(solution)/shard_map/ppermute | solution.py:126
  38.6 3.9 %collective-permute-start.16 = (f32[64,128]{1,0:T(8,128)S(1)}, f32[64,128]{1,0:T(8,128)S(1)}, u32[]{:S(2)}, u32[]{:S(2)}) collective-permute-start(f32[64,128]{1,0:T(8,128)S(1)} %head_kernel.1), channel_id=1, source_target_pairs={{0,8},{4,12},{8,0},{12,4},{16,24},{20,28},{24,16},{28,20},{1,9},{5... | collective-permute-start | bytes 98312 | tf_op jit(solution)/shard_map/ppermute | solution.py:126
  42.5 1.3 %collective-permute-start.17 = (f32[64,128]{1,0:T(8,128)S(1)}, f32[64,128]{1,0:T(8,128)S(1)}, u32[]{:S(2)}, u32[]{:S(2)}) collective-permute-start(f32[64,128]{1,0:T(8,128)S(1)} %select_select_fusion.refs_6_), channel_id=1, source_target_pairs={{0,4},{4,0},{8,12},{12,8},{16,20},{20,16},{24,28},{28,24},{1,5},{5... | collective-permute-start | bytes 98312 | tf_op jit(solution)/shard_map/ppermute | solution.py:126

commit v5 on v4

--- a/solution.py
+++ b/solution.py
@@ -58,9 +58,9 @@
     out_ref[...] = value_ref[0, :8, :128]
 
 
-def tile_kernel(scale, n_row, n_col, own_hbm, support_hbm, _, *refs):
+def tile_kernel(scale, n_row, n_col, own_hbm, support_ref, _, *refs):
     near, far, refs = refs[:2], refs[2:2 + n_row * (n_col // 2 - 1)], refs[2 + n_row * (n_col // 2 - 1):]
-    outs, (targets_ref, support_ref, sems) = refs[:n_col], refs[n_col:]
+    outs, (targets_ref, sems) = refs[:n_col + 1], refs[n_col + 1:]
     rows, features = own_hbm.shape
     row = lax.axis_index("row")
     chip, core = row // 2, row % 2
@@ -71,7 +71,6 @@
         cols = pl.ds(pl.multiple_of(side * half, half), half)
         loads = [
             (own_hbm.at[:, cols], targets_ref.at[pl.ds(0, rows), cols]),
-            (support_hbm.at[:, cols], support_ref.at[:, cols]),
             (near[part], targets_ref.at[pl.ds(rows, rows), cols]),
         ]
         steps.append((cols, loads))
@@ -88,8 +87,9 @@
     for cols, copies in steps:
         wait_all(copies)
         total = total + dot(targets_ref[:, cols], support_ref[:, cols], NT)
-    for plane in range(n_col):
-        outs[plane][...] = jnp.exp(scale * total[plane * rows:(plane + 1) * rows])
+    starts = [0, rows, rows + rows // 2, *range(2 * rows, n_col * rows, rows)]
+    for start, out_ref in zip(starts, outs):
+        out_ref[...] = jnp.exp(scale * total[start:start + out_ref.shape[0]])
 
 
 def head_kernel(mine_ref, other_ref, corner_ref, inverse_ref, out_ref):
@@ -100,7 +100,9 @@
 
 
 def solve_kernel(n_col, pivot, *refs):
-    tiles, (own_ref, panels_ref, mine_ref, other_ref, out_ref) = refs[:n_col], refs[n_col:]
+    tiles, refs = [ref[...] for ref in refs[:n_col + 1]], refs[n_col + 1:]
+    tiles[1:3] = [jnp.concatenate(tiles[1:3], axis=0)]
+    own_ref, panels_ref, mine_ref, other_ref, out_ref = refs
     span = own_ref.shape[2]
     row, col = lax.axis_index("row"), lax.axis_index("col")
     even = row % 2 == 0
@@ -110,7 +112,7 @@
     for step in range(n_col):
         plane = col ^ step
         block = own_ref if step == 0 else panels_ref.at[plane]
-        value = tiles[step][...] - dot32(first, block[0], NN) - dot32(second, block[1], NN)
+        value = tiles[step] - dot32(first, block[0], NN) - dot32(second, block[1], NN)
         out_ref[:, pl.ds(pl.multiple_of(plane * span, span), span)] = value
 
     @pl.when(row == 0)
@@ -180,12 +182,14 @@
 
     made = pl.pallas_call(
         functools.partial(tile_kernel, scale, n_row, n_col),
-        out_shape=[jax.ShapeDtypeStruct((rows, span), jnp.float32)] * n_col,
-        in_specs=[HBM] * (len(pieces) + 5),
-        out_specs=[VMEM] * n_col,
+        out_shape=[
+            jax.ShapeDtypeStruct((count, span), jnp.float32)
+            for count in [rows, rows // 2, rows // 2] + [rows] * (n_col - 2)
+        ],
+        in_specs=[HBM, VMEM] + [HBM] * (len(pieces) + 3),
+        out_specs=[VMEM] * (n_col + 1),
         scratch_shapes=[
             pltpu.VMEM((n_col * rows, features), jnp.bfloat16),
-            pltpu.VMEM((span, features), jnp.bfloat16),
             pltpu.SemaphoreType.DMA((2, len(pieces) + 3)),
         ],
         compiler_params=TILE_PARAMS,
@@ -193,12 +197,14 @@
         name="tile_kernel",
     )(targets, support, mark, *near, *pieces)
 
-    tiles = [made[0]] + [exchange(made[j], "col", n_col, j) for j in range(1, n_col)]
+    tiles = [made[0]] + [exchange(made[i], "col", n_col, max(1, i - 1)) for i in range(1, n_col + 1)]
     tiles, blocks = together(tiles, blocks)
     corner = blocks[0, 0, :, :pivot].astype(jnp.float32) * (1 / PANEL_UNIT)
-    head = tiles[0][:, :pivot]
+    heads = [tile[:, :pivot] for tile in tiles]
+    heads[1:3] = [jnp.concatenate(heads[1:3], axis=0)]
+    head = heads[0]
     for j in range(1, n_col):
-        head = jnp.where(col == j, tiles[j][:, :pivot], head)
+        head = jnp.where(col == j, heads[j], head)
     head = pl.pallas_call(
         head_kernel,
         out_shape=jax.ShapeDtypeStruct((rows, pivot), jnp.float32),
@@ -217,7 +223,7 @@
     return pl.pallas_call(
         functools.partial(solve_kernel, n_col, pivot),
         out_shape=jax.ShapeDtypeStruct((rows, span * n_col), jnp.float32),
-        in_specs=[VMEM] * (n_col + 4),
+        in_specs=[VMEM] * (n_col + 5),
         out_specs=VMEM,
         compiler_params=SOLVE_PARAMS,
         name="solve_kernel",

time: 45.1 us -> 44 us (0.976)
  waiting for transfers between devices: 16.5 us -> 13.7 us
  starting transfers between devices: 21.8 us -> 23.7 us
    ppermute x17 -> x18, waiting for transfers between devices: 16.5 us -> 13.7 us  [exchange(): return lax.ppermute(value, axis, [(i, i ^ mask) for i in range(size)])]
    ppermute x17 -> x18, starting transfers between devices: 14.3 us -> 16.2 us  [exchange(): return lax.ppermute(value, axis, [(i, i ^ mask) for i in range(size)])]
  transfers between devices with their start and end apart: 19 -> 20, of which waited for: 11 -> 10; matrix products, arithmetic and copies ran while one was open for 4% -> 5% of each run, Pallas kernels for 4% -> 3%
where the time goes in v5:
time: 44 us; the launch traced here: 43.8 us
  starting transfers between devices  23.7 us (54%)
  waiting for transfers between devices  13.7 us (31%)
  Pallas kernels  3.05 us (7%)
  other arithmetic  2.03 us (5%)
  local copies, waits for them, and re-layouts  1.07 us (2%)
    ppermute x18, starting transfers between devices, exchange(): return lax.ppermute(value, axis, [(i, i ^ mask) for i in range(size)])  16.2 us
    ppermute x18, waiting for transfers between devices, exchange(): return lax.ppermute(value, axis, [(i, i ^ mask) for i in range(size)])  13.7 us
    ppermute x1, starting transfers between devices, shards(): lax.ppermute(mine, ('row', 'col'), [(r * n_col + c, r * n_col + (c ^ j +...  4.1 us
    all_to_all x1, starting transfers between devices, shards(): blocks = lax.all_to_all(small, 'col', 0, 0)  3.47 us
    pallas_call x1, Pallas kernels, shards(): pl.pallas_call(functools.partial(tile_kernel, scale, n_row, n_col), out_s...  1.38 us
    pallas_call x1, Pallas kernels, shards(): pl.pallas_call(functools.partial(solve_kernel, n_col, pivot), out_shape=j...  1.08 us
    unnamed x10, local copies, waits for them, and re-layouts  1.06 us
    another operation x1, other arithmetic  0.97 us
  transfers between devices with their start and end apart: 20, of which 10 were waited for; matrix products, arithmetic and copies ran while one was open for 5% of the time, Pallas kernels for 3%

profile of v5, /device:TPU:0, one launch (start us, length us, event | category | flops | bytes accessed | tf_op | source)
XLA Modules:
  0.0 43.8 jit_solution(11079038538994575257)
XLA Ops:
  0.0 1.0 %copy-done.1 = bf16[64,4096]{1,0:T(8,128)(2,1)S(1)} copy-done((bf16[64,4096]{1,0:T(8,128)(2,1)S(1)}, bf16[64,4096]{1,0:T(8,128)(2,1)}, u32[]{:S(2)}) %copy-start.1) | copy-done | bytes 524312
  1.1 4.1 %collective-permute-start = (bf16[64,1024]{1,0:T(8,128)(2,1)S(1)}, bf16[64,1024]{1,0:T(8,128)(2,1)S(1)}, u32[]{:S(2)}, u32[]{:S(2)}) collective-permute-start(bf16[64,1024]{1,0:T(8,128)(2,1)S(1)} %get-tuple-element.20), channel_id=1, source_target_pairs={{0,2},{1,3},{2,0},{3,1},{4,7},{5,6},{6,5},{7,4},{8,10},{9,11},{10,... | collective-permute-start | bytes 393224 | tf_op jit(solution)/shard_map/ppermute | solution.py:158
  5.2 1.6 %collective-permute-start.1 = (bf16[64,2048]{1,0:T(8,128)(2,1)S(1)}, bf16[64,2048]{1,0:T(8,128)(2,1)S(1)}, u32[]{:S(2)}, u32[]{:S(2)}) collective-permute-start(bf16[64,2048]{1,0:T(8,128)(2,1)S(1)} %get-tuple-element.22), channel_id=1, source_target_pairs={{0,1},{1,0},{2,3},{3,2},{4,5},{5,4},{6,7},{7,6},{8,9},{9,8},{10,11... | collective-permute-start | bytes 786440 | tf_op jit(solution)/shard_map/ppermute | solution.py:128
  6.8 1.0 %multiply_convert_fusion = f16[2,128,256]{2,1,0:T(8,128)(2,1)S(1)} fusion(f32[2,128,256]{2,1,0:T(8,128)} %refs_5_.1), kind=kLoop, calls=%fused_computation.2 | loop fusion | flops 131072 | bytes 393216 | tf_op jit(solution)/shard_map/convert
  7.8 0.9 %pad_maximum_fusion = f16[8,128,256]{2,1,0:T(8,128)(2,1)} fusion(f16[2,128,256]{2,1,0:T(8,128)(2,1)S(1)} %multiply_convert_fusion), kind=kLoop, calls=%fused_computation.1 | loop fusion | flops 786432 | bytes 655360 | tf_op jit(solution)/shard_map/concatenate | solution.py:163
  8.7 3.5 %all-to-all-start = ((f16[4,2,128,256]{3,2,1,0:T(8,128)(2,1)}), f16[4,2,128,256]{3,2,1,0:T(8,128)(2,1)S(1)}, u32[]{:S(2)}, u32[]{:S(2)}) async-start(f16[4,2,128,256]{3,2,1,0:T(8,128)(2,1)} %bitcast), calls=%async_computation | async-start | bytes 1048576 | tf_op jit(solution)/shard_map/all_to_all | solution.py:165
  12.2 1.6 %collective-permute-start.4 = (bf16[64,1024]{1,0:T(8,128)(2,1)S(1)}, bf16[64,1024]{1,0:T(8,128)(2,1)S(1)}, u32[]{:S(2)}, u32[]{:S(2)}) collective-permute-start(bf16[64,1024]{1,0:T(8,128)(2,1)S(1)} %collective-permute-done.refs_2_), channel_id=1, source_target_pairs={{0,8},{4,12},{8,0},{12,4},{16,24},{20,28},{24,16},{28,20},{1,9},{5... | collective-permute-start | bytes 393224 | tf_op jit(solution)/shard_map/ppermute | solution.py:128
  13.8 1.5 %collective-permute-start.6 = (bf16[64,1024]{1,0:T(8,128)(2,1)S(1)}, bf16[64,1024]{1,0:T(8,128)(2,1)S(1)}, u32[]{:S(2)}, u32[]{:S(2)}) collective-permute-start(bf16[64,1024]{1,0:T(8,128)(2,1)S(1)} %collective-permute-done.refs_2_), channel_id=1, source_target_pairs={{0,16},{4,20},{8,24},{12,28},{16,0},{20,4},{24,8},{28,12},{1,17},{... | collective-permute-start | bytes 393224 | tf_op jit(solution)/shard_map/ppermute | solution.py:128
  15.3 0.5 %collective-permute-start.8 = (bf16[64,1024]{1,0:T(8,128)(2,1)S(1)}, bf16[64,1024]{1,0:T(8,128)(2,1)S(1)}, u32[]{:S(2)}, u32[]{:S(2)}) collective-permute-start(bf16[64,1024]{1,0:T(8,128)(2,1)S(1)} %collective-permute-done.refs_2_), channel_id=1, source_target_pairs={{0,24},{4,28},{8,16},{12,20},{16,8},{20,12},{24,0},{28,4},{1,25},{... | collective-permute-start | bytes 393224 | tf_op jit(solution)/shard_map/ppermute | solution.py:128
  15.8 0.5 %collective-permute-start.3 = (bf16[64,1024]{1,0:T(8,128)(2,1)S(1)}, bf16[64,1024]{1,0:T(8,128)(2,1)S(1)}, u32[]{:S(2)}, u32[]{:S(2)}) collective-permute-start(bf16[64,1024]{1,0:T(8,128)(2,1)S(1)} %collective-permute-done.refs_2_), channel_id=1, source_target_pairs={{0,4},{4,0},{8,12},{12,8},{16,20},{20,16},{24,28},{28,24},{1,5},{5... | collective-permute-start | bytes 393224 | tf_op jit(solution)/shard_map/ppermute | solution.py:128
  16.3 2.0 %collective-permute-done.4.refs_4_ = bf16[64,1024]{1,0:T(8,128)(2,1)S(1)} collective-permute-done((bf16[64,1024]{1,0:T(8,128)(2,1)S(1)}, bf16[64,1024]{1,0:T(8,128)(2,1)S(1)}, u32[]{:S(2)}, u32[]{:S(2)}) %collective-permute-start.4) | collective-permute-done | bytes 131104 | tf_op jit(solution)/shard_map/ppermute | solution.py:128
  18.3 3.1 %collective-permute-done.6.refs_6_ = bf16[64,1024]{1,0:T(8,128)(2,1)S(1)} collective-permute-done((bf16[64,1024]{1,0:T(8,128)(2,1)S(1)}, bf16[64,1024]{1,0:T(8,128)(2,1)S(1)}, u32[]{:S(2)}, u32[]{:S(2)}) %collective-permute-start.6) | collective-permute-done | bytes 131104 | tf_op jit(solution)/shard_map/ppermute | solution.py:128
  21.5 0.5 %collective-permute-start.9 = (bf16[64,1024]{1,0:T(8,128)(2,1)S(1)}, bf16[64,1024]{1,0:T(8,128)(2,1)S(1)}, u32[]{:S(2)}, u32[]{:S(2)}) collective-permute-start(bf16[64,1024]{1,0:T(8,128)(2,1)S(1)} %collective-permute-done.8.refs_8_), channel_id=1, source_target_pairs={{0,4},{4,0},{8,12},{12,8},{16,20},{20,16},{24,28},{28,24},{1,5},{5... | collective-permute-start | bytes 393224 | tf_op jit(solution)/shard_map/ppermute | solution.py:128
  22.0 0.8 %collective-permute-done.7.refs_7_ = bf16[64,1024]{1,0:T(8,128)(2,1)S(1)} collective-permute-done((bf16[64,1024]{1,0:T(8,128)(2,1)S(1)}, bf16[64,1024]{1,0:T(8,128)(2,1)S(1)}, u32[]{:S(2)}, u32[]{:S(2)}) %collective-permute-start.7) | collective-permute-done | bytes 131104 | tf_op jit(solution)/shard_map/ppermute | solution.py:128
  22.8 0.2 collective-permute-done.9.refs_9_
  23.0 1.4 %tile_kernel.1 = (f32[64,256]{1,0:T(8,128)S(1)}, f32[32,256]{1,0:T(8,128)S(1)}, f32[32,256]{1,0:T(8,128)S(1)}, f32[64,256]{1,0:T(8,128)S(1)}, f32[64,256]{1,0:T(8,128)S(1)}) custom-call(bf16[64,4096]{1,0:T(8,128)(2,1)S(1)} %copy-done.2, bf16[256,4096]{1,0:T(8,128)(2,1)S(1)} %copy-done, f32[8,128]{1,0:T(8,128)S(1)} %mark_kernel.1._, ...), custom_call_target="tpu_custom_call" | custom-call | flops 1000000 | tf_op jit(solution)/shard_map/tile_kernel/pallas_call | solution.py:183
  24.4 2.8 %collective-permute-start.12 = (f32[64,256]{1,0:T(8,128)S(1)}, f32[64,256]{1,0:T(8,128)S(1)}, u32[]{:S(2)}, u32[]{:S(2)}) collective-permute-start(f32[64,256]{1,0:T(8,128)S(1)} %get-tuple-element.27), channel_id=1, source_target_pairs={{0,2},{1,3},{2,0},{3,1},{4,6},{5,7},{6,4},{7,5},{8,10},{9,11},{10,... | collective-permute-start | bytes 196616 | tf_op jit(solution)/shard_map/ppermute | solution.py:128
  27.2 1.5 %collective-permute-start.13 = (f32[64,256]{1,0:T(8,128)S(1)}, f32[64,256]{1,0:T(8,128)S(1)}, u32[]{:S(2)}, u32[]{:S(2)}) collective-permute-start(f32[64,256]{1,0:T(8,128)S(1)} %get-tuple-element.28), channel_id=1, source_target_pairs={{0,3},{1,2},{2,1},{3,0},{4,7},{5,6},{6,5},{7,4},{8,11},{9,10},{10,... | collective-permute-start | bytes 196616 | tf_op jit(solution)/shard_map/ppermute | solution.py:128
  28.7 2.0 %collective-permute-start.11 = (f32[32,256]{1,0:T(8,128)S(1)}, f32[32,256]{1,0:T(8,128)S(1)}, u32[]{:S(2)}, u32[]{:S(2)}) collective-permute-start(f32[32,256]{1,0:T(8,128)S(1)} %get-tuple-element.26), channel_id=1, source_target_pairs={{0,1},{1,0},{2,3},{3,2},{4,5},{5,4},{6,7},{7,6},{8,9},{9,8},{10,11... | collective-permute-start | bytes 98312 | tf_op jit(solution)/shard_map/ppermute | solution.py:128
  30.7 2.7 %collective-permute-done.10.refs_1_ = f32[32,256]{1,0:T(8,128)S(1)} collective-permute-done((f32[32,256]{1,0:T(8,128)S(1)}, f32[32,256]{1,0:T(8,128)S(1)}, u32[]{:S(2)}, u32[]{:S(2)}) %collective-permute-start.10) | collective-permute-done | bytes 32800 | tf_op jit(solution)/shard_map/ppermute | solution.py:128
  33.5 0.5 %collective-permute-done.11.refs_2_ = f32[32,256]{1,0:T(8,128)S(1)} collective-permute-done((f32[32,256]{1,0:T(8,128)S(1)}, f32[32,256]{1,0:T(8,128)S(1)}, u32[]{:S(2)}, u32[]{:S(2)}) %collective-permute-start.11) | collective-permute-done | bytes 32800 | tf_op jit(solution)/shard_map/ppermute | solution.py:128
  34.0 0.1 collective-permute-start.14
  34.1 1.2 %collective-permute-done.14.other_ref = f32[64,128]{1,0:T(8,128)S(1)} collective-permute-done((f32[64,128]{1,0:T(8,128)S(1)}, f32[64,128]{1,0:T(8,128)S(1)}, u32[]{:S(2)}, u32[]{:S(2)}) %collective-permute-start.14) | collective-permute-done | bytes 32800 | tf_op jit(solution)/shard_map/ppermute | solution.py:128
  35.3 0.5 %head_kernel.1 = f32[64,128]{1,0:T(8,128)S(1)} custom-call(f32[64,128]{1,0:T(8,128)S(1)} %fusion.1.mine_ref, f32[64,128]{1,0:T(8,128)S(1)} %collective-permute-done.14.other_ref, f32[128,128]{1,0:T(8,128)S(1)} %multiply_bitcast_fusion.corner_ref, f32[2,128,128]{2,1,0:T(8,128)S(1)} %copy-done.4), custom_call_target="tpu_custom_call" | custom-call | flops 1000000 | tf_op jit(solution)/shard_map/head_kernel/pallas_call | solution.py:208
  35.8 0.7 %collective-permute-start.15 = (f32[64,128]{1,0:T(8,128)S(1)}, f32[64,128]{1,0:T(8,128)S(1)}, u32[]{:S(2)}, u32[]{:S(2)}) collective-permute-start(f32[64,128]{1,0:T(8,128)S(1)} %head_kernel.1), channel_id=1, source_target_pairs={{0,24},{4,28},{8,16},{12,20},{16,8},{20,12},{24,0},{28,4},{1,25},{... | collective-permute-start | bytes 98312 | tf_op jit(solution)/shard_map/ppermute | solution.py:128
  36.5 0.9 %collective-permute-start.16 = (f32[64,128]{1,0:T(8,128)S(1)}, f32[64,128]{1,0:T(8,128)S(1)}, u32[]{:S(2)}, u32[]{:S(2)}) collective-permute-start(f32[64,128]{1,0:T(8,128)S(1)} %head_kernel.1), channel_id=1, source_target_pairs={{0,16},{4,20},{8,24},{12,28},{16,0},{20,4},{24,8},{28,12},{1,17},{... | collective-permute-start | bytes 98312 | tf_op jit(solution)/shard_map/ppermute | solution.py:128
  37.5 1.9 %collective-permute-start.17 = (f32[64,128]{1,0:T(8,128)S(1)}, f32[64,128]{1,0:T(8,128)S(1)}, u32[]{:S(2)}, u32[]{:S(2)}) collective-permute-start(f32[64,128]{1,0:T(8,128)S(1)} %head_kernel.1), channel_id=1, source_target_pairs={{0,8},{4,12},{8,0},{12,4},{16,24},{20,28},{24,16},{28,20},{1,9},{5... | collective-permute-start | bytes 98312 | tf_op jit(solution)/shard_map/ppermute | solution.py:128
  39.4 1.6 %collective-permute-done.15 = f32[64,128]{1,0:T(8,128)S(1)} collective-permute-done((f32[64,128]{1,0:T(8,128)S(1)}, f32[64,128]{1,0:T(8,128)S(1)}, u32[]{:S(2)}, u32[]{:S(2)}) %collective-permute-start.15) | collective-permute-done | bytes 32800 | tf_op jit(solution)/shard_map/ppermute | solution.py:128
  41.0 0.4 collective-permute-done.17
  41.5 0.1 convert_multiply_fusion.refs_6_
  41.6 1.1 %collective-permute-done.18.refs_8_ = f32[64,128]{1,0:T(8,128)S(1)} collective-permute-done((f32[64,128]{1,0:T(8,128)S(1)}, f32[64,128]{1,0:T(8,128)S(1)}, u32[]{:S(2)}, u32[]{:S(2)}) %collective-permute-start.18) | collective-permute-done | bytes 32800 | tf_op jit(solution)/shard_map/ppermute | solution.py:128
  42.7 1.1 %solve_kernel.1 = f32[64,1024]{1,0:T(8,128)} custom-call(f32[64,256]{1,0:T(8,128)S(1)} %get-tuple-element.29.refs_0_, f32[32,256]{1,0:T(8,128)S(1)} %collective-permute-done.10.refs_1_, f32[32,256]{1,0:T(8,128)S(1)} %collective-permute-done.11.refs_2_, f32[64,256]{1,0:T(8,128)S(1)} %collective-permute-done.12.refs_3_, ...), custom_call_target="tpu_custom_call" | custom-call | tf_op jit(solution)/shard_map/solve_kernel/pallas_call | solution.py:223
  (31 shorter events, 0.2 us)
Async XLA Ops:
  0.0 1.0 %copy-start.1 = (bf16[64,4096]{1,0:T(8,128)(2,1)S(1)}, bf16[64,4096]{1,0:T(8,128)(2,1)}, u32[]{:S(2)}) copy-start(bf16[64,4096]{1,0:T(8,128)(2,1)} %own_hbm.1) | copy-start | bytes 1572868
  1.0 11.1 %copy-start.4 = (f32[2,128,128]{2,1,0:T(8,128)S(1)}, f32[2,128,128]{2,1,0:T(8,128)}, u32[]{:S(2)}) copy-start(f32[2,128,128]{2,1,0:T(8,128)} %inverse_ref.1) | copy-start | bytes 393220
  1.1 11.1 %collective-permute-start = (bf16[64,1024]{1,0:T(8,128)(2,1)S(1)}, bf16[64,1024]{1,0:T(8,128)(2,1)S(1)}, u32[]{:S(2)}, u32[]{:S(2)}) collective-permute-start(bf16[64,1024]{1,0:T(8,128)(2,1)S(1)} %get-tuple-element.20), channel_id=1, source_target_pairs={{0,2},{1,3},{2,0},{3,1},{4,7},{5,6},{6,5},{7,4},{8,10},{9,11},{10,... | collective-permute-start | bytes 393224 | tf_op jit(solution)/shard_map/ppermute | solution.py:158
  5.2 10.6 %collective-permute-start.1 = (bf16[64,2048]{1,0:T(8,128)(2,1)S(1)}, bf16[64,2048]{1,0:T(8,128)(2,1)S(1)}, u32[]{:S(2)}, u32[]{:S(2)}) collective-permute-start(bf16[64,2048]{1,0:T(8,128)(2,1)S(1)} %get-tuple-element.22), channel_id=1, source_target_pairs={{0,1},{1,0},{2,3},{3,2},{4,5},{5,4},{6,7},{7,6},{8,9},{9,8},{10,11... | collective-permute-start | bytes 786440 | tf_op jit(solution)/shard_map/ppermute | solution.py:128
  8.7 25.3 %all-to-all-start = ((f16[4,2,128,256]{3,2,1,0:T(8,128)(2,1)}), f16[4,2,128,256]{3,2,1,0:T(8,128)(2,1)S(1)}, u32[]{:S(2)}, u32[]{:S(2)}) async-start(f16[4,2,128,256]{3,2,1,0:T(8,128)(2,1)} %bitcast), calls=%async_computation | async-start | bytes 1048576 | tf_op jit(solution)/shard_map/all_to_all | solution.py:165
  12.2 10.8 %copy-start = (bf16[256,4096]{1,0:T(8,128)(2,1)S(1)}, bf16[256,4096]{1,0:T(8,128)(2,1)}, u32[]{:S(2)}) copy-start(bf16[256,4096]{1,0:T(8,128)(2,1)} %support_ref.1) | copy-start | bytes 6291460
  12.2 10.8 %copy-start.2 = (bf16[64,4096]{1,0:T(8,128)(2,1)S(1)}, bf16[64,4096]{1,0:T(8,128)(2,1)}, u32[]{:S(2)}) copy-start(bf16[64,4096]{1,0:T(8,128)(2,1)} %own_hbm.1) | copy-start | bytes 1572868
  12.2 6.1 %collective-permute-start.4 = (bf16[64,1024]{1,0:T(8,128)(2,1)S(1)}, bf16[64,1024]{1,0:T(8,128)(2,1)S(1)}, u32[]{:S(2)}, u32[]{:S(2)}) collective-permute-start(bf16[64,1024]{1,0:T(8,128)(2,1)S(1)} %collective-permute-done.refs_2_), channel_id=1, source_target_pairs={{0,8},{4,12},{8,0},{12,4},{16,24},{20,28},{24,16},{28,20},{1,9},{5... | collective-permute-start | bytes 393224 | tf_op jit(solution)/shard_map/ppermute | solution.py:128
  13.8 7.7 %collective-permute-start.6 = (bf16[64,1024]{1,0:T(8,128)(2,1)S(1)}, bf16[64,1024]{1,0:T(8,128)(2,1)S(1)}, u32[]{:S(2)}, u32[]{:S(2)}) collective-permute-start(bf16[64,1024]{1,0:T(8,128)(2,1)S(1)} %collective-permute-done.refs_2_), channel_id=1, source_target_pairs={{0,16},{4,20},{8,24},{12,28},{16,0},{20,4},{24,8},{28,12},{1,17},{... | collective-permute-start | bytes 393224 | tf_op jit(solution)/shard_map/ppermute | solution.py:128
  15.3 6.2 %collective-permute-start.8 = (bf16[64,1024]{1,0:T(8,128)(2,1)S(1)}, bf16[64,1024]{1,0:T(8,128)(2,1)S(1)}, u32[]{:S(2)}, u32[]{:S(2)}) collective-permute-start(bf16[64,1024]{1,0:T(8,128)(2,1)S(1)} %collective-permute-done.refs_2_), channel_id=1, source_target_pairs={{0,24},{4,28},{8,16},{12,20},{16,8},{20,12},{24,0},{28,4},{1,25},{... | collective-permute-start | bytes 393224 | tf_op jit(solution)/shard_map/ppermute | solution.py:128
  15.8 7.2 %collective-permute-start.2 = (bf16[64,2048]{1,0:T(8,128)(2,1)S(1)}, bf16[64,2048]{1,0:T(8,128)(2,1)S(1)}, u32[]{:S(2)}, u32[]{:S(2)}) collective-permute-start(bf16[64,2048]{1,0:T(8,128)(2,1)S(1)} %collective-permute-done.1.refs_0_), channel_id=1, source_target_pairs={{0,4},{4,0},{8,12},{12,8},{16,20},{20,16},{24,28},{28,24},{1,5},{5... | collective-permute-start | bytes 786440 | tf_op jit(solution)/shard_map/ppermute | solution.py:128
  15.8 6.2 %collective-permute-start.3 = (bf16[64,1024]{1,0:T(8,128)(2,1)S(1)}, bf16[64,1024]{1,0:T(8,128)(2,1)S(1)}, u32[]{:S(2)}, u32[]{:S(2)}) collective-permute-start(bf16[64,1024]{1,0:T(8,128)(2,1)S(1)} %collective-permute-done.refs_2_), channel_id=1, source_target_pairs={{0,4},{4,0},{8,12},{12,8},{16,20},{20,16},{24,28},{28,24},{1,5},{5... | collective-permute-start | bytes 393224 | tf_op jit(solution)/shard_map/ppermute | solution.py:128
  18.3 3.7 %collective-permute-start.5 = (bf16[64,1024]{1,0:T(8,128)(2,1)S(1)}, bf16[64,1024]{1,0:T(8,128)(2,1)S(1)}, u32[]{:S(2)}, u32[]{:S(2)}) collective-permute-start(bf16[64,1024]{1,0:T(8,128)(2,1)S(1)} %collective-permute-done.4.refs_4_), channel_id=1, source_target_pairs={{0,4},{4,0},{8,12},{12,8},{16,20},{20,16},{24,28},{28,24},{1,5},{5... | collective-permute-start | bytes 393224 | tf_op jit(solution)/shard_map/ppermute | solution.py:128
  21.5 1.3 %collective-permute-start.7 = (bf16[64,1024]{1,0:T(8,128)(2,1)S(1)}, bf16[64,1024]{1,0:T(8,128)(2,1)S(1)}, u32[]{:S(2)}, u32[]{:S(2)}) collective-permute-start(bf16[64,1024]{1,0:T(8,128)(2,1)S(1)} %collective-permute-done.6.refs_6_), channel_id=1, source_target_pairs={{0,4},{4,0},{8,12},{12,8},{16,20},{20,16},{24,28},{28,24},{1,5},{5... | collective-permute-start | bytes 393224 | tf_op jit(solution)/shard_map/ppermute | solution.py:128
  21.5 1.5 %collective-permute-start.9 = (bf16[64,1024]{1,0:T(8,128)(2,1)S(1)}, bf16[64,1024]{1,0:T(8,128)(2,1)S(1)}, u32[]{:S(2)}, u32[]{:S(2)}) collective-permute-start(bf16[64,1024]{1,0:T(8,128)(2,1)S(1)} %collective-permute-done.8.refs_8_), channel_id=1, source_target_pairs={{0,4},{4,0},{8,12},{12,8},{16,20},{20,16},{24,28},{28,24},{1,5},{5... | collective-permute-start | bytes 393224 | tf_op jit(solution)/shard_map/ppermute | solution.py:128
  24.4 18.3 %copy-start.3 = (f32[2,128,256]{2,1,0:T(8,128)S(1)}, f32[2,128,256]{2,1,0:T(8,128)}, u32[]{:S(2)}) copy-start(f32[2,128,256]{2,1,0:T(8,128)} %refs_5_.1) | copy-start | bytes 786436
  24.4 9.6 %collective-permute-start.12 = (f32[64,256]{1,0:T(8,128)S(1)}, f32[64,256]{1,0:T(8,128)S(1)}, u32[]{:S(2)}, u32[]{:S(2)}) collective-permute-start(f32[64,256]{1,0:T(8,128)S(1)} %get-tuple-element.27), channel_id=1, source_target_pairs={{0,2},{1,3},{2,0},{3,1},{4,6},{5,7},{6,4},{7,5},{8,10},{9,11},{10,... | collective-permute-start | bytes 196616 | tf_op jit(solution)/shard_map/ppermute | solution.py:128
  27.2 6.8 %collective-permute-start.13 = (f32[64,256]{1,0:T(8,128)S(1)}, f32[64,256]{1,0:T(8,128)S(1)}, u32[]{:S(2)}, u32[]{:S(2)}) collective-permute-start(f32[64,256]{1,0:T(8,128)S(1)} %get-tuple-element.28), channel_id=1, source_target_pairs={{0,3},{1,2},{2,1},{3,0},{4,7},{5,6},{6,5},{7,4},{8,11},{9,10},{10,... | collective-permute-start | bytes 196616 | tf_op jit(solution)/shard_map/ppermute | solution.py:128
  28.7 4.8 %collective-permute-start.10 = (f32[32,256]{1,0:T(8,128)S(1)}, f32[32,256]{1,0:T(8,128)S(1)}, u32[]{:S(2)}, u32[]{:S(2)}) collective-permute-start(f32[32,256]{1,0:T(8,128)S(1)} %get-tuple-element.25), channel_id=1, source_target_pairs={{0,1},{1,0},{2,3},{3,2},{4,5},{5,4},{6,7},{7,6},{8,9},{9,8},{10,11... | collective-permute-start | bytes 98312 | tf_op jit(solution)/shard_map/ppermute | solution.py:128
  28.7 5.3 %collective-permute-start.11 = (f32[32,256]{1,0:T(8,128)S(1)}, f32[32,256]{1,0:T(8,128)S(1)}, u32[]{:S(2)}, u32[]{:S(2)}) collective-permute-start(f32[32,256]{1,0:T(8,128)S(1)} %get-tuple-element.26), channel_id=1, source_target_pairs={{0,1},{1,0},{2,3},{3,2},{4,5},{5,4},{6,7},{7,6},{8,9},{9,8},{10,11... | collective-permute-start | bytes 98312 | tf_op jit(solution)/shard_map/ppermute | solution.py:128
  34.0 1.3 %collective-permute-start.14 = (f32[64,128]{1,0:T(8,128)S(1)}, f32[64,128]{1,0:T(8,128)S(1)}, u32[]{:S(2)}, u32[]{:S(2)}) collective-permute-start(f32[64,128]{1,0:T(8,128)S(1)} %fusion.1.mine_ref), channel_id=1, source_target_pairs={{0,4},{4,0},{8,12},{12,8},{16,20},{20,16},{24,28},{28,24},{1,5},{5... | collective-permute-start | bytes 98312 | tf_op jit(solution)/shard_map/ppermute | solution.py:128
  35.8 5.1 %collective-permute-start.15 = (f32[64,128]{1,0:T(8,128)S(1)}, f32[64,128]{1,0:T(8,128)S(1)}, u32[]{:S(2)}, u32[]{:S(2)}) collective-permute-start(f32[64,128]{1,0:T(8,128)S(1)} %head_kernel.1), channel_id=1, source_target_pairs={{0,24},{4,28},{8,16},{12,20},{16,8},{20,12},{24,0},{28,4},{1,25},{... | collective-permute-start | bytes 98312 | tf_op jit(solution)/shard_map/ppermute | solution.py:128
  36.5 4.4 %collective-permute-start.16 = (f32[64,128]{1,0:T(8,128)S(1)}, f32[64,128]{1,0:T(8,128)S(1)}, u32[]{:S(2)}, u32[]{:S(2)}) collective-permute-start(f32[64,128]{1,0:T(8,128)S(1)} %head_kernel.1), channel_id=1, source_target_pairs={{0,16},{4,20},{8,24},{12,28},{16,0},{20,4},{24,8},{28,12},{1,17},{... | collective-permute-start | bytes 98312 | tf_op jit(solution)/shard_map/ppermute | solution.py:128
  37.5 3.9 %collective-permute-start.17 = (f32[64,128]{1,0:T(8,128)S(1)}, f32[64,128]{1,0:T(8,128)S(1)}, u32[]{:S(2)}, u32[]{:S(2)}) collective-permute-start(f32[64,128]{1,0:T(8,128)S(1)} %head_kernel.1), channel_id=1, source_target_pairs={{0,8},{4,12},{8,0},{12,4},{16,24},{20,28},{24,16},{28,20},{1,9},{5... | collective-permute-start | bytes 98312 | tf_op jit(solution)/shard_map/ppermute | solution.py:128
  41.4 1.3 %collective-permute-start.18 = (f32[64,128]{1,0:T(8,128)S(1)}, f32[64,128]{1,0:T(8,128)S(1)}, u32[]{:S(2)}, u32[]{:S(2)}) collective-permute-start(f32[64,128]{1,0:T(8,128)S(1)} %select_select_fusion.refs_7_), channel_id=1, source_target_pairs={{0,4},{4,0},{8,12},{12,8},{16,20},{20,16},{24,28},{28,24},{1,5},{5... | collective-permute-start | bytes 98312 | tf_op jit(solution)/shard_map/ppermute | solution.py:128

commit v6 on v5

--- a/solution.py
+++ b/solution.py
@@ -92,36 +92,44 @@
         out_ref[...] = jnp.exp(scale * total[start:start + out_ref.shape[0]])
 
 
-def head_kernel(mine_ref, other_ref, corner_ref, inverse_ref, out_ref):
-    odd = lax.axis_index("row") % 2
-    other = jnp.where(odd == 1, other_ref[...], 0.0)
-    head = mine_ref[...] - dot32(dot32(other, inverse_ref[0], NT), corner_ref[...], NN)
-    out_ref[...] = dot32(head, inverse_ref[odd], NT)
-
-
-def solve_kernel(n_col, pivot, *refs):
+def mix_kernel(corner_ref, inverse_ref, out_ref):
+    out_ref[...] = dot32(dot32(inverse_ref[0], corner_ref[...], TN), inverse_ref[1], NT)
+
+
+def base_kernel(mine_ref, inverse_ref, out_ref):
+    out_ref[...] = dot32(mine_ref[...], inverse_ref[lax.axis_index("row") % 2], NT)
+
+
+def head_kernel(base_ref, other_ref, mix_ref, out_ref):
+    other = jnp.where(lax.axis_index("row") % 2 == 1, other_ref[...], 0.0)
+    out_ref[...] = base_ref[...] - dot32(other, mix_ref[...], NN)
+
+
+def mine_kernel(n_col, *refs):
     tiles, refs = [ref[...] for ref in refs[:n_col + 1]], refs[n_col + 1:]
     tiles[1:3] = [jnp.concatenate(tiles[1:3], axis=0)]
-    own_ref, panels_ref, mine_ref, other_ref, out_ref = refs
+    own_ref, panels_ref, mine_ref, out_ref = refs
     span = own_ref.shape[2]
     row, col = lax.axis_index("row"), lax.axis_index("col")
-    even = row % 2 == 0
-    mine, other = mine_ref[...], other_ref[...]
-    first = jnp.where(even, mine, other)
-    second = jnp.where(even, other, mine)
     for step in range(n_col):
         plane = col ^ step
         block = own_ref if step == 0 else panels_ref.at[plane]
-        value = tiles[step] - dot32(first, block[0], NN) - dot32(second, block[1], NN)
+        value = tiles[step] - dot32(mine_ref[...], block[row % 2], NN)
         out_ref[:, pl.ds(pl.multiple_of(plane * span, span), span)] = value
 
-    @pl.when(row == 0)
+
+def other_kernel(n_col, pivot, part_ref, own_ref, panels_ref, mine_ref, other_ref, out_ref):
+    span = own_ref.shape[2]
+    row, col = lax.axis_index("row"), lax.axis_index("col")
+    for step in range(n_col):
+        plane = col ^ step
+        block = own_ref if step == 0 else panels_ref.at[plane]
+        cols = pl.ds(pl.multiple_of(plane * span, span), span)
+        out_ref[:, cols] = part_ref[:, cols] - dot32(other_ref[...], block[1 - row % 2], NN)
+
+    @pl.when(row < 2)
     def _():
-        out_ref[:, :pivot] = first
-
-    @pl.when(row == 1)
-    def _():
-        out_ref[:, :pivot] = second
+        out_ref[:, :pivot] = mine_ref[...]
 
 
 def exchange(value, axis, size, mask):
@@ -205,29 +213,57 @@
     head = heads[0]
     for j in range(1, n_col):
         head = jnp.where(col == j, heads[j], head)
+    mix = pl.pallas_call(
+        mix_kernel,
+        out_shape=jax.ShapeDtypeStruct((pivot, pivot), jnp.float32),
+        in_specs=[VMEM] * 2,
+        out_specs=VMEM,
+        compiler_params=SOLVE_PARAMS,
+        cost_estimate=SHORT,
+        name="mix_kernel",
+    )(corner, diag_inverses)
+    base = pl.pallas_call(
+        base_kernel,
+        out_shape=jax.ShapeDtypeStruct((rows, pivot), jnp.float32),
+        in_specs=[VMEM] * 2,
+        out_specs=VMEM,
+        compiler_params=SOLVE_PARAMS,
+        cost_estimate=SHORT,
+        name="base_kernel",
+    )(head, diag_inverses)
     head = pl.pallas_call(
         head_kernel,
         out_shape=jax.ShapeDtypeStruct((rows, pivot), jnp.float32),
-        in_specs=[VMEM] * 4,
+        in_specs=[VMEM] * 3,
         out_specs=VMEM,
         compiler_params=SOLVE_PARAMS,
         cost_estimate=SHORT,
         name="head_kernel",
-    )(head, exchange(head, "row", n_row, 1), corner, diag_inverses)
+    )(base, exchange(head, "row", n_row, 1), mix)
     spread = head
     for i in range(2, n_row, 2):
         spread = jnp.where(row // 2 == i // 2, exchange(head, "row", n_row, i), spread)
     swapped = exchange(spread, "row", n_row, 1)
     blocks = blocks.astype(jnp.float32) * (1 / PANEL_UNIT)
 
+    part = pl.pallas_call(
+        functools.partial(mine_kernel, n_col),
+        out_shape=jax.ShapeDtypeStruct((rows, span * n_col), jnp.float32),
+        in_specs=[VMEM] * (n_col + 4),
+        out_specs=VMEM,
+        compiler_params=SOLVE_PARAMS,
+        cost_estimate=SHORT,
+        name="mine_kernel",
+    )(*tiles, panels, blocks, spread)
     return pl.pallas_call(
-        functools.partial(solve_kernel, n_col, pivot),
+        functools.partial(other_kernel, n_col, pivot),
         out_shape=jax.ShapeDtypeStruct((rows, span * n_col), jnp.float32),
-        in_specs=[VMEM] * (n_col + 5),
-        out_specs=VMEM,
-        compiler_params=SOLVE_PARAMS,
-        name="solve_kernel",
-    )(*tiles, panels, blocks, spread, swapped)
+        in_specs=[VMEM] * 5,
+        out_specs=VMEM,
+        compiler_params=SOLVE_PARAMS,
+        cost_estimate=SHORT,
+        name="other_kernel",
+    )(part, panels, blocks, spread, swapped)
 
 
 def solution(mesh):

time: 44 us -> 43.5 us (0.989)
  waiting for transfers between devices: 13.7 us -> 12.8 us
    ppermute x18, waiting for transfers between devices: 13.7 us -> 12.8 us  [exchange(): return lax.ppermute(value, axis, [(i, i ^ mask) for i in range(size)])]
    pallas_call x1 -> x4, Pallas kernels: 1.08 us -> 1.86 us  [the longest x1 0.98 us: shards(): pl.pallas_call(functools.partial(other_kernel, n_col, pivot), out_shape=j...]
  transfers between devices with their start and end apart: 20 -> 20, of which waited for: 10 -> 10; matrix products, arithmetic and copies ran while one was open for 5% -> 5% of each run, Pallas kernels for 3% -> 5%
where the time goes in v6:
time: 43.5 us; the launch traced here: 43.3 us
  starting transfers between devices  23.8 us (55%)
  waiting for transfers between devices  12.8 us (29%)
  Pallas kernels  3.44 us (8%)
  other arithmetic  2.03 us (5%)
  local copies, waits for them, and re-layouts  1.07 us (2%)
    ppermute x18, starting transfers between devices, exchange(): return lax.ppermute(value, axis, [(i, i ^ mask) for i in range(size)])  16.2 us
    ppermute x18, waiting for transfers between devices, exchange(): return lax.ppermute(value, axis, [(i, i ^ mask) for i in range(size)])  12.8 us
    ppermute x1, starting transfers between devices, shards(): lax.ppermute(mine, ('row', 'col'), [(r * n_col + c, r * n_col + (c ^ j +...  4.1 us
    all_to_all x1, starting transfers between devices, shards(): blocks = lax.all_to_all(small, 'col', 0, 0)  3.47 us
    pallas_call x1, Pallas kernels, shards(): pl.pallas_call(functools.partial(tile_kernel, scale, n_row, n_col), out_s...  1.38 us
    unnamed x10, local copies, waits for them, and re-layouts  1.06 us
    pallas_call x1, Pallas kernels, shards(): pl.pallas_call(functools.partial(other_kernel, n_col, pivot), out_shape=j...  0.98 us
    another operation x1, other arithmetic  0.97 us
  transfers between devices with their start and end apart: 20, of which 10 were waited for; matrix products, arithmetic and copies ran while one was open for 5% of the time, Pallas kernels for 5%

profile of v6, /device:TPU:0, one launch (start us, length us, event | category | flops | bytes accessed | tf_op | source)
XLA Modules:
  0.0 43.3 jit_solution(1073949602877378616)
XLA Ops:
  0.0 1.0 %copy-done.2 = bf16[64,4096]{1,0:T(8,128)(2,1)S(1)} copy-done((bf16[64,4096]{1,0:T(8,128)(2,1)S(1)}, bf16[64,4096]{1,0:T(8,128)(2,1)}, u32[]{:S(2)}) %copy-start.2) | copy-done | bytes 524312
  1.1 4.1 %collective-permute-start = (bf16[64,1024]{1,0:T(8,128)(2,1)S(1)}, bf16[64,1024]{1,0:T(8,128)(2,1)S(1)}, u32[]{:S(2)}, u32[]{:S(2)}) collective-permute-start(bf16[64,1024]{1,0:T(8,128)(2,1)S(1)} %get-tuple-element.20), channel_id=1, source_target_pairs={{0,2},{1,3},{2,0},{3,1},{4,7},{5,6},{6,5},{7,4},{8,10},{9,11},{10,... | collective-permute-start | bytes 393224 | tf_op jit(solution)/shard_map/ppermute | solution.py:166
  5.2 1.6 %collective-permute-start.1 = (bf16[64,2048]{1,0:T(8,128)(2,1)S(1)}, bf16[64,2048]{1,0:T(8,128)(2,1)S(1)}, u32[]{:S(2)}, u32[]{:S(2)}) collective-permute-start(bf16[64,2048]{1,0:T(8,128)(2,1)S(1)} %get-tuple-element.22), channel_id=1, source_target_pairs={{0,1},{1,0},{2,3},{3,2},{4,5},{5,4},{6,7},{7,6},{8,9},{9,8},{10,11... | collective-permute-start | bytes 786440 | tf_op jit(solution)/shard_map/ppermute | solution.py:136
  6.8 1.0 %multiply_convert_fusion = f16[2,128,256]{2,1,0:T(8,128)(2,1)S(1)} fusion(f32[2,128,256]{2,1,0:T(8,128)} %own_ref.1), kind=kLoop, calls=%fused_computation.2 | loop fusion | flops 131072 | bytes 393216 | tf_op jit(solution)/shard_map/convert
  7.8 0.9 %pad_maximum_fusion = f16[8,128,256]{2,1,0:T(8,128)(2,1)} fusion(f16[2,128,256]{2,1,0:T(8,128)(2,1)S(1)} %multiply_convert_fusion), kind=kLoop, calls=%fused_computation.1 | loop fusion | flops 786432 | bytes 655360 | tf_op jit(solution)/shard_map/concatenate | solution.py:171
  8.7 3.5 %all-to-all-start = ((f16[4,2,128,256]{3,2,1,0:T(8,128)(2,1)}), f16[4,2,128,256]{3,2,1,0:T(8,128)(2,1)S(1)}, u32[]{:S(2)}, u32[]{:S(2)}) async-start(f16[4,2,128,256]{3,2,1,0:T(8,128)(2,1)} %bitcast), calls=%async_computation | async-start | bytes 1048576 | tf_op jit(solution)/shard_map/all_to_all | solution.py:173
  12.2 1.6 %collective-permute-start.4 = (bf16[64,1024]{1,0:T(8,128)(2,1)S(1)}, bf16[64,1024]{1,0:T(8,128)(2,1)S(1)}, u32[]{:S(2)}, u32[]{:S(2)}) collective-permute-start(bf16[64,1024]{1,0:T(8,128)(2,1)S(1)} %collective-permute-done.refs_2_), channel_id=1, source_target_pairs={{0,8},{4,12},{8,0},{12,4},{16,24},{20,28},{24,16},{28,20},{1,9},{5... | collective-permute-start | bytes 393224 | tf_op jit(solution)/shard_map/ppermute | solution.py:136
  13.8 1.5 %collective-permute-start.6 = (bf16[64,1024]{1,0:T(8,128)(2,1)S(1)}, bf16[64,1024]{1,0:T(8,128)(2,1)S(1)}, u32[]{:S(2)}, u32[]{:S(2)}) collective-permute-start(bf16[64,1024]{1,0:T(8,128)(2,1)S(1)} %collective-permute-done.refs_2_), channel_id=1, source_target_pairs={{0,16},{4,20},{8,24},{12,28},{16,0},{20,4},{24,8},{28,12},{1,17},{... | collective-permute-start | bytes 393224 | tf_op jit(solution)/shard_map/ppermute | solution.py:136
  15.3 0.5 %collective-permute-start.8 = (bf16[64,1024]{1,0:T(8,128)(2,1)S(1)}, bf16[64,1024]{1,0:T(8,128)(2,1)S(1)}, u32[]{:S(2)}, u32[]{:S(2)}) collective-permute-start(bf16[64,1024]{1,0:T(8,128)(2,1)S(1)} %collective-permute-done.refs_2_), channel_id=1, source_target_pairs={{0,24},{4,28},{8,16},{12,20},{16,8},{20,12},{24,0},{28,4},{1,25},{... | collective-permute-start | bytes 393224 | tf_op jit(solution)/shard_map/ppermute | solution.py:136
  15.8 0.5 %collective-permute-start.3 = (bf16[64,1024]{1,0:T(8,128)(2,1)S(1)}, bf16[64,1024]{1,0:T(8,128)(2,1)S(1)}, u32[]{:S(2)}, u32[]{:S(2)}) collective-permute-start(bf16[64,1024]{1,0:T(8,128)(2,1)S(1)} %collective-permute-done.refs_2_), channel_id=1, source_target_pairs={{0,4},{4,0},{8,12},{12,8},{16,20},{20,16},{24,28},{28,24},{1,5},{5... | collective-permute-start | bytes 393224 | tf_op jit(solution)/shard_map/ppermute | solution.py:136
  16.3 2.0 %collective-permute-done.4.refs_4_ = bf16[64,1024]{1,0:T(8,128)(2,1)S(1)} collective-permute-done((bf16[64,1024]{1,0:T(8,128)(2,1)S(1)}, bf16[64,1024]{1,0:T(8,128)(2,1)S(1)}, u32[]{:S(2)}, u32[]{:S(2)}) %collective-permute-start.4) | collective-permute-done | bytes 131104 | tf_op jit(solution)/shard_map/ppermute | solution.py:136
  18.3 3.1 %collective-permute-done.6.refs_6_ = bf16[64,1024]{1,0:T(8,128)(2,1)S(1)} collective-permute-done((bf16[64,1024]{1,0:T(8,128)(2,1)S(1)}, bf16[64,1024]{1,0:T(8,128)(2,1)S(1)}, u32[]{:S(2)}, u32[]{:S(2)}) %collective-permute-start.6) | collective-permute-done | bytes 131104 | tf_op jit(solution)/shard_map/ppermute | solution.py:136
  21.5 0.5 %collective-permute-start.9 = (bf16[64,1024]{1,0:T(8,128)(2,1)S(1)}, bf16[64,1024]{1,0:T(8,128)(2,1)S(1)}, u32[]{:S(2)}, u32[]{:S(2)}) collective-permute-start(bf16[64,1024]{1,0:T(8,128)(2,1)S(1)} %collective-permute-done.8.refs_8_), channel_id=1, source_target_pairs={{0,4},{4,0},{8,12},{12,8},{16,20},{20,16},{24,28},{28,24},{1,5},{5... | collective-permute-start | bytes 393224 | tf_op jit(solution)/shard_map/ppermute | solution.py:136
  22.0 0.8 %collective-permute-done.7.refs_7_ = bf16[64,1024]{1,0:T(8,128)(2,1)S(1)} collective-permute-done((bf16[64,1024]{1,0:T(8,128)(2,1)S(1)}, bf16[64,1024]{1,0:T(8,128)(2,1)S(1)}, u32[]{:S(2)}, u32[]{:S(2)}) %collective-permute-start.7) | collective-permute-done | bytes 131104 | tf_op jit(solution)/shard_map/ppermute | solution.py:136
  22.8 0.2 collective-permute-done.9.refs_9_
  23.0 1.4 %tile_kernel.1 = (f32[64,256]{1,0:T(8,128)S(1)}, f32[32,256]{1,0:T(8,128)S(1)}, f32[32,256]{1,0:T(8,128)S(1)}, f32[64,256]{1,0:T(8,128)S(1)}, f32[64,256]{1,0:T(8,128)S(1)}) custom-call(bf16[64,4096]{1,0:T(8,128)(2,1)S(1)} %copy-done.3, bf16[256,4096]{1,0:T(8,128)(2,1)S(1)} %copy-done.1, f32[8,128]{1,0:T(8,128)S(1)} %mark_kernel.1._, ...), custom_call_target="tpu_custom_call" | custom-call | flops 1000000 | tf_op jit(solution)/shard_map/tile_kernel/pallas_call | solution.py:191
  24.4 2.8 %collective-permute-start.12 = (f32[64,256]{1,0:T(8,128)S(1)}, f32[64,256]{1,0:T(8,128)S(1)}, u32[]{:S(2)}, u32[]{:S(2)}) collective-permute-start(f32[64,256]{1,0:T(8,128)S(1)} %get-tuple-element.27), channel_id=1, source_target_pairs={{0,2},{1,3},{2,0},{3,1},{4,6},{5,7},{6,4},{7,5},{8,10},{9,11},{10,... | collective-permute-start | bytes 196616 | tf_op jit(solution)/shard_map/ppermute | solution.py:136
  27.2 1.5 %collective-permute-start.13 = (f32[64,256]{1,0:T(8,128)S(1)}, f32[64,256]{1,0:T(8,128)S(1)}, u32[]{:S(2)}, u32[]{:S(2)}) collective-permute-start(f32[64,256]{1,0:T(8,128)S(1)} %get-tuple-element.28), channel_id=1, source_target_pairs={{0,3},{1,2},{2,1},{3,0},{4,7},{5,6},{6,5},{7,4},{8,11},{9,10},{10,... | collective-permute-start | bytes 196616 | tf_op jit(solution)/shard_map/ppermute | solution.py:136
  28.7 2.0 %collective-permute-start.11 = (f32[32,256]{1,0:T(8,128)S(1)}, f32[32,256]{1,0:T(8,128)S(1)}, u32[]{:S(2)}, u32[]{:S(2)}) collective-permute-start(f32[32,256]{1,0:T(8,128)S(1)} %get-tuple-element.26), channel_id=1, source_target_pairs={{0,1},{1,0},{2,3},{3,2},{4,5},{5,4},{6,7},{7,6},{8,9},{9,8},{10,11... | collective-permute-start | bytes 98312 | tf_op jit(solution)/shard_map/ppermute | solution.py:136
  30.7 2.7 %collective-permute-done.10.refs_1_ = f32[32,256]{1,0:T(8,128)S(1)} collective-permute-done((f32[32,256]{1,0:T(8,128)S(1)}, f32[32,256]{1,0:T(8,128)S(1)}, u32[]{:S(2)}, u32[]{:S(2)}) %collective-permute-start.10) | collective-permute-done | bytes 32800 | tf_op jit(solution)/shard_map/ppermute | solution.py:136
  33.5 0.5 %collective-permute-done.11.refs_2_ = f32[32,256]{1,0:T(8,128)S(1)} collective-permute-done((f32[32,256]{1,0:T(8,128)S(1)}, f32[32,256]{1,0:T(8,128)S(1)}, u32[]{:S(2)}, u32[]{:S(2)}) %collective-permute-start.11) | collective-permute-done | bytes 32800 | tf_op jit(solution)/shard_map/ppermute | solution.py:136
  34.1 0.2 base_kernel.1.base_ref
  34.3 0.4 mix_kernel.1.mix_ref
  34.7 0.6 %collective-permute-done.14.other_ref = f32[64,128]{1,0:T(8,128)S(1)} collective-permute-done((f32[64,128]{1,0:T(8,128)S(1)}, f32[64,128]{1,0:T(8,128)S(1)}, u32[]{:S(2)}, u32[]{:S(2)}) %collective-permute-start.14) | collective-permute-done | bytes 32800 | tf_op jit(solution)/shard_map/ppermute | solution.py:136
  35.5 0.7 %collective-permute-start.15 = (f32[64,128]{1,0:T(8,128)S(1)}, f32[64,128]{1,0:T(8,128)S(1)}, u32[]{:S(2)}, u32[]{:S(2)}) collective-permute-start(f32[64,128]{1,0:T(8,128)S(1)} %head_kernel.1), channel_id=1, source_target_pairs={{0,24},{4,28},{8,16},{12,20},{16,8},{20,12},{24,0},{28,4},{1,25},{... | collective-permute-start | bytes 98312 | tf_op jit(solution)/shard_map/ppermute | solution.py:136
  36.2 0.9 %collective-permute-start.16 = (f32[64,128]{1,0:T(8,128)S(1)}, f32[64,128]{1,0:T(8,128)S(1)}, u32[]{:S(2)}, u32[]{:S(2)}) collective-permute-start(f32[64,128]{1,0:T(8,128)S(1)} %head_kernel.1), channel_id=1, source_target_pairs={{0,16},{4,20},{8,24},{12,28},{16,0},{20,4},{24,8},{28,12},{1,17},{... | collective-permute-start | bytes 98312 | tf_op jit(solution)/shard_map/ppermute | solution.py:136
  37.1 1.9 %collective-permute-start.17 = (f32[64,128]{1,0:T(8,128)S(1)}, f32[64,128]{1,0:T(8,128)S(1)}, u32[]{:S(2)}, u32[]{:S(2)}) collective-permute-start(f32[64,128]{1,0:T(8,128)S(1)} %head_kernel.1), channel_id=1, source_target_pairs={{0,8},{4,12},{8,0},{12,4},{16,24},{20,28},{24,16},{28,20},{1,9},{5... | collective-permute-start | bytes 98312 | tf_op jit(solution)/shard_map/ppermute | solution.py:136
  39.0 1.6 %collective-permute-done.15 = f32[64,128]{1,0:T(8,128)S(1)} collective-permute-done((f32[64,128]{1,0:T(8,128)S(1)}, f32[64,128]{1,0:T(8,128)S(1)}, u32[]{:S(2)}, u32[]{:S(2)}) %collective-permute-start.15) | collective-permute-done | bytes 32800 | tf_op jit(solution)/shard_map/ppermute | solution.py:136
  40.6 0.4 collective-permute-done.17
  41.2 0.3 mine_kernel.1.part_ref
  41.5 0.8 %collective-permute-done.18.other_ref = f32[64,128]{1,0:T(8,128)S(1)} collective-permute-done((f32[64,128]{1,0:T(8,128)S(1)}, f32[64,128]{1,0:T(8,128)S(1)}, u32[]{:S(2)}, u32[]{:S(2)}) %collective-permute-start.18) | collective-permute-done | bytes 32800 | tf_op jit(solution)/shard_map/ppermute | solution.py:136
  42.3 1.0 %other_kernel.1 = f32[64,1024]{1,0:T(8,128)} custom-call(f32[64,1024]{1,0:T(8,128)S(1)} %mine_kernel.1.part_ref, f32[2,128,256]{2,1,0:T(8,128)S(1)} %copy-done, f32[4,2,128,256]{3,2,1,0:T(8,128)S(1)} %convert_multiply_fusion.refs_6_.panels_ref, f32[64,128]{1,0:T(8,128)S(1)} %select_select_fusion.refs_7_.mine_ref, f32[64,128]{1,0:T(8,128)S(1)} %collective-permute-done.18.other_ref), custom_call_target="tpu_custom_call" | custom-call | flops 1000000 | tf_op jit(solution)/shard_map/other_kernel/pallas_call | solution.py:258
  (34 shorter events, 0.5 us)
Async XLA Ops:
  0.0 1.0 %copy-start.2 = (bf16[64,4096]{1,0:T(8,128)(2,1)S(1)}, bf16[64,4096]{1,0:T(8,128)(2,1)}, u32[]{:S(2)}) copy-start(bf16[64,4096]{1,0:T(8,128)(2,1)} %own_hbm.1) | copy-start | bytes 1572868
  1.0 11.1 %copy-start.4 = (f32[2,128,128]{2,1,0:T(8,128)S(1)}, f32[2,128,128]{2,1,0:T(8,128)}, u32[]{:S(2)}) copy-start(f32[2,128,128]{2,1,0:T(8,128)} %inverse_ref.3) | copy-start | bytes 393220
  1.1 11.1 %collective-permute-start = (bf16[64,1024]{1,0:T(8,128)(2,1)S(1)}, bf16[64,1024]{1,0:T(8,128)(2,1)S(1)}, u32[]{:S(2)}, u32[]{:S(2)}) collective-permute-start(bf16[64,1024]{1,0:T(8,128)(2,1)S(1)} %get-tuple-element.20), channel_id=1, source_target_pairs={{0,2},{1,3},{2,0},{3,1},{4,7},{5,6},{6,5},{7,4},{8,10},{9,11},{10,... | collective-permute-start | bytes 393224 | tf_op jit(solution)/shard_map/ppermute | solution.py:166
  5.2 10.6 %collective-permute-start.1 = (bf16[64,2048]{1,0:T(8,128)(2,1)S(1)}, bf16[64,2048]{1,0:T(8,128)(2,1)S(1)}, u32[]{:S(2)}, u32[]{:S(2)}) collective-permute-start(bf16[64,2048]{1,0:T(8,128)(2,1)S(1)} %get-tuple-element.22), channel_id=1, source_target_pairs={{0,1},{1,0},{2,3},{3,2},{4,5},{5,4},{6,7},{7,6},{8,9},{9,8},{10,11... | collective-permute-start | bytes 786440 | tf_op jit(solution)/shard_map/ppermute | solution.py:136
  8.7 25.3 %all-to-all-start = ((f16[4,2,128,256]{3,2,1,0:T(8,128)(2,1)}), f16[4,2,128,256]{3,2,1,0:T(8,128)(2,1)S(1)}, u32[]{:S(2)}, u32[]{:S(2)}) async-start(f16[4,2,128,256]{3,2,1,0:T(8,128)(2,1)} %bitcast), calls=%async_computation | async-start | bytes 1048576 | tf_op jit(solution)/shard_map/all_to_all | solution.py:173
  12.2 10.8 %copy-start.1 = (bf16[256,4096]{1,0:T(8,128)(2,1)S(1)}, bf16[256,4096]{1,0:T(8,128)(2,1)}, u32[]{:S(2)}) copy-start(bf16[256,4096]{1,0:T(8,128)(2,1)} %support_ref.1) | copy-start | bytes 6291460
  12.2 10.8 %copy-start.3 = (bf16[64,4096]{1,0:T(8,128)(2,1)S(1)}, bf16[64,4096]{1,0:T(8,128)(2,1)}, u32[]{:S(2)}) copy-start(bf16[64,4096]{1,0:T(8,128)(2,1)} %own_hbm.1) | copy-start | bytes 1572868
  12.2 6.1 %collective-permute-start.4 = (bf16[64,1024]{1,0:T(8,128)(2,1)S(1)}, bf16[64,1024]{1,0:T(8,128)(2,1)S(1)}, u32[]{:S(2)}, u32[]{:S(2)}) collective-permute-start(bf16[64,1024]{1,0:T(8,128)(2,1)S(1)} %collective-permute-done.refs_2_), channel_id=1, source_target_pairs={{0,8},{4,12},{8,0},{12,4},{16,24},{20,28},{24,16},{28,20},{1,9},{5... | collective-permute-start | bytes 393224 | tf_op jit(solution)/shard_map/ppermute | solution.py:136
  13.8 7.7 %collective-permute-start.6 = (bf16[64,1024]{1,0:T(8,128)(2,1)S(1)}, bf16[64,1024]{1,0:T(8,128)(2,1)S(1)}, u32[]{:S(2)}, u32[]{:S(2)}) collective-permute-start(bf16[64,1024]{1,0:T(8,128)(2,1)S(1)} %collective-permute-done.refs_2_), channel_id=1, source_target_pairs={{0,16},{4,20},{8,24},{12,28},{16,0},{20,4},{24,8},{28,12},{1,17},{... | collective-permute-start | bytes 393224 | tf_op jit(solution)/shard_map/ppermute | solution.py:136
  15.3 6.2 %collective-permute-start.8 = (bf16[64,1024]{1,0:T(8,128)(2,1)S(1)}, bf16[64,1024]{1,0:T(8,128)(2,1)S(1)}, u32[]{:S(2)}, u32[]{:S(2)}) collective-permute-start(bf16[64,1024]{1,0:T(8,128)(2,1)S(1)} %collective-permute-done.refs_2_), channel_id=1, source_target_pairs={{0,24},{4,28},{8,16},{12,20},{16,8},{20,12},{24,0},{28,4},{1,25},{... | collective-permute-start | bytes 393224 | tf_op jit(solution)/shard_map/ppermute | solution.py:136
  15.8 7.2 %collective-permute-start.2 = (bf16[64,2048]{1,0:T(8,128)(2,1)S(1)}, bf16[64,2048]{1,0:T(8,128)(2,1)S(1)}, u32[]{:S(2)}, u32[]{:S(2)}) collective-permute-start(bf16[64,2048]{1,0:T(8,128)(2,1)S(1)} %collective-permute-done.1.refs_0_), channel_id=1, source_target_pairs={{0,4},{4,0},{8,12},{12,8},{16,20},{20,16},{24,28},{28,24},{1,5},{5... | collective-permute-start | bytes 786440 | tf_op jit(solution)/shard_map/ppermute | solution.py:136
  15.8 6.2 %collective-permute-start.3 = (bf16[64,1024]{1,0:T(8,128)(2,1)S(1)}, bf16[64,1024]{1,0:T(8,128)(2,1)S(1)}, u32[]{:S(2)}, u32[]{:S(2)}) collective-permute-start(bf16[64,1024]{1,0:T(8,128)(2,1)S(1)} %collective-permute-done.refs_2_), channel_id=1, source_target_pairs={{0,4},{4,0},{8,12},{12,8},{16,20},{20,16},{24,28},{28,24},{1,5},{5... | collective-permute-start | bytes 393224 | tf_op jit(solution)/shard_map/ppermute | solution.py:136
  18.3 3.7 %collective-permute-start.5 = (bf16[64,1024]{1,0:T(8,128)(2,1)S(1)}, bf16[64,1024]{1,0:T(8,128)(2,1)S(1)}, u32[]{:S(2)}, u32[]{:S(2)}) collective-permute-start(bf16[64,1024]{1,0:T(8,128)(2,1)S(1)} %collective-permute-done.4.refs_4_), channel_id=1, source_target_pairs={{0,4},{4,0},{8,12},{12,8},{16,20},{20,16},{24,28},{28,24},{1,5},{5... | collective-permute-start | bytes 393224 | tf_op jit(solution)/shard_map/ppermute | solution.py:136
  21.5 1.3 %collective-permute-start.7 = (bf16[64,1024]{1,0:T(8,128)(2,1)S(1)}, bf16[64,1024]{1,0:T(8,128)(2,1)S(1)}, u32[]{:S(2)}, u32[]{:S(2)}) collective-permute-start(bf16[64,1024]{1,0:T(8,128)(2,1)S(1)} %collective-permute-done.6.refs_6_), channel_id=1, source_target_pairs={{0,4},{4,0},{8,12},{12,8},{16,20},{20,16},{24,28},{28,24},{1,5},{5... | collective-permute-start | bytes 393224 | tf_op jit(solution)/shard_map/ppermute | solution.py:136
  21.5 1.5 %collective-permute-start.9 = (bf16[64,1024]{1,0:T(8,128)(2,1)S(1)}, bf16[64,1024]{1,0:T(8,128)(2,1)S(1)}, u32[]{:S(2)}, u32[]{:S(2)}) collective-permute-start(bf16[64,1024]{1,0:T(8,128)(2,1)S(1)} %collective-permute-done.8.refs_8_), channel_id=1, source_target_pairs={{0,4},{4,0},{8,12},{12,8},{16,20},{20,16},{24,28},{28,24},{1,5},{5... | collective-permute-start | bytes 393224 | tf_op jit(solution)/shard_map/ppermute | solution.py:136
  24.4 16.8 %copy-start = (f32[2,128,256]{2,1,0:T(8,128)S(1)}, f32[2,128,256]{2,1,0:T(8,128)}, u32[]{:S(2)}) copy-start(f32[2,128,256]{2,1,0:T(8,128)} %own_ref.1) | copy-start | bytes 786436
  24.4 9.6 %collective-permute-start.12 = (f32[64,256]{1,0:T(8,128)S(1)}, f32[64,256]{1,0:T(8,128)S(1)}, u32[]{:S(2)}, u32[]{:S(2)}) collective-permute-start(f32[64,256]{1,0:T(8,128)S(1)} %get-tuple-element.27), channel_id=1, source_target_pairs={{0,2},{1,3},{2,0},{3,1},{4,6},{5,7},{6,4},{7,5},{8,10},{9,11},{10,... | collective-permute-start | bytes 196616 | tf_op jit(solution)/shard_map/ppermute | solution.py:136
  27.2 6.8 %collective-permute-start.13 = (f32[64,256]{1,0:T(8,128)S(1)}, f32[64,256]{1,0:T(8,128)S(1)}, u32[]{:S(2)}, u32[]{:S(2)}) collective-permute-start(f32[64,256]{1,0:T(8,128)S(1)} %get-tuple-element.28), channel_id=1, source_target_pairs={{0,3},{1,2},{2,1},{3,0},{4,7},{5,6},{6,5},{7,4},{8,11},{9,10},{10,... | collective-permute-start | bytes 196616 | tf_op jit(solution)/shard_map/ppermute | solution.py:136
  28.7 4.8 %collective-permute-start.10 = (f32[32,256]{1,0:T(8,128)S(1)}, f32[32,256]{1,0:T(8,128)S(1)}, u32[]{:S(2)}, u32[]{:S(2)}) collective-permute-start(f32[32,256]{1,0:T(8,128)S(1)} %get-tuple-element.25), channel_id=1, source_target_pairs={{0,1},{1,0},{2,3},{3,2},{4,5},{5,4},{6,7},{7,6},{8,9},{9,8},{10,11... | collective-permute-start | bytes 98312 | tf_op jit(solution)/shard_map/ppermute | solution.py:136
  28.7 5.3 %collective-permute-start.11 = (f32[32,256]{1,0:T(8,128)S(1)}, f32[32,256]{1,0:T(8,128)S(1)}, u32[]{:S(2)}, u32[]{:S(2)}) collective-permute-start(f32[32,256]{1,0:T(8,128)S(1)} %get-tuple-element.26), channel_id=1, source_target_pairs={{0,1},{1,0},{2,3},{3,2},{4,5},{5,4},{6,7},{7,6},{8,9},{9,8},{10,11... | collective-permute-start | bytes 98312 | tf_op jit(solution)/shard_map/ppermute | solution.py:136
  34.0 1.3 %collective-permute-start.14 = (f32[64,128]{1,0:T(8,128)S(1)}, f32[64,128]{1,0:T(8,128)S(1)}, u32[]{:S(2)}, u32[]{:S(2)}) collective-permute-start(f32[64,128]{1,0:T(8,128)S(1)} %fusion.1.mine_ref), channel_id=1, source_target_pairs={{0,4},{4,0},{8,12},{12,8},{16,20},{20,16},{24,28},{28,24},{1,5},{5... | collective-permute-start | bytes 98312 | tf_op jit(solution)/shard_map/ppermute | solution.py:136
  35.5 5.2 %collective-permute-start.15 = (f32[64,128]{1,0:T(8,128)S(1)}, f32[64,128]{1,0:T(8,128)S(1)}, u32[]{:S(2)}, u32[]{:S(2)}) collective-permute-start(f32[64,128]{1,0:T(8,128)S(1)} %head_kernel.1), channel_id=1, source_target_pairs={{0,24},{4,28},{8,16},{12,20},{16,8},{20,12},{24,0},{28,4},{1,25},{... | collective-permute-start | bytes 98312 | tf_op jit(solution)/shard_map/ppermute | solution.py:136
  36.2 4.4 %collective-permute-start.16 = (f32[64,128]{1,0:T(8,128)S(1)}, f32[64,128]{1,0:T(8,128)S(1)}, u32[]{:S(2)}, u32[]{:S(2)}) collective-permute-start(f32[64,128]{1,0:T(8,128)S(1)} %head_kernel.1), channel_id=1, source_target_pairs={{0,16},{4,20},{8,24},{12,28},{16,0},{20,4},{24,8},{28,12},{1,17},{... | collective-permute-start | bytes 98312 | tf_op jit(solution)/shard_map/ppermute | solution.py:136
  37.1 3.9 %collective-permute-start.17 = (f32[64,128]{1,0:T(8,128)S(1)}, f32[64,128]{1,0:T(8,128)S(1)}, u32[]{:S(2)}, u32[]{:S(2)}) collective-permute-start(f32[64,128]{1,0:T(8,128)S(1)} %head_kernel.1), channel_id=1, source_target_pairs={{0,8},{4,12},{8,0},{12,4},{16,24},{20,28},{24,16},{28,20},{1,9},{5... | collective-permute-start | bytes 98312 | tf_op jit(solution)/shard_map/ppermute | solution.py:136
  41.1 1.3 %collective-permute-start.18 = (f32[64,128]{1,0:T(8,128)S(1)}, f32[64,128]{1,0:T(8,128)S(1)}, u32[]{:S(2)}, u32[]{:S(2)}) collective-permute-start(f32[64,128]{1,0:T(8,128)S(1)} %select_select_fusion.refs_7_.mine_ref), channel_id=1, source_target_pairs={{0,4},{4,0},{8,12},{12,8},{16,20},{20,16},{24,28},{28,24},{1,5},{5... | collective-permute-start | bytes 98312 | tf_op jit(solution)/shard_map/ppermute | solution.py:136

commit v7 on v6

--- a/solution.py
+++ b/solution.py
@@ -58,38 +58,48 @@
     out_ref[...] = value_ref[0, :8, :128]
 
 
-def tile_kernel(scale, n_row, n_col, own_hbm, support_ref, _, *refs):
-    near, far, refs = refs[:2], refs[2:2 + n_row * (n_col // 2 - 1)], refs[2 + n_row * (n_col // 2 - 1):]
-    outs, (targets_ref, sems) = refs[:n_col + 1], refs[n_col + 1:]
-    rows, features = own_hbm.shape
+def mine_tile_kernel(scale, n_row, own_hbm, support_ref, _, *refs):
+    planes = (len(refs) - 3) // (n_row // 2 + 1)
+    far, outs, (targets_ref, sems) = refs[:-3 - planes], refs[-3 - planes:-2], refs[-2:]
+    rows = own_hbm.shape[0]
+    loads = [(own_hbm, targets_ref.at[pl.ds(0, rows)])] + far_loads(n_row, rows, far, targets_ref, 1)
+    wait_all(start_all(loads, sems))
+    kernel = jnp.exp(scale * dot(targets_ref[...], support_ref[...], NT))
+    for plane, out_ref in enumerate(outs):
+        out_ref[...] = kernel[plane * rows:(plane + 1) * rows]
+
+
+def far_loads(n_row, rows, far, targets_ref, first):
+    chip, width = lax.axis_index("row") // 2, far[0].shape[1]
+    loads = []
+    for i, piece in enumerate(far):
+        plane, step = divmod(i, n_row // 2)
+        cols = pl.ds(pl.multiple_of((chip ^ step) * width, width), width)
+        loads.append((piece, targets_ref.at[pl.ds((first + plane) * rows, rows), cols]))
+    return loads
+
+
+def other_tile_kernel(scale, n_row, support_ref, *refs):
+    planes = (len(refs) - 6) // (n_row // 2 + 1)
+    near, far, refs = refs[:2], refs[2:-4 - planes], refs[-4 - planes:]
+    outs, (targets_ref, sems) = refs[:-2], refs[-2:]
+    rows, half = near[0].shape
     row = lax.axis_index("row")
-    chip, core = row // 2, row % 2
-    half, width = features // 2, 2 * features // n_row
-    steps = []
+    loads = far_loads(n_row, rows, far, targets_ref, 1)
     for part in range(2):
-        side = core ^ part
-        cols = pl.ds(pl.multiple_of(side * half, half), half)
-        loads = [
-            (own_hbm.at[:, cols], targets_ref.at[pl.ds(0, rows), cols]),
-            (near[part], targets_ref.at[pl.ds(rows, rows), cols]),
-        ]
-        steps.append((cols, loads))
-    loads = []
-    for pair in range(n_col // 2 - 1):
-        for step in range(n_row):
-            plane = 2 * pair + 2 + (core ^ (step % 2))
-            cols = pl.ds(pl.multiple_of((chip ^ (step // 2)) * width, width), width)
-            spot = targets_ref.at[pl.ds(pl.multiple_of(plane * rows, rows), rows), cols]
-            loads.append((far[pair * n_row + step], spot))
-    steps[0][1].extend(loads)
-    steps = [(cols, start_all(loads, sems.at[i])) for i, (cols, loads) in enumerate(steps)]
-    total = 0.0
-    for cols, copies in steps:
-        wait_all(copies)
-        total = total + dot(targets_ref[:, cols], support_ref[:, cols], NT)
-    starts = [0, rows, rows + rows // 2, *range(2 * rows, n_col * rows, rows)]
+        cols = pl.ds(pl.multiple_of((row % 2 ^ part) * half, half), half)
+        loads.append((near[part], targets_ref.at[pl.ds(0, rows), cols]))
+    wait_all(start_all(loads, sems))
+    kernel = jnp.exp(scale * dot(targets_ref[...], support_ref[...], NT))
+    starts = [0, rows // 2, *range(rows, targets_ref.shape[0], rows)]
     for start, out_ref in zip(starts, outs):
-        out_ref[...] = jnp.exp(scale * total[start:start + out_ref.shape[0]])
+        out_ref[...] = kernel[start:start + out_ref.shape[0]]
+
+
+def plane_offsets(n_col, core):
+    return [0, 1] + [2 * pair + 2 + core for pair in range(n_col // 2 - 1)] + [
+        2 * pair + 3 - core for pair in range(n_col // 2 - 1)
+    ]
 
 
 def mix_kernel(corner_ref, inverse_ref, out_ref):
@@ -111,8 +121,8 @@
     own_ref, panels_ref, mine_ref, out_ref = refs
     span = own_ref.shape[2]
     row, col = lax.axis_index("row"), lax.axis_index("col")
-    for step in range(n_col):
-        plane = col ^ step
+    for step, offset in enumerate(plane_offsets(n_col, row % 2)):
+        plane = col ^ offset
         block = own_ref if step == 0 else panels_ref.at[plane]
         value = tiles[step] - dot32(mine_ref[...], block[row % 2], NN)
         out_ref[:, pl.ds(pl.multiple_of(plane * span, span), span)] = value
@@ -183,36 +193,49 @@
     )(diag_inverses)
     far, mark = together(far, mark)
     near = [near, exchange(near, "row", n_row, 1)]
-    pieces = []
-    for own in far:
-        for piece in [own] + [exchange(own, "row", n_row, i) for i in range(2, n_row, 2)]:
-            pieces += [piece, exchange(piece, "row", n_row, 1)]
-
-    made = pl.pallas_call(
-        functools.partial(tile_kernel, scale, n_row, n_col),
-        out_shape=[
-            jax.ShapeDtypeStruct((count, span), jnp.float32)
-            for count in [rows, rows // 2, rows // 2] + [rows] * (n_col - 2)
-        ],
-        in_specs=[HBM, VMEM] + [HBM] * (len(pieces) + 3),
-        out_specs=[VMEM] * (n_col + 1),
-        scratch_shapes=[
-            pltpu.VMEM((n_col * rows, features), jnp.bfloat16),
-            pltpu.SemaphoreType.DMA((2, len(pieces) + 3)),
-        ],
-        compiler_params=TILE_PARAMS,
-        cost_estimate=SHORT,
-        name="tile_kernel",
-    )(targets, support, mark, *near, *pieces)
-
-    tiles = [made[0]] + [exchange(made[i], "col", n_col, max(1, i - 1)) for i in range(1, n_col + 1)]
+    mine_far = [
+        piece for own in far for piece in [own] + [exchange(own, "row", n_row, i) for i in range(2, n_row, 2)]
+    ]
+    other_far = [exchange(piece, "row", n_row, 1) for piece in mine_far]
+
+    def tile_call(body, name, counts, *operands):
+        pieces = len(operands) - 1
+        return list(pl.pallas_call(
+            functools.partial(body, scale, n_row),
+            out_shape=[jax.ShapeDtypeStruct((count, span), jnp.float32) for count in counts],
+            in_specs=[VMEM if operand is support else HBM for operand in operands],
+            out_specs=[VMEM] * len(counts),
+            scratch_shapes=[
+                pltpu.VMEM(((1 + len(far)) * rows, features), jnp.bfloat16),
+                pltpu.SemaphoreType.DMA((pieces,)),
+            ],
+            compiler_params=TILE_PARAMS,
+            cost_estimate=SHORT,
+            name=name,
+        )(*operands))
+
+    first = tile_call(
+        mine_tile_kernel, "mine_tile_kernel", [rows] * (1 + len(far)), targets, support, mark, *mine_far
+    )
+    first[0], *other_far = together(first[0], *other_far)
+    last = tile_call(
+        other_tile_kernel, "other_tile_kernel", [rows // 2] * 2 + [rows] * len(far), support, *near, *other_far
+    )
+    made = [first[0], *last[:2], *first[1:], *last[2:]]
+
+    tiles = [made[0]] + [exchange(tile, "col", n_col, 1) for tile in made[1:3]]
+    for i, tile in enumerate(made[3:]):
+        turn, pair = divmod(i, len(far))
+        tiles.append(lax.ppermute(tile, ("row", "col"), [
+            (r * n_col + c, r * n_col + (c ^ (2 * pair + 2 + (r + turn) % 2))) for r in range(n_row) for c in range(n_col)
+        ]))
     tiles, blocks = together(tiles, blocks)
     corner = blocks[0, 0, :, :pivot].astype(jnp.float32) * (1 / PANEL_UNIT)
     heads = [tile[:, :pivot] for tile in tiles]
     heads[1:3] = [jnp.concatenate(heads[1:3], axis=0)]
     head = heads[0]
-    for j in range(1, n_col):
-        head = jnp.where(col == j, heads[j], head)
+    for offset, value in zip(plane_offsets(n_col, row % 2)[1:], heads[1:]):
+        head = jnp.where(col == offset, value, head)
     mix = pl.pallas_call(
         mix_kernel,
         out_shape=jax.ShapeDtypeStruct((pivot, pivot), jnp.float32),

time: 43.5 us -> 43.2 us (level)
  waiting for transfers between devices: 12.8 us -> 11.7 us
  Pallas kernels: 3.44 us -> 4.12 us
    ppermute x0 -> x2, starting transfers between devices: none -> 4.38 us  [shards(): lax.ppermute(tile, ('row', 'col'), [(r * n_col + c, r * n_col + (c ^ 2 *...]
    ppermute x18 -> x16, starting transfers between devices: 16.2 us -> 11.9 us  [exchange(): return lax.ppermute(value, axis, [(i, i ^ mask) for i in range(size)])]
    ppermute x18 -> x16, waiting for transfers between devices: 12.8 us -> 11.3 us  [exchange(): return lax.ppermute(value, axis, [(i, i ^ mask) for i in range(size)])]
    pallas_call x1 -> x2, Pallas kernels: 1.38 us -> 2.06 us  [tile_call(): pl.pallas_call(functools.partial(body, scale, n_row), out_shape=[jax.Shap...]
  transfers between devices with their start and end apart: 20 -> 20, of which waited for: 10 -> 9; matrix products, arithmetic and copies ran while one was open for 5% -> 5% of each run, Pallas kernels for 5% -> 7%
where the time goes in v7:
time: 43.2 us; the launch traced here: 43 us
  starting transfers between devices  23.8 us (55%)
  waiting for transfers between devices  11.7 us (27%)
  Pallas kernels  4.12 us (10%)
  other arithmetic  2.03 us (5%)
  local copies, waits for them, and re-layouts  1.07 us (2%)
    ppermute x16, starting transfers between devices, exchange(): return lax.ppermute(value, axis, [(i, i ^ mask) for i in range(size)])  11.9 us
    ppermute x16, waiting for transfers between devices, exchange(): return lax.ppermute(value, axis, [(i, i ^ mask) for i in range(size)])  11.3 us
    ppermute x2, starting transfers between devices, shards(): lax.ppermute(tile, ('row', 'col'), [(r * n_col + c, r * n_col + (c ^ 2 *...  4.38 us
    ppermute x1, starting transfers between devices, shards(): lax.ppermute(mine, ('row', 'col'), [(r * n_col + c, r * n_col + (c ^ j +...  4.1 us
    all_to_all x1, starting transfers between devices, shards(): blocks = lax.all_to_all(small, 'col', 0, 0)  3.47 us
    pallas_call x2, Pallas kernels, tile_call(): pl.pallas_call(functools.partial(body, scale, n_row), out_shape=[jax.Shap...  2.06 us
    unnamed x10, local copies, waits for them, and re-layouts  1.06 us
    pallas_call x1, Pallas kernels, shards(): pl.pallas_call(functools.partial(other_kernel, n_col, pivot), out_shape=j...  0.98 us
  transfers between devices with their start and end apart: 20, of which 9 were waited for; matrix products, arithmetic and copies ran while one was open for 5% of the time, Pallas kernels for 7%

profile of v7, /device:TPU:0, one launch (start us, length us, event | category | flops | bytes accessed | tf_op | source)
XLA Modules:
  0.0 43.0 jit_solution(8880414407524706093)
XLA Ops:
  0.0 1.0 %copy-done.2 = bf16[64,4096]{1,0:T(8,128)(2,1)S(1)} copy-done((bf16[64,4096]{1,0:T(8,128)(2,1)S(1)}, bf16[64,4096]{1,0:T(8,128)(2,1)}, u32[]{:S(2)}) %copy-start.2) | copy-done | bytes 524312
  1.1 4.1 %collective-permute-start = (bf16[64,1024]{1,0:T(8,128)(2,1)S(1)}, bf16[64,1024]{1,0:T(8,128)(2,1)S(1)}, u32[]{:S(2)}, u32[]{:S(2)}) collective-permute-start(bf16[64,1024]{1,0:T(8,128)(2,1)S(1)} %get-tuple-element.25), channel_id=1, source_target_pairs={{0,2},{1,3},{2,0},{3,1},{4,7},{5,6},{6,5},{7,4},{8,10},{9,11},{10,... | collective-permute-start | bytes 393224 | tf_op jit(solution)/shard_map/ppermute | solution.py:176
  5.2 1.6 %collective-permute-start.8 = (bf16[64,2048]{1,0:T(8,128)(2,1)S(1)}, bf16[64,2048]{1,0:T(8,128)(2,1)S(1)}, u32[]{:S(2)}, u32[]{:S(2)}) collective-permute-start(bf16[64,2048]{1,0:T(8,128)(2,1)S(1)} %get-tuple-element.30), channel_id=1, source_target_pairs={{0,1},{1,0},{2,3},{3,2},{4,5},{5,4},{6,7},{7,6},{8,9},{9,8},{10,11... | collective-permute-start | bytes 786440 | tf_op jit(solution)/shard_map/ppermute | solution.py:146
  6.8 1.0 %multiply_convert_fusion = f16[2,128,256]{2,1,0:T(8,128)(2,1)S(1)} fusion(f32[2,128,256]{2,1,0:T(8,128)} %own_ref.1), kind=kLoop, calls=%fused_computation.2 | loop fusion | flops 131072 | bytes 393216 | tf_op jit(solution)/shard_map/convert
  7.8 0.9 %pad_maximum_fusion = f16[8,128,256]{2,1,0:T(8,128)(2,1)} fusion(f16[2,128,256]{2,1,0:T(8,128)(2,1)S(1)} %multiply_convert_fusion), kind=kLoop, calls=%fused_computation.1 | loop fusion | flops 786432 | bytes 655360 | tf_op jit(solution)/shard_map/concatenate | solution.py:181
  8.7 3.5 %all-to-all-start = ((f16[4,2,128,256]{3,2,1,0:T(8,128)(2,1)}), f16[4,2,128,256]{3,2,1,0:T(8,128)(2,1)S(1)}, u32[]{:S(2)}, u32[]{:S(2)}) async-start(f16[4,2,128,256]{3,2,1,0:T(8,128)(2,1)} %bitcast), calls=%async_computation | async-start | bytes 1048576 | tf_op jit(solution)/shard_map/all_to_all | solution.py:183
  12.2 1.6 %collective-permute-start.1 = (bf16[64,1024]{1,0:T(8,128)(2,1)S(1)}, bf16[64,1024]{1,0:T(8,128)(2,1)S(1)}, u32[]{:S(2)}, u32[]{:S(2)}) collective-permute-start(bf16[64,1024]{1,0:T(8,128)(2,1)S(1)} %collective-permute-done.refs_0_), channel_id=1, source_target_pairs={{0,8},{4,12},{8,0},{12,4},{16,24},{20,28},{24,16},{28,20},{1,9},{5... | collective-permute-start | bytes 393224 | tf_op jit(solution)/shard_map/ppermute | solution.py:146
  13.8 1.5 %collective-permute-start.2 = (bf16[64,1024]{1,0:T(8,128)(2,1)S(1)}, bf16[64,1024]{1,0:T(8,128)(2,1)S(1)}, u32[]{:S(2)}, u32[]{:S(2)}) collective-permute-start(bf16[64,1024]{1,0:T(8,128)(2,1)S(1)} %collective-permute-done.refs_0_), channel_id=1, source_target_pairs={{0,16},{4,20},{8,24},{12,28},{16,0},{20,4},{24,8},{28,12},{1,17},{... | collective-permute-start | bytes 393224 | tf_op jit(solution)/shard_map/ppermute | solution.py:146
  15.3 0.5 %collective-permute-start.3 = (bf16[64,1024]{1,0:T(8,128)(2,1)S(1)}, bf16[64,1024]{1,0:T(8,128)(2,1)S(1)}, u32[]{:S(2)}, u32[]{:S(2)}) collective-permute-start(bf16[64,1024]{1,0:T(8,128)(2,1)S(1)} %collective-permute-done.refs_0_), channel_id=1, source_target_pairs={{0,24},{4,28},{8,16},{12,20},{16,8},{20,12},{24,0},{28,4},{1,25},{... | collective-permute-start | bytes 393224 | tf_op jit(solution)/shard_map/ppermute | solution.py:146
  15.8 0.5 %collective-permute-start.4 = (bf16[64,1024]{1,0:T(8,128)(2,1)S(1)}, bf16[64,1024]{1,0:T(8,128)(2,1)S(1)}, u32[]{:S(2)}, u32[]{:S(2)}) collective-permute-start(bf16[64,1024]{1,0:T(8,128)(2,1)S(1)} %collective-permute-done.refs_0_), channel_id=1, source_target_pairs={{0,4},{4,0},{8,12},{12,8},{16,20},{20,16},{24,28},{28,24},{1,5},{5... | collective-permute-start | bytes 393224 | tf_op jit(solution)/shard_map/ppermute | solution.py:146
  16.3 2.0 %collective-permute-done.1.refs_1_ = bf16[64,1024]{1,0:T(8,128)(2,1)S(1)} collective-permute-done((bf16[64,1024]{1,0:T(8,128)(2,1)S(1)}, bf16[64,1024]{1,0:T(8,128)(2,1)S(1)}, u32[]{:S(2)}, u32[]{:S(2)}) %collective-permute-start.1) | collective-permute-done | bytes 131104 | tf_op jit(solution)/shard_map/ppermute | solution.py:146
  18.3 3.1 %collective-permute-done.2.refs_2_ = bf16[64,1024]{1,0:T(8,128)(2,1)S(1)} collective-permute-done((bf16[64,1024]{1,0:T(8,128)(2,1)S(1)}, bf16[64,1024]{1,0:T(8,128)(2,1)S(1)}, u32[]{:S(2)}, u32[]{:S(2)}) %collective-permute-start.2) | collective-permute-done | bytes 131104 | tf_op jit(solution)/shard_map/ppermute | solution.py:146
  21.5 0.5 %collective-permute-start.7 = (bf16[64,1024]{1,0:T(8,128)(2,1)S(1)}, bf16[64,1024]{1,0:T(8,128)(2,1)S(1)}, u32[]{:S(2)}, u32[]{:S(2)}) collective-permute-start(bf16[64,1024]{1,0:T(8,128)(2,1)S(1)} %collective-permute-done.3.refs_3_), channel_id=1, source_target_pairs={{0,4},{4,0},{8,12},{12,8},{16,20},{20,16},{24,28},{28,24},{1,5},{5... | collective-permute-start | bytes 393224 | tf_op jit(solution)/shard_map/ppermute | solution.py:146
  22.0 1.0 %mine_tile_kernel.1 = (f32[64,256]{1,0:T(8,128)S(1)}, f32[64,256]{1,0:T(8,128)S(1)}) custom-call(bf16[64,4096]{1,0:T(8,128)(2,1)S(1)} %copy-done.3, bf16[256,4096]{1,0:T(8,128)(2,1)S(1)} %copy-done, f32[8,128]{1,0:T(8,128)S(1)} %mark_kernel.1._, bf16[64,1024]{1,0:T(8,128)(2,1)S(1)} %collective-permute-done.refs_0_, ...), custom_call_target="tpu_custom_call" | custom-call | flops 1000000 | tf_op jit(solution)/shard_map/mine_tile_kernel/pallas_call | solution.py:203
  23.0 2.8 %collective-permute-start.12 = (f32[64,256]{1,0:T(8,128)S(1)}, f32[64,256]{1,0:T(8,128)S(1)}, u32[]{:S(2)}, u32[]{:S(2)}) collective-permute-start(f32[64,256]{1,0:T(8,128)S(1)} %get-tuple-element.37), channel_id=1, source_target_pairs={{0,2},{1,3},{2,0},{3,1},{4,7},{5,6},{6,5},{7,4},{8,10},{9,11},{10,... | collective-permute-start | bytes 196616 | tf_op jit(solution)/shard_map/ppermute | solution.py:229
  25.9 1.0 %other_tile_kernel.1 = (f32[32,256]{1,0:T(8,128)S(1)}, f32[32,256]{1,0:T(8,128)S(1)}, f32[64,256]{1,0:T(8,128)S(1)}) custom-call(bf16[256,4096]{1,0:T(8,128)(2,1)S(1)} %copy-done, bf16[64,2048]{1,0:T(8,128)(2,1)S(1)} %collective-permute-done.8.refs_0_, bf16[64,2048]{1,0:T(8,128)(2,1)S(1)} %collective-permute-done.9.refs_1_, ...), custom_call_target="tpu_custom_call" | custom-call | flops 1000000 | tf_op jit(solution)/shard_map/other_tile_kernel/pallas_call | solution.py:203
  26.9 1.6 %collective-permute-start.13 = (f32[64,256]{1,0:T(8,128)S(1)}, f32[64,256]{1,0:T(8,128)S(1)}, u32[]{:S(2)}, u32[]{:S(2)}) collective-permute-start(f32[64,256]{1,0:T(8,128)S(1)} %get-tuple-element.38), channel_id=1, source_target_pairs={{0,3},{1,2},{2,1},{3,0},{4,6},{5,7},{6,4},{7,5},{8,11},{9,10},{10,... | collective-permute-start | bytes 196616 | tf_op jit(solution)/shard_map/ppermute | solution.py:229
  28.5 2.0 %collective-permute-start.11 = (f32[32,256]{1,0:T(8,128)S(1)}, f32[32,256]{1,0:T(8,128)S(1)}, u32[]{:S(2)}, u32[]{:S(2)}) collective-permute-start(f32[32,256]{1,0:T(8,128)S(1)} %get-tuple-element.36), channel_id=1, source_target_pairs={{0,1},{1,0},{2,3},{3,2},{4,5},{5,4},{6,7},{7,6},{8,9},{9,8},{10,11... | collective-permute-start | bytes 98312 | tf_op jit(solution)/shard_map/ppermute | solution.py:146
  30.5 2.1 %collective-permute-done.10.refs_1_ = f32[32,256]{1,0:T(8,128)S(1)} collective-permute-done((f32[32,256]{1,0:T(8,128)S(1)}, f32[32,256]{1,0:T(8,128)S(1)}, u32[]{:S(2)}, u32[]{:S(2)}) %collective-permute-start.10) | collective-permute-done | bytes 32800 | tf_op jit(solution)/shard_map/ppermute | solution.py:146
  32.6 0.7 %collective-permute-done.11.refs_2_ = f32[32,256]{1,0:T(8,128)S(1)} collective-permute-done((f32[32,256]{1,0:T(8,128)S(1)}, f32[32,256]{1,0:T(8,128)S(1)}, u32[]{:S(2)}, u32[]{:S(2)}) %collective-permute-start.11) | collective-permute-done | bytes 32800 | tf_op jit(solution)/shard_map/ppermute | solution.py:146
  33.3 0.4 collective-permute-done.13.refs_4_
  33.9 0.2 base_kernel.1.base_ref
  34.0 0.4 mix_kernel.1.mix_ref
  34.5 0.6 %collective-permute-done.14.other_ref = f32[64,128]{1,0:T(8,128)S(1)} collective-permute-done((f32[64,128]{1,0:T(8,128)S(1)}, f32[64,128]{1,0:T(8,128)S(1)}, u32[]{:S(2)}, u32[]{:S(2)}) %collective-permute-start.14) | collective-permute-done | bytes 32800 | tf_op jit(solution)/shard_map/ppermute | solution.py:146
  35.2 0.7 %collective-permute-start.15 = (f32[64,128]{1,0:T(8,128)S(1)}, f32[64,128]{1,0:T(8,128)S(1)}, u32[]{:S(2)}, u32[]{:S(2)}) collective-permute-start(f32[64,128]{1,0:T(8,128)S(1)} %head_kernel.1), channel_id=1, source_target_pairs={{0,24},{4,28},{8,16},{12,20},{16,8},{20,12},{24,0},{28,4},{1,25},{... | collective-permute-start | bytes 98312 | tf_op jit(solution)/shard_map/ppermute | solution.py:146
  35.9 0.9 %collective-permute-start.16 = (f32[64,128]{1,0:T(8,128)S(1)}, f32[64,128]{1,0:T(8,128)S(1)}, u32[]{:S(2)}, u32[]{:S(2)}) collective-permute-start(f32[64,128]{1,0:T(8,128)S(1)} %head_kernel.1), channel_id=1, source_target_pairs={{0,16},{4,20},{8,24},{12,28},{16,0},{20,4},{24,8},{28,12},{1,17},{... | collective-permute-start | bytes 98312 | tf_op jit(solution)/shard_map/ppermute | solution.py:146
  36.8 1.9 %collective-permute-start.17 = (f32[64,128]{1,0:T(8,128)S(1)}, f32[64,128]{1,0:T(8,128)S(1)}, u32[]{:S(2)}, u32[]{:S(2)}) collective-permute-start(f32[64,128]{1,0:T(8,128)S(1)} %head_kernel.1), channel_id=1, source_target_pairs={{0,8},{4,12},{8,0},{12,4},{16,24},{20,28},{24,16},{28,20},{1,9},{5... | collective-permute-start | bytes 98312 | tf_op jit(solution)/shard_map/ppermute | solution.py:146
  38.7 1.6 %collective-permute-done.15 = f32[64,128]{1,0:T(8,128)S(1)} collective-permute-done((f32[64,128]{1,0:T(8,128)S(1)}, f32[64,128]{1,0:T(8,128)S(1)}, u32[]{:S(2)}, u32[]{:S(2)}) %collective-permute-start.15) | collective-permute-done | bytes 32800 | tf_op jit(solution)/shard_map/ppermute | solution.py:146
  40.4 0.4 collective-permute-done.17
  40.9 0.3 mine_kernel.1.part_ref
  41.2 0.8 %collective-permute-done.18.other_ref = f32[64,128]{1,0:T(8,128)S(1)} collective-permute-done((f32[64,128]{1,0:T(8,128)S(1)}, f32[64,128]{1,0:T(8,128)S(1)}, u32[]{:S(2)}, u32[]{:S(2)}) %collective-permute-start.18) | collective-permute-done | bytes 32800 | tf_op jit(solution)/shard_map/ppermute | solution.py:146
  42.0 1.0 %other_kernel.1 = f32[64,1024]{1,0:T(8,128)} custom-call(f32[64,1024]{1,0:T(8,128)S(1)} %mine_kernel.1.part_ref, f32[2,128,256]{2,1,0:T(8,128)S(1)} %copy-done.1, f32[4,2,128,256]{3,2,1,0:T(8,128)S(1)} %convert_multiply_fusion.refs_6_.panels_ref, f32[64,128]{1,0:T(8,128)S(1)} %select_select_fusion.refs_7_.mine_ref, ...), custom_call_target="tpu_custom_call" | custom-call | flops 1000000 | tf_op jit(solution)/shard_map/other_kernel/pallas_call | solution.py:281
  (35 shorter events, 0.6 us)
Async XLA Ops:
  0.0 1.0 %copy-start.2 = (bf16[64,4096]{1,0:T(8,128)(2,1)S(1)}, bf16[64,4096]{1,0:T(8,128)(2,1)}, u32[]{:S(2)}) copy-start(bf16[64,4096]{1,0:T(8,128)(2,1)} %own_hbm.1) | copy-start | bytes 1572868
  1.0 11.1 %copy-start.4 = (f32[2,128,128]{2,1,0:T(8,128)S(1)}, f32[2,128,128]{2,1,0:T(8,128)}, u32[]{:S(2)}) copy-start(f32[2,128,128]{2,1,0:T(8,128)} %inverse_ref.3) | copy-start | bytes 393220
  1.1 11.1 %collective-permute-start = (bf16[64,1024]{1,0:T(8,128)(2,1)S(1)}, bf16[64,1024]{1,0:T(8,128)(2,1)S(1)}, u32[]{:S(2)}, u32[]{:S(2)}) collective-permute-start(bf16[64,1024]{1,0:T(8,128)(2,1)S(1)} %get-tuple-element.25), channel_id=1, source_target_pairs={{0,2},{1,3},{2,0},{3,1},{4,7},{5,6},{6,5},{7,4},{8,10},{9,11},{10,... | collective-permute-start | bytes 393224 | tf_op jit(solution)/shard_map/ppermute | solution.py:176
  5.2 10.6 %collective-permute-start.8 = (bf16[64,2048]{1,0:T(8,128)(2,1)S(1)}, bf16[64,2048]{1,0:T(8,128)(2,1)S(1)}, u32[]{:S(2)}, u32[]{:S(2)}) collective-permute-start(bf16[64,2048]{1,0:T(8,128)(2,1)S(1)} %get-tuple-element.30), channel_id=1, source_target_pairs={{0,1},{1,0},{2,3},{3,2},{4,5},{5,4},{6,7},{7,6},{8,9},{9,8},{10,11... | collective-permute-start | bytes 786440 | tf_op jit(solution)/shard_map/ppermute | solution.py:146
  8.7 25.0 %all-to-all-start = ((f16[4,2,128,256]{3,2,1,0:T(8,128)(2,1)}), f16[4,2,128,256]{3,2,1,0:T(8,128)(2,1)S(1)}, u32[]{:S(2)}, u32[]{:S(2)}) async-start(f16[4,2,128,256]{3,2,1,0:T(8,128)(2,1)} %bitcast), calls=%async_computation | async-start | bytes 1048576 | tf_op jit(solution)/shard_map/all_to_all | solution.py:183
  12.2 9.8 %copy-start = (bf16[256,4096]{1,0:T(8,128)(2,1)S(1)}, bf16[256,4096]{1,0:T(8,128)(2,1)}, u32[]{:S(2)}) copy-start(bf16[256,4096]{1,0:T(8,128)(2,1)} %support_ref.3) | copy-start | bytes 6291460
  12.2 9.8 %copy-start.3 = (bf16[64,4096]{1,0:T(8,128)(2,1)S(1)}, bf16[64,4096]{1,0:T(8,128)(2,1)}, u32[]{:S(2)}) copy-start(bf16[64,4096]{1,0:T(8,128)(2,1)} %own_hbm.1) | copy-start | bytes 1572868
  12.2 6.1 %collective-permute-start.1 = (bf16[64,1024]{1,0:T(8,128)(2,1)S(1)}, bf16[64,1024]{1,0:T(8,128)(2,1)S(1)}, u32[]{:S(2)}, u32[]{:S(2)}) collective-permute-start(bf16[64,1024]{1,0:T(8,128)(2,1)S(1)} %collective-permute-done.refs_0_), channel_id=1, source_target_pairs={{0,8},{4,12},{8,0},{12,4},{16,24},{20,28},{24,16},{28,20},{1,9},{5... | collective-permute-start | bytes 393224 | tf_op jit(solution)/shard_map/ppermute | solution.py:146
  13.8 7.7 %collective-permute-start.2 = (bf16[64,1024]{1,0:T(8,128)(2,1)S(1)}, bf16[64,1024]{1,0:T(8,128)(2,1)S(1)}, u32[]{:S(2)}, u32[]{:S(2)}) collective-permute-start(bf16[64,1024]{1,0:T(8,128)(2,1)S(1)} %collective-permute-done.refs_0_), channel_id=1, source_target_pairs={{0,16},{4,20},{8,24},{12,28},{16,0},{20,4},{24,8},{28,12},{1,17},{... | collective-permute-start | bytes 393224 | tf_op jit(solution)/shard_map/ppermute | solution.py:146
  15.3 6.2 %collective-permute-start.3 = (bf16[64,1024]{1,0:T(8,128)(2,1)S(1)}, bf16[64,1024]{1,0:T(8,128)(2,1)S(1)}, u32[]{:S(2)}, u32[]{:S(2)}) collective-permute-start(bf16[64,1024]{1,0:T(8,128)(2,1)S(1)} %collective-permute-done.refs_0_), channel_id=1, source_target_pairs={{0,24},{4,28},{8,16},{12,20},{16,8},{20,12},{24,0},{28,4},{1,25},{... | collective-permute-start | bytes 393224 | tf_op jit(solution)/shard_map/ppermute | solution.py:146
  15.8 10.1 %collective-permute-start.9 = (bf16[64,2048]{1,0:T(8,128)(2,1)S(1)}, bf16[64,2048]{1,0:T(8,128)(2,1)S(1)}, u32[]{:S(2)}, u32[]{:S(2)}) collective-permute-start(bf16[64,2048]{1,0:T(8,128)(2,1)S(1)} %collective-permute-done.8.refs_0_), channel_id=1, source_target_pairs={{0,4},{4,0},{8,12},{12,8},{16,20},{20,16},{24,28},{28,24},{1,5},{5... | collective-permute-start | bytes 786440 | tf_op jit(solution)/shard_map/ppermute | solution.py:146
  15.8 7.2 %collective-permute-start.4 = (bf16[64,1024]{1,0:T(8,128)(2,1)S(1)}, bf16[64,1024]{1,0:T(8,128)(2,1)S(1)}, u32[]{:S(2)}, u32[]{:S(2)}) collective-permute-start(bf16[64,1024]{1,0:T(8,128)(2,1)S(1)} %collective-permute-done.refs_0_), channel_id=1, source_target_pairs={{0,4},{4,0},{8,12},{12,8},{16,20},{20,16},{24,28},{28,24},{1,5},{5... | collective-permute-start | bytes 393224 | tf_op jit(solution)/shard_map/ppermute | solution.py:146
  18.3 7.5 %collective-permute-start.5 = (bf16[64,1024]{1,0:T(8,128)(2,1)S(1)}, bf16[64,1024]{1,0:T(8,128)(2,1)S(1)}, u32[]{:S(2)}, u32[]{:S(2)}) collective-permute-start(bf16[64,1024]{1,0:T(8,128)(2,1)S(1)} %collective-permute-done.1.refs_1_), channel_id=1, source_target_pairs={{0,4},{4,0},{8,12},{12,8},{16,20},{20,16},{24,28},{28,24},{1,5},{5... | collective-permute-start | bytes 393224 | tf_op jit(solution)/shard_map/ppermute | solution.py:146
  21.5 4.4 %collective-permute-start.6 = (bf16[64,1024]{1,0:T(8,128)(2,1)S(1)}, bf16[64,1024]{1,0:T(8,128)(2,1)S(1)}, u32[]{:S(2)}, u32[]{:S(2)}) collective-permute-start(bf16[64,1024]{1,0:T(8,128)(2,1)S(1)} %collective-permute-done.2.refs_2_), channel_id=1, source_target_pairs={{0,4},{4,0},{8,12},{12,8},{16,20},{20,16},{24,28},{28,24},{1,5},{5... | collective-permute-start | bytes 393224 | tf_op jit(solution)/shard_map/ppermute | solution.py:146
  21.5 4.4 %collective-permute-start.7 = (bf16[64,1024]{1,0:T(8,128)(2,1)S(1)}, bf16[64,1024]{1,0:T(8,128)(2,1)S(1)}, u32[]{:S(2)}, u32[]{:S(2)}) collective-permute-start(bf16[64,1024]{1,0:T(8,128)(2,1)S(1)} %collective-permute-done.3.refs_3_), channel_id=1, source_target_pairs={{0,4},{4,0},{8,12},{12,8},{16,20},{20,16},{24,28},{28,24},{1,5},{5... | collective-permute-start | bytes 393224 | tf_op jit(solution)/shard_map/ppermute | solution.py:146
  23.0 7.5 %collective-permute-start.12 = (f32[64,256]{1,0:T(8,128)S(1)}, f32[64,256]{1,0:T(8,128)S(1)}, u32[]{:S(2)}, u32[]{:S(2)}) collective-permute-start(f32[64,256]{1,0:T(8,128)S(1)} %get-tuple-element.37), channel_id=1, source_target_pairs={{0,2},{1,3},{2,0},{3,1},{4,7},{5,6},{6,5},{7,4},{8,10},{9,11},{10,... | collective-permute-start | bytes 196616 | tf_op jit(solution)/shard_map/ppermute | solution.py:229
  26.9 14.0 %copy-start.1 = (f32[2,128,256]{2,1,0:T(8,128)S(1)}, f32[2,128,256]{2,1,0:T(8,128)}, u32[]{:S(2)}) copy-start(f32[2,128,256]{2,1,0:T(8,128)} %own_ref.1) | copy-start | bytes 786436
  26.9 6.8 %collective-permute-start.13 = (f32[64,256]{1,0:T(8,128)S(1)}, f32[64,256]{1,0:T(8,128)S(1)}, u32[]{:S(2)}, u32[]{:S(2)}) collective-permute-start(f32[64,256]{1,0:T(8,128)S(1)} %get-tuple-element.38), channel_id=1, source_target_pairs={{0,3},{1,2},{2,1},{3,0},{4,6},{5,7},{6,4},{7,5},{8,11},{9,10},{10,... | collective-permute-start | bytes 196616 | tf_op jit(solution)/shard_map/ppermute | solution.py:229
  28.5 4.1 %collective-permute-start.10 = (f32[32,256]{1,0:T(8,128)S(1)}, f32[32,256]{1,0:T(8,128)S(1)}, u32[]{:S(2)}, u32[]{:S(2)}) collective-permute-start(f32[32,256]{1,0:T(8,128)S(1)} %get-tuple-element.35), channel_id=1, source_target_pairs={{0,1},{1,0},{2,3},{3,2},{4,5},{5,4},{6,7},{7,6},{8,9},{9,8},{10,11... | collective-permute-start | bytes 98312 | tf_op jit(solution)/shard_map/ppermute | solution.py:146
  28.5 4.8 %collective-permute-start.11 = (f32[32,256]{1,0:T(8,128)S(1)}, f32[32,256]{1,0:T(8,128)S(1)}, u32[]{:S(2)}, u32[]{:S(2)}) collective-permute-start(f32[32,256]{1,0:T(8,128)S(1)} %get-tuple-element.36), channel_id=1, source_target_pairs={{0,1},{1,0},{2,3},{3,2},{4,5},{5,4},{6,7},{7,6},{8,9},{9,8},{10,11... | collective-permute-start | bytes 98312 | tf_op jit(solution)/shard_map/ppermute | solution.py:146
  33.8 1.3 %collective-permute-start.14 = (f32[64,128]{1,0:T(8,128)S(1)}, f32[64,128]{1,0:T(8,128)S(1)}, u32[]{:S(2)}, u32[]{:S(2)}) collective-permute-start(f32[64,128]{1,0:T(8,128)S(1)} %fusion.1.mine_ref), channel_id=1, source_target_pairs={{0,4},{4,0},{8,12},{12,8},{16,20},{20,16},{24,28},{28,24},{1,5},{5... | collective-permute-start | bytes 98312 | tf_op jit(solution)/shard_map/ppermute | solution.py:146
  35.2 5.2 %collective-permute-start.15 = (f32[64,128]{1,0:T(8,128)S(1)}, f32[64,128]{1,0:T(8,128)S(1)}, u32[]{:S(2)}, u32[]{:S(2)}) collective-permute-start(f32[64,128]{1,0:T(8,128)S(1)} %head_kernel.1), channel_id=1, source_target_pairs={{0,24},{4,28},{8,16},{12,20},{16,8},{20,12},{24,0},{28,4},{1,25},{... | collective-permute-start | bytes 98312 | tf_op jit(solution)/shard_map/ppermute | solution.py:146
  35.9 4.5 %collective-permute-start.16 = (f32[64,128]{1,0:T(8,128)S(1)}, f32[64,128]{1,0:T(8,128)S(1)}, u32[]{:S(2)}, u32[]{:S(2)}) collective-permute-start(f32[64,128]{1,0:T(8,128)S(1)} %head_kernel.1), channel_id=1, source_target_pairs={{0,16},{4,20},{8,24},{12,28},{16,0},{20,4},{24,8},{28,12},{1,17},{... | collective-permute-start | bytes 98312 | tf_op jit(solution)/shard_map/ppermute | solution.py:146
  36.8 3.9 %collective-permute-start.17 = (f32[64,128]{1,0:T(8,128)S(1)}, f32[64,128]{1,0:T(8,128)S(1)}, u32[]{:S(2)}, u32[]{:S(2)}) collective-permute-start(f32[64,128]{1,0:T(8,128)S(1)} %head_kernel.1), channel_id=1, source_target_pairs={{0,8},{4,12},{8,0},{12,4},{16,24},{20,28},{24,16},{28,20},{1,9},{5... | collective-permute-start | bytes 98312 | tf_op jit(solution)/shard_map/ppermute | solution.py:146
  40.7 1.3 %collective-permute-start.18 = (f32[64,128]{1,0:T(8,128)S(1)}, f32[64,128]{1,0:T(8,128)S(1)}, u32[]{:S(2)}, u32[]{:S(2)}) collective-permute-start(f32[64,128]{1,0:T(8,128)S(1)} %select_select_fusion.refs_7_.mine_ref), channel_id=1, source_target_pairs={{0,4},{4,0},{8,12},{12,8},{16,20},{20,16},{24,28},{28,24},{1,5},{5... | collective-permute-start | bytes 98312 | tf_op jit(solution)/shard_map/ppermute | solution.py:146

commit v8 on v7

--- a/solution.py
+++ b/solution.py
@@ -32,6 +32,11 @@
 def dot32(a, b, dims):
     (a_high, a_low), (b_high, b_low) = halves(a), halves(b)
     return dot(a_high, b_high, dims) + (dot(a_low, b_high, dims) + dot(a_high, b_low, dims))
+
+
+def chip_offset(step, core):
+    swapped = {1: 2, 2: 1}.get(step, step)
+    return step + core * (swapped - step)
 
 
 def start_all(pairs, sems):
@@ -144,6 +149,12 @@
 
 def exchange(value, axis, size, mask):
     return lax.ppermute(value, axis, [(i, i ^ mask) for i in range(size)])
+
+
+def exchange_chips(value, n_row, n_col, step):
+    return lax.ppermute(value, ("row", "col"), [
+        (r * n_col + c, (r ^ (2 * chip_offset(step, r % 2))) * n_col + c) for r in range(n_row) for c in range(n_col)
+    ])
 
 
 def together(*values):
@@ -264,8 +275,9 @@
         name="head_kernel",
     )(base, exchange(head, "row", n_row, 1), mix)
     spread = head
-    for i in range(2, n_row, 2):
-        spread = jnp.where(row // 2 == i // 2, exchange(head, "row", n_row, i), spread)
+    for step in range(1, n_row // 2):
+        moved = exchange_chips(head, n_row, n_col, step)
+        spread = jnp.where(row // 2 == chip_offset(step, row % 2), moved, spread)
     swapped = exchange(spread, "row", n_row, 1)
     blocks = blocks.astype(jnp.float32) * (1 / PANEL_UNIT)
 

time: 43.2 us -> 43.2 us (level)
    ppermute x0 -> x3, starting transfers between devices: none -> 3.55 us  [exchange_chips(): lax.ppermute(value, ('row', 'col'), [(r * n_col + c, (r ^ 2 * chip_offset...]
    ppermute x16 -> x13, starting transfers between devices: 11.9 us -> 8.32 us  [exchange(): return lax.ppermute(value, axis, [(i, i ^ mask) for i in range(size)])]
    ppermute x0 -> x3, waiting for transfers between devices: none -> 1.96 us  [exchange_chips(): lax.ppermute(value, ('row', 'col'), [(r * n_col + c, (r ^ 2 * chip_offset...]
    ppermute x16 -> x13, waiting for transfers between devices: 11.3 us -> 9.34 us  [exchange(): return lax.ppermute(value, axis, [(i, i ^ mask) for i in range(size)])]
where the time goes in v8:
time: 43.2 us; the launch traced here: 43 us
  starting transfers between devices  23.8 us (55%)
  waiting for transfers between devices  11.7 us (27%)
  Pallas kernels  4.12 us (10%)
  other arithmetic  2.03 us (5%)
  local copies, waits for them, and re-layouts  1.07 us (2%)
    ppermute x13, waiting for transfers between devices, exchange(): return lax.ppermute(value, axis, [(i, i ^ mask) for i in range(size)])  9.34 us
    ppermute x13, starting transfers between devices, exchange(): return lax.ppermute(value, axis, [(i, i ^ mask) for i in range(size)])  8.32 us
    ppermute x2, starting transfers between devices, shards(): lax.ppermute(tile, ('row', 'col'), [(r * n_col + c, r * n_col + (c ^ 2 *...  4.38 us
    ppermute x1, starting transfers between devices, shards(): lax.ppermute(mine, ('row', 'col'), [(r * n_col + c, r * n_col + (c ^ j +...  4.1 us
    ppermute x3, starting transfers between devices, exchange_chips(): lax.ppermute(value, ('row', 'col'), [(r * n_col + c, (r ^ 2 * chip_offset...  3.55 us
    all_to_all x1, starting transfers between devices, shards(): blocks = lax.all_to_all(small, 'col', 0, 0)  3.47 us
    pallas_call x2, Pallas kernels, tile_call(): pl.pallas_call(functools.partial(body, scale, n_row), out_shape=[jax.Shap...  2.06 us
    ppermute x3, waiting for transfers between devices, exchange_chips(): lax.ppermute(value, ('row', 'col'), [(r * n_col + c, (r ^ 2 * chip_offset...  1.96 us
  transfers between devices with their start and end apart: 20, of which 9 were waited for; matrix products, arithmetic and copies ran while one was open for 5% of the time, Pallas kernels for 7%

profile of v8, /device:TPU:0, one launch (start us, length us, event | category | flops | bytes accessed | tf_op | source)
XLA Modules:
  0.0 43.0 jit_solution(9543621130069092423)
XLA Ops:
  0.0 1.0 %copy-done.2 = bf16[64,4096]{1,0:T(8,128)(2,1)S(1)} copy-done((bf16[64,4096]{1,0:T(8,128)(2,1)S(1)}, bf16[64,4096]{1,0:T(8,128)(2,1)}, u32[]{:S(2)}) %copy-start.2) | copy-done | bytes 524312
  1.1 4.1 %collective-permute-start = (bf16[64,1024]{1,0:T(8,128)(2,1)S(1)}, bf16[64,1024]{1,0:T(8,128)(2,1)S(1)}, u32[]{:S(2)}, u32[]{:S(2)}) collective-permute-start(bf16[64,1024]{1,0:T(8,128)(2,1)S(1)} %get-tuple-element.25), channel_id=1, source_target_pairs={{0,2},{1,3},{2,0},{3,1},{4,7},{5,6},{6,5},{7,4},{8,10},{9,11},{10,... | collective-permute-start | bytes 393224 | tf_op jit(solution)/shard_map/ppermute | solution.py:187
  5.2 1.6 %collective-permute-start.8 = (bf16[64,2048]{1,0:T(8,128)(2,1)S(1)}, bf16[64,2048]{1,0:T(8,128)(2,1)S(1)}, u32[]{:S(2)}, u32[]{:S(2)}) collective-permute-start(bf16[64,2048]{1,0:T(8,128)(2,1)S(1)} %get-tuple-element.30), channel_id=1, source_target_pairs={{0,1},{1,0},{2,3},{3,2},{4,5},{5,4},{6,7},{7,6},{8,9},{9,8},{10,11... | collective-permute-start | bytes 786440 | tf_op jit(solution)/shard_map/ppermute | solution.py:151
  6.8 1.0 %multiply_convert_fusion = f16[2,128,256]{2,1,0:T(8,128)(2,1)S(1)} fusion(f32[2,128,256]{2,1,0:T(8,128)} %own_ref.1), kind=kLoop, calls=%fused_computation.2 | loop fusion | flops 131072 | bytes 393216 | tf_op jit(solution)/shard_map/convert
  7.8 0.9 %pad_maximum_fusion = f16[8,128,256]{2,1,0:T(8,128)(2,1)} fusion(f16[2,128,256]{2,1,0:T(8,128)(2,1)S(1)} %multiply_convert_fusion), kind=kLoop, calls=%fused_computation.1 | loop fusion | flops 786432 | bytes 655360 | tf_op jit(solution)/shard_map/concatenate | solution.py:192
  8.7 3.5 %all-to-all-start = ((f16[4,2,128,256]{3,2,1,0:T(8,128)(2,1)}), f16[4,2,128,256]{3,2,1,0:T(8,128)(2,1)S(1)}, u32[]{:S(2)}, u32[]{:S(2)}) async-start(f16[4,2,128,256]{3,2,1,0:T(8,128)(2,1)} %bitcast), calls=%async_computation | async-start | bytes 1048576 | tf_op jit(solution)/shard_map/all_to_all | solution.py:194
  12.2 1.6 %collective-permute-start.1 = (bf16[64,1024]{1,0:T(8,128)(2,1)S(1)}, bf16[64,1024]{1,0:T(8,128)(2,1)S(1)}, u32[]{:S(2)}, u32[]{:S(2)}) collective-permute-start(bf16[64,1024]{1,0:T(8,128)(2,1)S(1)} %collective-permute-done.refs_0_), channel_id=1, source_target_pairs={{0,8},{4,12},{8,0},{12,4},{16,24},{20,28},{24,16},{28,20},{1,9},{5... | collective-permute-start | bytes 393224 | tf_op jit(solution)/shard_map/ppermute | solution.py:151
  13.8 1.5 %collective-permute-start.2 = (bf16[64,1024]{1,0:T(8,128)(2,1)S(1)}, bf16[64,1024]{1,0:T(8,128)(2,1)S(1)}, u32[]{:S(2)}, u32[]{:S(2)}) collective-permute-start(bf16[64,1024]{1,0:T(8,128)(2,1)S(1)} %collective-permute-done.refs_0_), channel_id=1, source_target_pairs={{0,16},{4,20},{8,24},{12,28},{16,0},{20,4},{24,8},{28,12},{1,17},{... | collective-permute-start | bytes 393224 | tf_op jit(solution)/shard_map/ppermute | solution.py:151
  15.3 0.5 %collective-permute-start.3 = (bf16[64,1024]{1,0:T(8,128)(2,1)S(1)}, bf16[64,1024]{1,0:T(8,128)(2,1)S(1)}, u32[]{:S(2)}, u32[]{:S(2)}) collective-permute-start(bf16[64,1024]{1,0:T(8,128)(2,1)S(1)} %collective-permute-done.refs_0_), channel_id=1, source_target_pairs={{0,24},{4,28},{8,16},{12,20},{16,8},{20,12},{24,0},{28,4},{1,25},{... | collective-permute-start | bytes 393224 | tf_op jit(solution)/shard_map/ppermute | solution.py:151
  15.8 0.5 %collective-permute-start.4 = (bf16[64,1024]{1,0:T(8,128)(2,1)S(1)}, bf16[64,1024]{1,0:T(8,128)(2,1)S(1)}, u32[]{:S(2)}, u32[]{:S(2)}) collective-permute-start(bf16[64,1024]{1,0:T(8,128)(2,1)S(1)} %collective-permute-done.refs_0_), channel_id=1, source_target_pairs={{0,4},{4,0},{8,12},{12,8},{16,20},{20,16},{24,28},{28,24},{1,5},{5... | collective-permute-start | bytes 393224 | tf_op jit(solution)/shard_map/ppermute | solution.py:151
  16.3 2.0 %collective-permute-done.1.refs_1_ = bf16[64,1024]{1,0:T(8,128)(2,1)S(1)} collective-permute-done((bf16[64,1024]{1,0:T(8,128)(2,1)S(1)}, bf16[64,1024]{1,0:T(8,128)(2,1)S(1)}, u32[]{:S(2)}, u32[]{:S(2)}) %collective-permute-start.1) | collective-permute-done | bytes 131104 | tf_op jit(solution)/shard_map/ppermute | solution.py:151
  18.3 3.1 %collective-permute-done.2.refs_2_ = bf16[64,1024]{1,0:T(8,128)(2,1)S(1)} collective-permute-done((bf16[64,1024]{1,0:T(8,128)(2,1)S(1)}, bf16[64,1024]{1,0:T(8,128)(2,1)S(1)}, u32[]{:S(2)}, u32[]{:S(2)}) %collective-permute-start.2) | collective-permute-done | bytes 131104 | tf_op jit(solution)/shard_map/ppermute | solution.py:151
  21.5 0.5 %collective-permute-start.7 = (bf16[64,1024]{1,0:T(8,128)(2,1)S(1)}, bf16[64,1024]{1,0:T(8,128)(2,1)S(1)}, u32[]{:S(2)}, u32[]{:S(2)}) collective-permute-start(bf16[64,1024]{1,0:T(8,128)(2,1)S(1)} %collective-permute-done.3.refs_3_), channel_id=1, source_target_pairs={{0,4},{4,0},{8,12},{12,8},{16,20},{20,16},{24,28},{28,24},{1,5},{5... | collective-permute-start | bytes 393224 | tf_op jit(solution)/shard_map/ppermute | solution.py:151
  22.0 1.0 %mine_tile_kernel.1 = (f32[64,256]{1,0:T(8,128)S(1)}, f32[64,256]{1,0:T(8,128)S(1)}) custom-call(bf16[64,4096]{1,0:T(8,128)(2,1)S(1)} %copy-done.3, bf16[256,4096]{1,0:T(8,128)(2,1)S(1)} %copy-done, f32[8,128]{1,0:T(8,128)S(1)} %mark_kernel.1._, bf16[64,1024]{1,0:T(8,128)(2,1)S(1)} %collective-permute-done.refs_0_, ...), custom_call_target="tpu_custom_call" | custom-call | flops 1000000 | tf_op jit(solution)/shard_map/mine_tile_kernel/pallas_call | solution.py:214
  23.0 2.8 %collective-permute-start.12 = (f32[64,256]{1,0:T(8,128)S(1)}, f32[64,256]{1,0:T(8,128)S(1)}, u32[]{:S(2)}, u32[]{:S(2)}) collective-permute-start(f32[64,256]{1,0:T(8,128)S(1)} %get-tuple-element.37), channel_id=1, source_target_pairs={{0,2},{1,3},{2,0},{3,1},{4,7},{5,6},{6,5},{7,4},{8,10},{9,11},{10,... | collective-permute-start | bytes 196616 | tf_op jit(solution)/shard_map/ppermute | solution.py:240
  25.9 1.0 %other_tile_kernel.1 = (f32[32,256]{1,0:T(8,128)S(1)}, f32[32,256]{1,0:T(8,128)S(1)}, f32[64,256]{1,0:T(8,128)S(1)}) custom-call(bf16[256,4096]{1,0:T(8,128)(2,1)S(1)} %copy-done, bf16[64,2048]{1,0:T(8,128)(2,1)S(1)} %collective-permute-done.8.refs_0_, bf16[64,2048]{1,0:T(8,128)(2,1)S(1)} %collective-permute-done.9.refs_1_, ...), custom_call_target="tpu_custom_call" | custom-call | flops 1000000 | tf_op jit(solution)/shard_map/other_tile_kernel/pallas_call | solution.py:214
  26.9 1.6 %collective-permute-start.13 = (f32[64,256]{1,0:T(8,128)S(1)}, f32[64,256]{1,0:T(8,128)S(1)}, u32[]{:S(2)}, u32[]{:S(2)}) collective-permute-start(f32[64,256]{1,0:T(8,128)S(1)} %get-tuple-element.38), channel_id=1, source_target_pairs={{0,3},{1,2},{2,1},{3,0},{4,6},{5,7},{6,4},{7,5},{8,11},{9,10},{10,... | collective-permute-start | bytes 196616 | tf_op jit(solution)/shard_map/ppermute | solution.py:240
  28.5 2.0 %collective-permute-start.11 = (f32[32,256]{1,0:T(8,128)S(1)}, f32[32,256]{1,0:T(8,128)S(1)}, u32[]{:S(2)}, u32[]{:S(2)}) collective-permute-start(f32[32,256]{1,0:T(8,128)S(1)} %get-tuple-element.36), channel_id=1, source_target_pairs={{0,1},{1,0},{2,3},{3,2},{4,5},{5,4},{6,7},{7,6},{8,9},{9,8},{10,11... | collective-permute-start | bytes 98312 | tf_op jit(solution)/shard_map/ppermute | solution.py:151
  30.5 2.1 %collective-permute-done.10.refs_1_ = f32[32,256]{1,0:T(8,128)S(1)} collective-permute-done((f32[32,256]{1,0:T(8,128)S(1)}, f32[32,256]{1,0:T(8,128)S(1)}, u32[]{:S(2)}, u32[]{:S(2)}) %collective-permute-start.10) | collective-permute-done | bytes 32800 | tf_op jit(solution)/shard_map/ppermute | solution.py:151
  32.6 0.7 %collective-permute-done.11.refs_2_ = f32[32,256]{1,0:T(8,128)S(1)} collective-permute-done((f32[32,256]{1,0:T(8,128)S(1)}, f32[32,256]{1,0:T(8,128)S(1)}, u32[]{:S(2)}, u32[]{:S(2)}) %collective-permute-start.11) | collective-permute-done | bytes 32800 | tf_op jit(solution)/shard_map/ppermute | solution.py:151
  33.3 0.4 collective-permute-done.13.refs_4_
  33.9 0.2 base_kernel.1.base_ref
  34.0 0.4 mix_kernel.1.mix_ref
  34.5 0.6 %collective-permute-done.14.other_ref = f32[64,128]{1,0:T(8,128)S(1)} collective-permute-done((f32[64,128]{1,0:T(8,128)S(1)}, f32[64,128]{1,0:T(8,128)S(1)}, u32[]{:S(2)}, u32[]{:S(2)}) %collective-permute-start.14) | collective-permute-done | bytes 32800 | tf_op jit(solution)/shard_map/ppermute | solution.py:151
  35.2 0.7 %collective-permute-start.15 = (f32[64,128]{1,0:T(8,128)S(1)}, f32[64,128]{1,0:T(8,128)S(1)}, u32[]{:S(2)}, u32[]{:S(2)}) collective-permute-start(f32[64,128]{1,0:T(8,128)S(1)} %head_kernel.1), channel_id=1, source_target_pairs={{0,24},{1,25},{2,26},{3,27},{4,28},{5,29},{6,30},{7,31},{8,16},{9,... | collective-permute-start | bytes 98312 | tf_op jit(solution)/shard_map/ppermute | solution.py:155
  35.9 0.9 %collective-permute-start.16 = (f32[64,128]{1,0:T(8,128)S(1)}, f32[64,128]{1,0:T(8,128)S(1)}, u32[]{:S(2)}, u32[]{:S(2)}) collective-permute-start(f32[64,128]{1,0:T(8,128)S(1)} %head_kernel.1), channel_id=1, source_target_pairs={{0,16},{1,17},{2,18},{3,19},{4,12},{5,13},{6,14},{7,15},{8,24},{9,... | collective-permute-start | bytes 98312 | tf_op jit(solution)/shard_map/ppermute | solution.py:155
  36.8 1.9 %collective-permute-start.17 = (f32[64,128]{1,0:T(8,128)S(1)}, f32[64,128]{1,0:T(8,128)S(1)}, u32[]{:S(2)}, u32[]{:S(2)}) collective-permute-start(f32[64,128]{1,0:T(8,128)S(1)} %head_kernel.1), channel_id=1, source_target_pairs={{0,8},{1,9},{2,10},{3,11},{4,20},{5,21},{6,22},{7,23},{8,0},{9,1},... | collective-permute-start | bytes 98312 | tf_op jit(solution)/shard_map/ppermute | solution.py:155
  38.7 1.4 %collective-permute-done.15 = f32[64,128]{1,0:T(8,128)S(1)} collective-permute-done((f32[64,128]{1,0:T(8,128)S(1)}, f32[64,128]{1,0:T(8,128)S(1)}, u32[]{:S(2)}, u32[]{:S(2)}) %collective-permute-start.15) | collective-permute-done | bytes 32800 | tf_op jit(solution)/shard_map/ppermute | solution.py:155
  40.2 0.5 %collective-permute-done.17 = f32[64,128]{1,0:T(8,128)S(1)} collective-permute-done((f32[64,128]{1,0:T(8,128)S(1)}, f32[64,128]{1,0:T(8,128)S(1)}, u32[]{:S(2)}, u32[]{:S(2)}) %collective-permute-start.17) | collective-permute-done | bytes 32800 | tf_op jit(solution)/shard_map/ppermute | solution.py:155
  40.9 0.3 mine_kernel.1.part_ref
  41.2 0.8 %collective-permute-done.18.other_ref = f32[64,128]{1,0:T(8,128)S(1)} collective-permute-done((f32[64,128]{1,0:T(8,128)S(1)}, f32[64,128]{1,0:T(8,128)S(1)}, u32[]{:S(2)}, u32[]{:S(2)}) %collective-permute-start.18) | collective-permute-done | bytes 32800 | tf_op jit(solution)/shard_map/ppermute | solution.py:151
  42.0 1.0 %other_kernel.1 = f32[64,1024]{1,0:T(8,128)} custom-call(f32[64,1024]{1,0:T(8,128)S(1)} %mine_kernel.1.part_ref, f32[2,128,256]{2,1,0:T(8,128)S(1)} %copy-done.1, f32[4,2,128,256]{3,2,1,0:T(8,128)S(1)} %convert_multiply_fusion.refs_6_.panels_ref, f32[64,128]{1,0:T(8,128)S(1)} %select_select_fusion.refs_7_.mine_ref, ...), custom_call_target="tpu_custom_call" | custom-call | flops 1000000 | tf_op jit(solution)/shard_map/other_kernel/pallas_call | solution.py:293
  (35 shorter events, 0.6 us)
Async XLA Ops:
  0.0 1.0 %copy-start.2 = (bf16[64,4096]{1,0:T(8,128)(2,1)S(1)}, bf16[64,4096]{1,0:T(8,128)(2,1)}, u32[]{:S(2)}) copy-start(bf16[64,4096]{1,0:T(8,128)(2,1)} %own_hbm.1) | copy-start | bytes 1572868
  1.0 11.1 %copy-start.4 = (f32[2,128,128]{2,1,0:T(8,128)S(1)}, f32[2,128,128]{2,1,0:T(8,128)}, u32[]{:S(2)}) copy-start(f32[2,128,128]{2,1,0:T(8,128)} %inverse_ref.3) | copy-start | bytes 393220
  1.1 11.1 %collective-permute-start = (bf16[64,1024]{1,0:T(8,128)(2,1)S(1)}, bf16[64,1024]{1,0:T(8,128)(2,1)S(1)}, u32[]{:S(2)}, u32[]{:S(2)}) collective-permute-start(bf16[64,1024]{1,0:T(8,128)(2,1)S(1)} %get-tuple-element.25), channel_id=1, source_target_pairs={{0,2},{1,3},{2,0},{3,1},{4,7},{5,6},{6,5},{7,4},{8,10},{9,11},{10,... | collective-permute-start | bytes 393224 | tf_op jit(solution)/shard_map/ppermute | solution.py:187
  5.2 10.6 %collective-permute-start.8 = (bf16[64,2048]{1,0:T(8,128)(2,1)S(1)}, bf16[64,2048]{1,0:T(8,128)(2,1)S(1)}, u32[]{:S(2)}, u32[]{:S(2)}) collective-permute-start(bf16[64,2048]{1,0:T(8,128)(2,1)S(1)} %get-tuple-element.30), channel_id=1, source_target_pairs={{0,1},{1,0},{2,3},{3,2},{4,5},{5,4},{6,7},{7,6},{8,9},{9,8},{10,11... | collective-permute-start | bytes 786440 | tf_op jit(solution)/shard_map/ppermute | solution.py:151
  8.7 25.0 %all-to-all-start = ((f16[4,2,128,256]{3,2,1,0:T(8,128)(2,1)}), f16[4,2,128,256]{3,2,1,0:T(8,128)(2,1)S(1)}, u32[]{:S(2)}, u32[]{:S(2)}) async-start(f16[4,2,128,256]{3,2,1,0:T(8,128)(2,1)} %bitcast), calls=%async_computation | async-start | bytes 1048576 | tf_op jit(solution)/shard_map/all_to_all | solution.py:194
  12.2 9.8 %copy-start = (bf16[256,4096]{1,0:T(8,128)(2,1)S(1)}, bf16[256,4096]{1,0:T(8,128)(2,1)}, u32[]{:S(2)}) copy-start(bf16[256,4096]{1,0:T(8,128)(2,1)} %support_ref.3) | copy-start | bytes 6291460
  12.2 9.8 %copy-start.3 = (bf16[64,4096]{1,0:T(8,128)(2,1)S(1)}, bf16[64,4096]{1,0:T(8,128)(2,1)}, u32[]{:S(2)}) copy-start(bf16[64,4096]{1,0:T(8,128)(2,1)} %own_hbm.1) | copy-start | bytes 1572868
  12.2 6.1 %collective-permute-start.1 = (bf16[64,1024]{1,0:T(8,128)(2,1)S(1)}, bf16[64,1024]{1,0:T(8,128)(2,1)S(1)}, u32[]{:S(2)}, u32[]{:S(2)}) collective-permute-start(bf16[64,1024]{1,0:T(8,128)(2,1)S(1)} %collective-permute-done.refs_0_), channel_id=1, source_target_pairs={{0,8},{4,12},{8,0},{12,4},{16,24},{20,28},{24,16},{28,20},{1,9},{5... | collective-permute-start | bytes 393224 | tf_op jit(solution)/shard_map/ppermute | solution.py:151
  13.8 7.7 %collective-permute-start.2 = (bf16[64,1024]{1,0:T(8,128)(2,1)S(1)}, bf16[64,1024]{1,0:T(8,128)(2,1)S(1)}, u32[]{:S(2)}, u32[]{:S(2)}) collective-permute-start(bf16[64,1024]{1,0:T(8,128)(2,1)S(1)} %collective-permute-done.refs_0_), channel_id=1, source_target_pairs={{0,16},{4,20},{8,24},{12,28},{16,0},{20,4},{24,8},{28,12},{1,17},{... | collective-permute-start | bytes 393224 | tf_op jit(solution)/shard_map/ppermute | solution.py:151
  15.3 6.2 %collective-permute-start.3 = (bf16[64,1024]{1,0:T(8,128)(2,1)S(1)}, bf16[64,1024]{1,0:T(8,128)(2,1)S(1)}, u32[]{:S(2)}, u32[]{:S(2)}) collective-permute-start(bf16[64,1024]{1,0:T(8,128)(2,1)S(1)} %collective-permute-done.refs_0_), channel_id=1, source_target_pairs={{0,24},{4,28},{8,16},{12,20},{16,8},{20,12},{24,0},{28,4},{1,25},{... | collective-permute-start | bytes 393224 | tf_op jit(solution)/shard_map/ppermute | solution.py:151
  15.8 10.1 %collective-permute-start.9 = (bf16[64,2048]{1,0:T(8,128)(2,1)S(1)}, bf16[64,2048]{1,0:T(8,128)(2,1)S(1)}, u32[]{:S(2)}, u32[]{:S(2)}) collective-permute-start(bf16[64,2048]{1,0:T(8,128)(2,1)S(1)} %collective-permute-done.8.refs_0_), channel_id=1, source_target_pairs={{0,4},{4,0},{8,12},{12,8},{16,20},{20,16},{24,28},{28,24},{1,5},{5... | collective-permute-start | bytes 786440 | tf_op jit(solution)/shard_map/ppermute | solution.py:151
  15.8 7.2 %collective-permute-start.4 = (bf16[64,1024]{1,0:T(8,128)(2,1)S(1)}, bf16[64,1024]{1,0:T(8,128)(2,1)S(1)}, u32[]{:S(2)}, u32[]{:S(2)}) collective-permute-start(bf16[64,1024]{1,0:T(8,128)(2,1)S(1)} %collective-permute-done.refs_0_), channel_id=1, source_target_pairs={{0,4},{4,0},{8,12},{12,8},{16,20},{20,16},{24,28},{28,24},{1,5},{5... | collective-permute-start | bytes 393224 | tf_op jit(solution)/shard_map/ppermute | solution.py:151
  18.3 7.5 %collective-permute-start.5 = (bf16[64,1024]{1,0:T(8,128)(2,1)S(1)}, bf16[64,1024]{1,0:T(8,128)(2,1)S(1)}, u32[]{:S(2)}, u32[]{:S(2)}) collective-permute-start(bf16[64,1024]{1,0:T(8,128)(2,1)S(1)} %collective-permute-done.1.refs_1_), channel_id=1, source_target_pairs={{0,4},{4,0},{8,12},{12,8},{16,20},{20,16},{24,28},{28,24},{1,5},{5... | collective-permute-start | bytes 393224 | tf_op jit(solution)/shard_map/ppermute | solution.py:151
  21.5 4.4 %collective-permute-start.6 = (bf16[64,1024]{1,0:T(8,128)(2,1)S(1)}, bf16[64,1024]{1,0:T(8,128)(2,1)S(1)}, u32[]{:S(2)}, u32[]{:S(2)}) collective-permute-start(bf16[64,1024]{1,0:T(8,128)(2,1)S(1)} %collective-permute-done.2.refs_2_), channel_id=1, source_target_pairs={{0,4},{4,0},{8,12},{12,8},{16,20},{20,16},{24,28},{28,24},{1,5},{5... | collective-permute-start | bytes 393224 | tf_op jit(solution)/shard_map/ppermute | solution.py:151
  21.5 4.4 %collective-permute-start.7 = (bf16[64,1024]{1,0:T(8,128)(2,1)S(1)}, bf16[64,1024]{1,0:T(8,128)(2,1)S(1)}, u32[]{:S(2)}, u32[]{:S(2)}) collective-permute-start(bf16[64,1024]{1,0:T(8,128)(2,1)S(1)} %collective-permute-done.3.refs_3_), channel_id=1, source_target_pairs={{0,4},{4,0},{8,12},{12,8},{16,20},{20,16},{24,28},{28,24},{1,5},{5... | collective-permute-start | bytes 393224 | tf_op jit(solution)/shard_map/ppermute | solution.py:151
  23.0 7.5 %collective-permute-start.12 = (f32[64,256]{1,0:T(8,128)S(1)}, f32[64,256]{1,0:T(8,128)S(1)}, u32[]{:S(2)}, u32[]{:S(2)}) collective-permute-start(f32[64,256]{1,0:T(8,128)S(1)} %get-tuple-element.37), channel_id=1, source_target_pairs={{0,2},{1,3},{2,0},{3,1},{4,7},{5,6},{6,5},{7,4},{8,10},{9,11},{10,... | collective-permute-start | bytes 196616 | tf_op jit(solution)/shard_map/ppermute | solution.py:240
  26.9 14.0 %copy-start.1 = (f32[2,128,256]{2,1,0:T(8,128)S(1)}, f32[2,128,256]{2,1,0:T(8,128)}, u32[]{:S(2)}) copy-start(f32[2,128,256]{2,1,0:T(8,128)} %own_ref.1) | copy-start | bytes 786436
  26.9 6.8 %collective-permute-start.13 = (f32[64,256]{1,0:T(8,128)S(1)}, f32[64,256]{1,0:T(8,128)S(1)}, u32[]{:S(2)}, u32[]{:S(2)}) collective-permute-start(f32[64,256]{1,0:T(8,128)S(1)} %get-tuple-element.38), channel_id=1, source_target_pairs={{0,3},{1,2},{2,1},{3,0},{4,6},{5,7},{6,4},{7,5},{8,11},{9,10},{10,... | collective-permute-start | bytes 196616 | tf_op jit(solution)/shard_map/ppermute | solution.py:240
  28.5 4.1 %collective-permute-start.10 = (f32[32,256]{1,0:T(8,128)S(1)}, f32[32,256]{1,0:T(8,128)S(1)}, u32[]{:S(2)}, u32[]{:S(2)}) collective-permute-start(f32[32,256]{1,0:T(8,128)S(1)} %get-tuple-element.35), channel_id=1, source_target_pairs={{0,1},{1,0},{2,3},{3,2},{4,5},{5,4},{6,7},{7,6},{8,9},{9,8},{10,11... | collective-permute-start | bytes 98312 | tf_op jit(solution)/shard_map/ppermute | solution.py:151
  28.5 4.8 %collective-permute-start.11 = (f32[32,256]{1,0:T(8,128)S(1)}, f32[32,256]{1,0:T(8,128)S(1)}, u32[]{:S(2)}, u32[]{:S(2)}) collective-permute-start(f32[32,256]{1,0:T(8,128)S(1)} %get-tuple-element.36), channel_id=1, source_target_pairs={{0,1},{1,0},{2,3},{3,2},{4,5},{5,4},{6,7},{7,6},{8,9},{9,8},{10,11... | collective-permute-start | bytes 98312 | tf_op jit(solution)/shard_map/ppermute | solution.py:151
  33.8 1.3 %collective-permute-start.14 = (f32[64,128]{1,0:T(8,128)S(1)}, f32[64,128]{1,0:T(8,128)S(1)}, u32[]{:S(2)}, u32[]{:S(2)}) collective-permute-start(f32[64,128]{1,0:T(8,128)S(1)} %fusion.1.mine_ref), channel_id=1, source_target_pairs={{0,4},{4,0},{8,12},{12,8},{16,20},{20,16},{24,28},{28,24},{1,5},{5... | collective-permute-start | bytes 98312 | tf_op jit(solution)/shard_map/ppermute | solution.py:151
  35.2 5.0 %collective-permute-start.15 = (f32[64,128]{1,0:T(8,128)S(1)}, f32[64,128]{1,0:T(8,128)S(1)}, u32[]{:S(2)}, u32[]{:S(2)}) collective-permute-start(f32[64,128]{1,0:T(8,128)S(1)} %head_kernel.1), channel_id=1, source_target_pairs={{0,24},{1,25},{2,26},{3,27},{4,28},{5,29},{6,30},{7,31},{8,16},{9,... | collective-permute-start | bytes 98312 | tf_op jit(solution)/shard_map/ppermute | solution.py:155
  35.9 4.3 %collective-permute-start.16 = (f32[64,128]{1,0:T(8,128)S(1)}, f32[64,128]{1,0:T(8,128)S(1)}, u32[]{:S(2)}, u32[]{:S(2)}) collective-permute-start(f32[64,128]{1,0:T(8,128)S(1)} %head_kernel.1), channel_id=1, source_target_pairs={{0,16},{1,17},{2,18},{3,19},{4,12},{5,13},{6,14},{7,15},{8,24},{9,... | collective-permute-start | bytes 98312 | tf_op jit(solution)/shard_map/ppermute | solution.py:155
  36.8 3.9 %collective-permute-start.17 = (f32[64,128]{1,0:T(8,128)S(1)}, f32[64,128]{1,0:T(8,128)S(1)}, u32[]{:S(2)}, u32[]{:S(2)}) collective-permute-start(f32[64,128]{1,0:T(8,128)S(1)} %head_kernel.1), channel_id=1, source_target_pairs={{0,8},{1,9},{2,10},{3,11},{4,20},{5,21},{6,22},{7,23},{8,0},{9,1},... | collective-permute-start | bytes 98312 | tf_op jit(solution)/shard_map/ppermute | solution.py:155
  40.7 1.3 %collective-permute-start.18 = (f32[64,128]{1,0:T(8,128)S(1)}, f32[64,128]{1,0:T(8,128)S(1)}, u32[]{:S(2)}, u32[]{:S(2)}) collective-permute-start(f32[64,128]{1,0:T(8,128)S(1)} %select_select_fusion.refs_7_.mine_ref), channel_id=1, source_target_pairs={{0,4},{4,0},{8,12},{12,8},{16,20},{20,16},{24,28},{28,24},{1,5},{5... | collective-permute-start | bytes 98312 | tf_op jit(solution)/shard_map/ppermute | solution.py:151

commit v9 on v8

--- a/solution.py
+++ b/solution.py
@@ -63,13 +63,12 @@
     out_ref[...] = value_ref[0, :8, :128]
 
 
-def mine_tile_kernel(scale, n_row, own_hbm, support_ref, _, *refs):
-    planes = (len(refs) - 3) // (n_row // 2 + 1)
-    far, outs, (targets_ref, sems) = refs[:-3 - planes], refs[-3 - planes:-2], refs[-2:]
-    rows = own_hbm.shape[0]
-    loads = [(own_hbm, targets_ref.at[pl.ds(0, rows)])] + far_loads(n_row, rows, far, targets_ref, 1)
-    wait_all(start_all(loads, sems))
-    kernel = jnp.exp(scale * dot(targets_ref[...], support_ref[...], NT))
+def mine_tile_kernel(scale, n_row, support_ref, _, *refs):
+    planes = (len(refs) - 2) // (n_row // 2 + 1)
+    far, outs, (targets_ref, sems) = refs[:-2 - planes], refs[-2 - planes:-2], refs[-2:]
+    rows = outs[0].shape[0]
+    wait_all(start_all(far_loads(n_row, rows, far, targets_ref, 0), sems))
+    kernel = jnp.exp(scale * dot(targets_ref[pl.ds(0, planes * rows)], support_ref[...], NT))
     for plane, out_ref in enumerate(outs):
         out_ref[...] = kernel[plane * rows:(plane + 1) * rows]
 
@@ -84,13 +83,14 @@
     return loads
 
 
-def other_tile_kernel(scale, n_row, support_ref, *refs):
-    planes = (len(refs) - 6) // (n_row // 2 + 1)
-    near, far, refs = refs[:2], refs[2:-4 - planes], refs[-4 - planes:]
+def other_tile_kernel(scale, n_row, own_hbm, support_ref, *refs):
+    planes = (len(refs) - 7) // (n_row // 2 + 1)
+    near, far, refs = refs[:2], refs[2:-5 - planes], refs[-5 - planes:]
     outs, (targets_ref, sems) = refs[:-2], refs[-2:]
     rows, half = near[0].shape
     row = lax.axis_index("row")
     loads = far_loads(n_row, rows, far, targets_ref, 1)
+    loads.append((own_hbm, targets_ref.at[pl.ds((1 + planes) * rows, rows)]))
     for part in range(2):
         cols = pl.ds(pl.multiple_of((row % 2 ^ part) * half, half), half)
         loads.append((near[part], targets_ref.at[pl.ds(0, rows), cols]))
@@ -169,6 +169,8 @@
     row, col = lax.axis_index("row"), lax.axis_index("col")
     width = 2 * features // n_row
 
+    small = (panels * PANEL_UNIT).astype(jnp.float16)
+    targets, small = together(targets, small)
     mine, half = pl.pallas_call(
         functools.partial(cut_kernel, n_row),
         out_shape=[
@@ -189,8 +191,7 @@
         ])
         for j in range(2, n_col, 2)
     ]
-    small = jnp.concatenate([panels * PANEL_UNIT] * n_col, axis=0).astype(jnp.float16)
-    small = small.reshape(n_col, *panels.shape)
+    small = jnp.concatenate([small] * n_col, axis=0).reshape(n_col, *panels.shape)
     blocks = lax.all_to_all(small, "col", 0, 0)
     mark = pl.pallas_call(
         mark_kernel,
@@ -217,7 +218,7 @@
             in_specs=[VMEM if operand is support else HBM for operand in operands],
             out_specs=[VMEM] * len(counts),
             scratch_shapes=[
-                pltpu.VMEM(((1 + len(far)) * rows, features), jnp.bfloat16),
+                pltpu.VMEM(((2 + len(far)) * rows, features), jnp.bfloat16),
                 pltpu.SemaphoreType.DMA((pieces,)),
             ],
             compiler_params=TILE_PARAMS,
@@ -226,13 +227,13 @@
         )(*operands))
 
     first = tile_call(
-        mine_tile_kernel, "mine_tile_kernel", [rows] * (1 + len(far)), targets, support, mark, *mine_far
+        mine_tile_kernel, "mine_tile_kernel", [rows] * len(far), support, mark, *mine_far
     )
     first[0], *other_far = together(first[0], *other_far)
     last = tile_call(
-        other_tile_kernel, "other_tile_kernel", [rows // 2] * 2 + [rows] * len(far), support, *near, *other_far
+        other_tile_kernel, "other_tile_kernel", [rows // 2] * 2 + [rows] * (1 + len(far)), targets, support, *near, *other_far
     )
-    made = [first[0], *last[:2], *first[1:], *last[2:]]
+    made = [last[-1], *last[:2], *first, *last[2:-1]]
 
     tiles = [made[0]] + [exchange(tile, "col", n_col, 1) for tile in made[1:3]]
     for i, tile in enumerate(made[3:]):

time: 43.2 us -> 43.3 us (level)
  waiting for transfers between devices: 11.7 us -> 12.4 us
  starting transfers between devices: 23.8 us -> 23.2 us
    convert_element_type x0 -> x1, other arithmetic: none -> 1.01 us  [shards(): small = (panels * PANEL_UNIT).astype(jnp.float16)]
    another operation x1 -> x0, other arithmetic: 0.97 us -> none
    ppermute x13, waiting for transfers between devices: 9.34 us -> 9.93 us  [exchange(): return lax.ppermute(value, axis, [(i, i ^ mask) for i in range(size)])]
    ppermute x1, waiting for transfers between devices: 0.01 us -> 0.55 us  [shards(): lax.ppermute(mine, ('row', 'col'), [(r * n_col + c, r * n_col + (c ^ j +...]
    ppermute x13, starting transfers between devices: 8.32 us -> 7.86 us  [exchange(): return lax.ppermute(value, axis, [(i, i ^ mask) for i in range(size)])]
  transfers between devices with their start and end apart: 20 -> 20, of which waited for: 9 -> 12; matrix products, arithmetic and copies ran while one was open for 5% -> 2% of each run, Pallas kernels for 7% -> 7%
where the time goes in v9:
time: 43.3 us; the launch traced here: 43 us
  starting transfers between devices  23.2 us (54%)
  waiting for transfers between devices  12.4 us (29%)
  Pallas kernels  4.06 us (9%)
  other arithmetic  2.07 us (5%)
  local copies, waits for them, and re-layouts  1.06 us (2%)
    ppermute x13, waiting for transfers between devices, exchange(): return lax.ppermute(value, axis, [(i, i ^ mask) for i in range(size)])  9.93 us
    ppermute x13, starting transfers between devices, exchange(): return lax.ppermute(value, axis, [(i, i ^ mask) for i in range(size)])  7.86 us
    ppermute x2, starting transfers between devices, shards(): lax.ppermute(tile, ('row', 'col'), [(r * n_col + c, r * n_col + (c ^ 2 *...  4.25 us
    ppermute x1, starting transfers between devices, shards(): lax.ppermute(mine, ('row', 'col'), [(r * n_col + c, r * n_col + (c ^ j +...  4.1 us
    ppermute x3, starting transfers between devices, exchange_chips(): lax.ppermute(value, ('row', 'col'), [(r * n_col + c, (r ^ 2 * chip_offset...  3.55 us
    all_to_all x1, starting transfers between devices, shards(): blocks = lax.all_to_all(small, 'col', 0, 0)  3.47 us
    pallas_call x2, Pallas kernels, tile_call(): pl.pallas_call(functools.partial(body, scale, n_row), out_shape=[jax.Shap...  2 us
    ppermute x3, waiting for transfers between devices, exchange_chips(): lax.ppermute(value, ('row', 'col'), [(r * n_col + c, (r ^ 2 * chip_offset...  1.9 us
  transfers between devices with their start and end apart: 20, of which 12 were waited for; matrix products, arithmetic and copies ran while one was open for 2% of the time, Pallas kernels for 7%

profile of v9, /device:TPU:0, one launch (start us, length us, event | category | flops | bytes accessed | tf_op | source)
XLA Modules:
  0.0 43.0 jit_solution(2942318394674397857)
XLA Ops:
  0.0 1.0 %multiply_convert_fusion = f16[2,128,256]{2,1,0:T(8,128)(2,1)S(1)} fusion(f32[2,128,256]{2,1,0:T(8,128)} %own_ref.1), kind=kLoop, calls=%fused_computation.2 | loop fusion | flops 131072 | bytes 393216 | tf_op jit(solution)/shard_map/convert_element_type | solution.py:172
  1.0 1.0 %copy-done.2 = bf16[64,4096]{1,0:T(8,128)(2,1)S(1)} copy-done((bf16[64,4096]{1,0:T(8,128)(2,1)S(1)}, bf16[64,4096]{1,0:T(8,128)(2,1)}, u32[]{:S(2)}) %copy-start.2) | copy-done | bytes 524312
  2.1 4.1 %collective-permute-start.2 = (bf16[64,1024]{1,0:T(8,128)(2,1)S(1)}, bf16[64,1024]{1,0:T(8,128)(2,1)S(1)}, u32[]{:S(2)}, u32[]{:S(2)}) collective-permute-start(bf16[64,1024]{1,0:T(8,128)(2,1)S(1)} %get-tuple-element.28), channel_id=1, source_target_pairs={{0,2},{1,3},{2,0},{3,1},{4,7},{5,6},{6,5},{7,4},{8,10},{9,11},{10,... | collective-permute-start | bytes 393224 | tf_op jit(solution)/shard_map/ppermute | solution.py:189
  6.2 1.6 %collective-permute-start = (bf16[64,2048]{1,0:T(8,128)(2,1)S(1)}, bf16[64,2048]{1,0:T(8,128)(2,1)S(1)}, u32[]{:S(2)}, u32[]{:S(2)}) collective-permute-start(bf16[64,2048]{1,0:T(8,128)(2,1)S(1)} %get-tuple-element.27), channel_id=1, source_target_pairs={{0,1},{1,0},{2,3},{3,2},{4,5},{5,4},{6,7},{7,6},{8,9},{9,8},{10,11... | collective-permute-start | bytes 786440 | tf_op jit(solution)/shard_map/ppermute | solution.py:151
  7.8 0.9 %pad_maximum_fusion = f16[8,128,256]{2,1,0:T(8,128)(2,1)} fusion(f16[2,128,256]{2,1,0:T(8,128)(2,1)S(1)} %multiply_convert_fusion), kind=kLoop, calls=%fused_computation.1 | loop fusion | flops 786432 | bytes 655360 | tf_op jit(solution)/shard_map/concatenate | solution.py:194
  8.7 3.5 %all-to-all-start = ((f16[4,2,128,256]{3,2,1,0:T(8,128)(2,1)}), f16[4,2,128,256]{3,2,1,0:T(8,128)(2,1)S(1)}, u32[]{:S(2)}, u32[]{:S(2)}) async-start(f16[4,2,128,256]{3,2,1,0:T(8,128)(2,1)} %bitcast), calls=%async_computation | async-start | bytes 1048576 | tf_op jit(solution)/shard_map/all_to_all | solution.py:195
  12.3 0.5 %collective-permute-done.2.refs_0_ = bf16[64,1024]{1,0:T(8,128)(2,1)S(1)} collective-permute-done((bf16[64,1024]{1,0:T(8,128)(2,1)S(1)}, bf16[64,1024]{1,0:T(8,128)(2,1)S(1)}, u32[]{:S(2)}, u32[]{:S(2)}) %collective-permute-start.2) | collective-permute-done | bytes 131104 | tf_op jit(solution)/shard_map/ppermute | solution.py:189
  12.8 1.5 %collective-permute-start.3 = (bf16[64,1024]{1,0:T(8,128)(2,1)S(1)}, bf16[64,1024]{1,0:T(8,128)(2,1)S(1)}, u32[]{:S(2)}, u32[]{:S(2)}) collective-permute-start(bf16[64,1024]{1,0:T(8,128)(2,1)S(1)} %collective-permute-done.2.refs_0_), channel_id=1, source_target_pairs={{0,8},{4,12},{8,0},{12,4},{16,24},{20,28},{24,16},{28,20},{1,9},{5... | collective-permute-start | bytes 393224 | tf_op jit(solution)/shard_map/ppermute | solution.py:151
  14.3 1.5 %collective-permute-start.4 = (bf16[64,1024]{1,0:T(8,128)(2,1)S(1)}, bf16[64,1024]{1,0:T(8,128)(2,1)S(1)}, u32[]{:S(2)}, u32[]{:S(2)}) collective-permute-start(bf16[64,1024]{1,0:T(8,128)(2,1)S(1)} %collective-permute-done.2.refs_0_), channel_id=1, source_target_pairs={{0,16},{4,20},{8,24},{12,28},{16,0},{20,4},{24,8},{28,12},{1,17},{... | collective-permute-start | bytes 393224 | tf_op jit(solution)/shard_map/ppermute | solution.py:151
  15.8 0.5 %collective-permute-start.5 = (bf16[64,1024]{1,0:T(8,128)(2,1)S(1)}, bf16[64,1024]{1,0:T(8,128)(2,1)S(1)}, u32[]{:S(2)}, u32[]{:S(2)}) collective-permute-start(bf16[64,1024]{1,0:T(8,128)(2,1)S(1)} %collective-permute-done.2.refs_0_), channel_id=1, source_target_pairs={{0,24},{4,28},{8,16},{12,20},{16,8},{20,12},{24,0},{28,4},{1,25},{... | collective-permute-start | bytes 393224 | tf_op jit(solution)/shard_map/ppermute | solution.py:151
  16.3 3.0 %collective-permute-done.refs_0_ = bf16[64,2048]{1,0:T(8,128)(2,1)S(1)} collective-permute-done((bf16[64,2048]{1,0:T(8,128)(2,1)S(1)}, bf16[64,2048]{1,0:T(8,128)(2,1)S(1)}, u32[]{:S(2)}, u32[]{:S(2)}) %collective-permute-start) | collective-permute-done | bytes 262176 | tf_op jit(solution)/shard_map/ppermute | solution.py:151
  19.3 0.5 %collective-permute-start.6 = (bf16[64,1024]{1,0:T(8,128)(2,1)S(1)}, bf16[64,1024]{1,0:T(8,128)(2,1)S(1)}, u32[]{:S(2)}, u32[]{:S(2)}) collective-permute-start(bf16[64,1024]{1,0:T(8,128)(2,1)S(1)} %collective-permute-done.2.refs_0_), channel_id=1, source_target_pairs={{0,4},{4,0},{8,12},{12,8},{16,20},{20,16},{24,28},{28,24},{1,5},{5... | collective-permute-start | bytes 393224 | tf_op jit(solution)/shard_map/ppermute | solution.py:151
  19.8 0.5 %collective-permute-done.4.refs_2_ = bf16[64,1024]{1,0:T(8,128)(2,1)S(1)} collective-permute-done((bf16[64,1024]{1,0:T(8,128)(2,1)S(1)}, bf16[64,1024]{1,0:T(8,128)(2,1)S(1)}, u32[]{:S(2)}, u32[]{:S(2)}) %collective-permute-start.4) | collective-permute-done | bytes 131104 | tf_op jit(solution)/shard_map/ppermute | solution.py:151
  20.4 1.4 %collective-permute-done.5.refs_3_ = bf16[64,1024]{1,0:T(8,128)(2,1)S(1)} collective-permute-done((bf16[64,1024]{1,0:T(8,128)(2,1)S(1)}, bf16[64,1024]{1,0:T(8,128)(2,1)S(1)}, u32[]{:S(2)}, u32[]{:S(2)}) %collective-permute-start.5) | collective-permute-done | bytes 131104 | tf_op jit(solution)/shard_map/ppermute | solution.py:151
  21.8 0.9 %mine_tile_kernel.1 = f32[64,256]{1,0:T(8,128)S(1)} custom-call(bf16[256,4096]{1,0:T(8,128)(2,1)S(1)} %copy-done, f32[8,128]{1,0:T(8,128)S(1)} %mark_kernel.1._, bf16[64,1024]{1,0:T(8,128)(2,1)S(1)} %collective-permute-done.2.refs_0_, bf16[64,1024]{1,0:T(8,128)(2,1)S(1)} %collective-permute-done.3.refs_1_, ...), custom_call_target="tpu_custom_call" | custom-call | flops 1000000 | tf_op jit(solution)/shard_map/mine_tile_kernel/pallas_call | solution.py:215
  22.7 0.4 collective-permute-done.9.refs_5_
  23.1 2.7 %collective-permute-start.12 = (f32[64,256]{1,0:T(8,128)S(1)}, f32[64,256]{1,0:T(8,128)S(1)}, u32[]{:S(2)}, u32[]{:S(2)}) collective-permute-start(f32[64,256]{1,0:T(8,128)S(1)} %mine_tile_kernel.1), channel_id=1, source_target_pairs={{0,2},{1,3},{2,0},{3,1},{4,7},{5,6},{6,5},{7,4},{8,10},{9,11},{10,... | collective-permute-start | bytes 196616 | tf_op jit(solution)/shard_map/ppermute | solution.py:241
  25.8 1.1 %other_tile_kernel.1 = (f32[32,256]{1,0:T(8,128)S(1)}, f32[32,256]{1,0:T(8,128)S(1)}, f32[64,256]{1,0:T(8,128)S(1)}, f32[64,256]{1,0:T(8,128)S(1)}) custom-call(bf16[64,4096]{1,0:T(8,128)(2,1)S(1)} %copy-done.3, bf16[256,4096]{1,0:T(8,128)(2,1)S(1)} %copy-done, bf16[64,2048]{1,0:T(8,128)(2,1)S(1)} %collective-permute-done.refs_0_, ...), custom_call_target="tpu_custom_call" | custom-call | flops 1000000 | tf_op jit(solution)/shard_map/other_tile_kernel/pallas_call | solution.py:215
  26.9 1.5 %collective-permute-start.13 = (f32[64,256]{1,0:T(8,128)S(1)}, f32[64,256]{1,0:T(8,128)S(1)}, u32[]{:S(2)}, u32[]{:S(2)}) collective-permute-start(f32[64,256]{1,0:T(8,128)S(1)} %get-tuple-element.39), channel_id=1, source_target_pairs={{0,3},{1,2},{2,1},{3,0},{4,6},{5,7},{6,4},{7,5},{8,11},{9,10},{10,... | collective-permute-start | bytes 196616 | tf_op jit(solution)/shard_map/ppermute | solution.py:241
  28.5 2.0 %collective-permute-start.11 = (f32[32,256]{1,0:T(8,128)S(1)}, f32[32,256]{1,0:T(8,128)S(1)}, u32[]{:S(2)}, u32[]{:S(2)}) collective-permute-start(f32[32,256]{1,0:T(8,128)S(1)} %get-tuple-element.37), channel_id=1, source_target_pairs={{0,1},{1,0},{2,3},{3,2},{4,5},{5,4},{6,7},{7,6},{8,9},{9,8},{10,11... | collective-permute-start | bytes 98312 | tf_op jit(solution)/shard_map/ppermute | solution.py:151
  30.5 2.9 %collective-permute-done.10.refs_1_ = f32[32,256]{1,0:T(8,128)S(1)} collective-permute-done((f32[32,256]{1,0:T(8,128)S(1)}, f32[32,256]{1,0:T(8,128)S(1)}, u32[]{:S(2)}, u32[]{:S(2)}) %collective-permute-start.10) | collective-permute-done | bytes 32800 | tf_op jit(solution)/shard_map/ppermute | solution.py:151
  33.4 0.5 %collective-permute-done.11.refs_2_ = f32[32,256]{1,0:T(8,128)S(1)} collective-permute-done((f32[32,256]{1,0:T(8,128)S(1)}, f32[32,256]{1,0:T(8,128)S(1)}, u32[]{:S(2)}, u32[]{:S(2)}) %collective-permute-start.11) | collective-permute-done | bytes 32800 | tf_op jit(solution)/shard_map/ppermute | solution.py:151
  34.2 0.4 mix_kernel.1.mix_ref
  34.6 0.6 %collective-permute-done.14.other_ref = f32[64,128]{1,0:T(8,128)S(1)} collective-permute-done((f32[64,128]{1,0:T(8,128)S(1)}, f32[64,128]{1,0:T(8,128)S(1)}, u32[]{:S(2)}, u32[]{:S(2)}) %collective-permute-start.14) | collective-permute-done | bytes 32800 | tf_op jit(solution)/shard_map/ppermute | solution.py:151
  35.3 0.8 %collective-permute-start.15 = (f32[64,128]{1,0:T(8,128)S(1)}, f32[64,128]{1,0:T(8,128)S(1)}, u32[]{:S(2)}, u32[]{:S(2)}) collective-permute-start(f32[64,128]{1,0:T(8,128)S(1)} %head_kernel.1), channel_id=1, source_target_pairs={{0,24},{1,25},{2,26},{3,27},{4,28},{5,29},{6,30},{7,31},{8,16},{9,... | collective-permute-start | bytes 98312 | tf_op jit(solution)/shard_map/ppermute | solution.py:155
  36.1 0.7 %collective-permute-start.16 = (f32[64,128]{1,0:T(8,128)S(1)}, f32[64,128]{1,0:T(8,128)S(1)}, u32[]{:S(2)}, u32[]{:S(2)}) collective-permute-start(f32[64,128]{1,0:T(8,128)S(1)} %head_kernel.1), channel_id=1, source_target_pairs={{0,16},{1,17},{2,18},{3,19},{4,12},{5,13},{6,14},{7,15},{8,24},{9,... | collective-permute-start | bytes 98312 | tf_op jit(solution)/shard_map/ppermute | solution.py:155
  36.8 2.0 %collective-permute-start.17 = (f32[64,128]{1,0:T(8,128)S(1)}, f32[64,128]{1,0:T(8,128)S(1)}, u32[]{:S(2)}, u32[]{:S(2)}) collective-permute-start(f32[64,128]{1,0:T(8,128)S(1)} %head_kernel.1), channel_id=1, source_target_pairs={{0,8},{1,9},{2,10},{3,11},{4,20},{5,21},{6,22},{7,23},{8,0},{9,1},... | collective-permute-start | bytes 98312 | tf_op jit(solution)/shard_map/ppermute | solution.py:155
  38.9 1.4 %collective-permute-done.15 = f32[64,128]{1,0:T(8,128)S(1)} collective-permute-done((f32[64,128]{1,0:T(8,128)S(1)}, f32[64,128]{1,0:T(8,128)S(1)}, u32[]{:S(2)}, u32[]{:S(2)}) %collective-permute-start.15) | collective-permute-done | bytes 32800 | tf_op jit(solution)/shard_map/ppermute | solution.py:155
  40.3 0.3 collective-permute-done.16
  41.1 0.3 mine_kernel.1.part_ref
  41.4 0.7 %collective-permute-done.18.other_ref = f32[64,128]{1,0:T(8,128)S(1)} collective-permute-done((f32[64,128]{1,0:T(8,128)S(1)}, f32[64,128]{1,0:T(8,128)S(1)}, u32[]{:S(2)}, u32[]{:S(2)}) %collective-permute-start.18) | collective-permute-done | bytes 32800 | tf_op jit(solution)/shard_map/ppermute | solution.py:151
  42.0 1.0 %other_kernel.1 = f32[64,1024]{1,0:T(8,128)} custom-call(f32[64,1024]{1,0:T(8,128)S(1)} %mine_kernel.1.part_ref, f32[2,128,256]{2,1,0:T(8,128)S(1)} %copy-done.1, f32[4,2,128,256]{3,2,1,0:T(8,128)S(1)} %convert_multiply_fusion.refs_6_.panels_ref, f32[64,128]{1,0:T(8,128)S(1)} %select_select_fusion.refs_7_.mine_ref, ...), custom_call_target="tpu_custom_call" | custom-call | flops 1000000 | tf_op jit(solution)/shard_map/other_kernel/pallas_call | solution.py:294
  (35 shorter events, 1.1 us)
Async XLA Ops:
  0.0 12.2 %copy-start.4 = (f32[2,128,128]{2,1,0:T(8,128)S(1)}, f32[2,128,128]{2,1,0:T(8,128)}, u32[]{:S(2)}) copy-start(f32[2,128,128]{2,1,0:T(8,128)} %inverse_ref.3) | copy-start | bytes 393220
  1.0 1.0 %copy-start.2 = (bf16[64,4096]{1,0:T(8,128)(2,1)S(1)}, bf16[64,4096]{1,0:T(8,128)(2,1)}, u32[]{:S(2)}) copy-start(bf16[64,4096]{1,0:T(8,128)(2,1)} %own_hbm) | copy-start | bytes 1572868
  2.1 10.7 %collective-permute-start.2 = (bf16[64,1024]{1,0:T(8,128)(2,1)S(1)}, bf16[64,1024]{1,0:T(8,128)(2,1)S(1)}, u32[]{:S(2)}, u32[]{:S(2)}) collective-permute-start(bf16[64,1024]{1,0:T(8,128)(2,1)S(1)} %get-tuple-element.28), channel_id=1, source_target_pairs={{0,2},{1,3},{2,0},{3,1},{4,7},{5,6},{6,5},{7,4},{8,10},{9,11},{10,... | collective-permute-start | bytes 393224 | tf_op jit(solution)/shard_map/ppermute | solution.py:189
  6.2 13.1 %collective-permute-start = (bf16[64,2048]{1,0:T(8,128)(2,1)S(1)}, bf16[64,2048]{1,0:T(8,128)(2,1)S(1)}, u32[]{:S(2)}, u32[]{:S(2)}) collective-permute-start(bf16[64,2048]{1,0:T(8,128)(2,1)S(1)} %get-tuple-element.27), channel_id=1, source_target_pairs={{0,1},{1,0},{2,3},{3,2},{4,5},{5,4},{6,7},{7,6},{8,9},{9,8},{10,11... | collective-permute-start | bytes 786440 | tf_op jit(solution)/shard_map/ppermute | solution.py:151
  8.7 25.1 %all-to-all-start = ((f16[4,2,128,256]{3,2,1,0:T(8,128)(2,1)}), f16[4,2,128,256]{3,2,1,0:T(8,128)(2,1)S(1)}, u32[]{:S(2)}, u32[]{:S(2)}) async-start(f16[4,2,128,256]{3,2,1,0:T(8,128)(2,1)} %bitcast), calls=%async_computation | async-start | bytes 1048576 | tf_op jit(solution)/shard_map/all_to_all | solution.py:195
  12.2 9.5 %copy-start = (bf16[256,4096]{1,0:T(8,128)(2,1)S(1)}, bf16[256,4096]{1,0:T(8,128)(2,1)}, u32[]{:S(2)}) copy-start(bf16[256,4096]{1,0:T(8,128)(2,1)} %support_ref.3) | copy-start | bytes 6291460
  12.2 13.6 %copy-start.3 = (bf16[64,4096]{1,0:T(8,128)(2,1)S(1)}, bf16[64,4096]{1,0:T(8,128)(2,1)}, u32[]{:S(2)}) copy-start(bf16[64,4096]{1,0:T(8,128)(2,1)} %own_hbm) | copy-start | bytes 1572868
  12.8 7.0 %collective-permute-start.3 = (bf16[64,1024]{1,0:T(8,128)(2,1)S(1)}, bf16[64,1024]{1,0:T(8,128)(2,1)S(1)}, u32[]{:S(2)}, u32[]{:S(2)}) collective-permute-start(bf16[64,1024]{1,0:T(8,128)(2,1)S(1)} %collective-permute-done.2.refs_0_), channel_id=1, source_target_pairs={{0,8},{4,12},{8,0},{12,4},{16,24},{20,28},{24,16},{28,20},{1,9},{5... | collective-permute-start | bytes 393224 | tf_op jit(solution)/shard_map/ppermute | solution.py:151
  14.3 6.1 %collective-permute-start.4 = (bf16[64,1024]{1,0:T(8,128)(2,1)S(1)}, bf16[64,1024]{1,0:T(8,128)(2,1)S(1)}, u32[]{:S(2)}, u32[]{:S(2)}) collective-permute-start(bf16[64,1024]{1,0:T(8,128)(2,1)S(1)} %collective-permute-done.2.refs_0_), channel_id=1, source_target_pairs={{0,16},{4,20},{8,24},{12,28},{16,0},{20,4},{24,8},{28,12},{1,17},{... | collective-permute-start | bytes 393224 | tf_op jit(solution)/shard_map/ppermute | solution.py:151
  15.8 5.9 %collective-permute-start.5 = (bf16[64,1024]{1,0:T(8,128)(2,1)S(1)}, bf16[64,1024]{1,0:T(8,128)(2,1)S(1)}, u32[]{:S(2)}, u32[]{:S(2)}) collective-permute-start(bf16[64,1024]{1,0:T(8,128)(2,1)S(1)} %collective-permute-done.2.refs_0_), channel_id=1, source_target_pairs={{0,24},{4,28},{8,16},{12,20},{16,8},{20,12},{24,0},{28,4},{1,25},{... | collective-permute-start | bytes 393224 | tf_op jit(solution)/shard_map/ppermute | solution.py:151
  19.3 6.5 %collective-permute-start.1 = (bf16[64,2048]{1,0:T(8,128)(2,1)S(1)}, bf16[64,2048]{1,0:T(8,128)(2,1)S(1)}, u32[]{:S(2)}, u32[]{:S(2)}) collective-permute-start(bf16[64,2048]{1,0:T(8,128)(2,1)S(1)} %collective-permute-done.refs_0_), channel_id=1, source_target_pairs={{0,4},{4,0},{8,12},{12,8},{16,20},{20,16},{24,28},{28,24},{1,5},{5... | collective-permute-start | bytes 786440 | tf_op jit(solution)/shard_map/ppermute | solution.py:151
  19.3 3.4 %collective-permute-start.6 = (bf16[64,1024]{1,0:T(8,128)(2,1)S(1)}, bf16[64,1024]{1,0:T(8,128)(2,1)S(1)}, u32[]{:S(2)}, u32[]{:S(2)}) collective-permute-start(bf16[64,1024]{1,0:T(8,128)(2,1)S(1)} %collective-permute-done.2.refs_0_), channel_id=1, source_target_pairs={{0,4},{4,0},{8,12},{12,8},{16,20},{20,16},{24,28},{28,24},{1,5},{5... | collective-permute-start | bytes 393224 | tf_op jit(solution)/shard_map/ppermute | solution.py:151
  19.8 2.9 %collective-permute-start.7 = (bf16[64,1024]{1,0:T(8,128)(2,1)S(1)}, bf16[64,1024]{1,0:T(8,128)(2,1)S(1)}, u32[]{:S(2)}, u32[]{:S(2)}) collective-permute-start(bf16[64,1024]{1,0:T(8,128)(2,1)S(1)} %collective-permute-done.3.refs_1_), channel_id=1, source_target_pairs={{0,4},{4,0},{8,12},{12,8},{16,20},{20,16},{24,28},{28,24},{1,5},{5... | collective-permute-start | bytes 393224 | tf_op jit(solution)/shard_map/ppermute | solution.py:151
  20.4 2.3 %collective-permute-start.8 = (bf16[64,1024]{1,0:T(8,128)(2,1)S(1)}, bf16[64,1024]{1,0:T(8,128)(2,1)S(1)}, u32[]{:S(2)}, u32[]{:S(2)}) collective-permute-start(bf16[64,1024]{1,0:T(8,128)(2,1)S(1)} %collective-permute-done.4.refs_2_), channel_id=1, source_target_pairs={{0,4},{4,0},{8,12},{12,8},{16,20},{20,16},{24,28},{28,24},{1,5},{5... | collective-permute-start | bytes 393224 | tf_op jit(solution)/shard_map/ppermute | solution.py:151
  21.8 1.3 %collective-permute-start.9 = (bf16[64,1024]{1,0:T(8,128)(2,1)S(1)}, bf16[64,1024]{1,0:T(8,128)(2,1)S(1)}, u32[]{:S(2)}, u32[]{:S(2)}) collective-permute-start(bf16[64,1024]{1,0:T(8,128)(2,1)S(1)} %collective-permute-done.5.refs_3_), channel_id=1, source_target_pairs={{0,4},{4,0},{8,12},{12,8},{16,20},{20,16},{24,28},{28,24},{1,5},{5... | collective-permute-start | bytes 393224 | tf_op jit(solution)/shard_map/ppermute | solution.py:151
  23.1 7.4 %collective-permute-start.12 = (f32[64,256]{1,0:T(8,128)S(1)}, f32[64,256]{1,0:T(8,128)S(1)}, u32[]{:S(2)}, u32[]{:S(2)}) collective-permute-start(f32[64,256]{1,0:T(8,128)S(1)} %mine_tile_kernel.1), channel_id=1, source_target_pairs={{0,2},{1,3},{2,0},{3,1},{4,7},{5,6},{6,5},{7,4},{8,10},{9,11},{10,... | collective-permute-start | bytes 196616 | tf_op jit(solution)/shard_map/ppermute | solution.py:241
  26.9 14.2 %copy-start.1 = (f32[2,128,256]{2,1,0:T(8,128)S(1)}, f32[2,128,256]{2,1,0:T(8,128)}, u32[]{:S(2)}) copy-start(f32[2,128,256]{2,1,0:T(8,128)} %own_ref.1) | copy-start | bytes 786436
  26.9 6.9 %collective-permute-start.13 = (f32[64,256]{1,0:T(8,128)S(1)}, f32[64,256]{1,0:T(8,128)S(1)}, u32[]{:S(2)}, u32[]{:S(2)}) collective-permute-start(f32[64,256]{1,0:T(8,128)S(1)} %get-tuple-element.39), channel_id=1, source_target_pairs={{0,3},{1,2},{2,1},{3,0},{4,6},{5,7},{6,4},{7,5},{8,11},{9,10},{10,... | collective-permute-start | bytes 196616 | tf_op jit(solution)/shard_map/ppermute | solution.py:241
  28.5 4.9 %collective-permute-start.10 = (f32[32,256]{1,0:T(8,128)S(1)}, f32[32,256]{1,0:T(8,128)S(1)}, u32[]{:S(2)}, u32[]{:S(2)}) collective-permute-start(f32[32,256]{1,0:T(8,128)S(1)} %get-tuple-element.36), channel_id=1, source_target_pairs={{0,1},{1,0},{2,3},{3,2},{4,5},{5,4},{6,7},{7,6},{8,9},{9,8},{10,11... | collective-permute-start | bytes 98312 | tf_op jit(solution)/shard_map/ppermute | solution.py:151
  28.5 5.3 %collective-permute-start.11 = (f32[32,256]{1,0:T(8,128)S(1)}, f32[32,256]{1,0:T(8,128)S(1)}, u32[]{:S(2)}, u32[]{:S(2)}) collective-permute-start(f32[32,256]{1,0:T(8,128)S(1)} %get-tuple-element.37), channel_id=1, source_target_pairs={{0,1},{1,0},{2,3},{3,2},{4,5},{5,4},{6,7},{7,6},{8,9},{9,8},{10,11... | collective-permute-start | bytes 98312 | tf_op jit(solution)/shard_map/ppermute | solution.py:151
  33.9 1.3 %collective-permute-start.14 = (f32[64,128]{1,0:T(8,128)S(1)}, f32[64,128]{1,0:T(8,128)S(1)}, u32[]{:S(2)}, u32[]{:S(2)}) collective-permute-start(f32[64,128]{1,0:T(8,128)S(1)} %fusion.1.mine_ref), channel_id=1, source_target_pairs={{0,4},{4,0},{8,12},{12,8},{16,20},{20,16},{24,28},{28,24},{1,5},{5... | collective-permute-start | bytes 98312 | tf_op jit(solution)/shard_map/ppermute | solution.py:151
  35.3 5.0 %collective-permute-start.15 = (f32[64,128]{1,0:T(8,128)S(1)}, f32[64,128]{1,0:T(8,128)S(1)}, u32[]{:S(2)}, u32[]{:S(2)}) collective-permute-start(f32[64,128]{1,0:T(8,128)S(1)} %head_kernel.1), channel_id=1, source_target_pairs={{0,24},{1,25},{2,26},{3,27},{4,28},{5,29},{6,30},{7,31},{8,16},{9,... | collective-permute-start | bytes 98312 | tf_op jit(solution)/shard_map/ppermute | solution.py:155
  36.1 4.4 %collective-permute-start.16 = (f32[64,128]{1,0:T(8,128)S(1)}, f32[64,128]{1,0:T(8,128)S(1)}, u32[]{:S(2)}, u32[]{:S(2)}) collective-permute-start(f32[64,128]{1,0:T(8,128)S(1)} %head_kernel.1), channel_id=1, source_target_pairs={{0,16},{1,17},{2,18},{3,19},{4,12},{5,13},{6,14},{7,15},{8,24},{9,... | collective-permute-start | bytes 98312 | tf_op jit(solution)/shard_map/ppermute | solution.py:155
  36.8 3.9 %collective-permute-start.17 = (f32[64,128]{1,0:T(8,128)S(1)}, f32[64,128]{1,0:T(8,128)S(1)}, u32[]{:S(2)}, u32[]{:S(2)}) collective-permute-start(f32[64,128]{1,0:T(8,128)S(1)} %head_kernel.1), channel_id=1, source_target_pairs={{0,8},{1,9},{2,10},{3,11},{4,20},{5,21},{6,22},{7,23},{8,0},{9,1},... | collective-permute-start | bytes 98312 | tf_op jit(solution)/shard_map/ppermute | solution.py:155
  40.8 1.3 %collective-permute-start.18 = (f32[64,128]{1,0:T(8,128)S(1)}, f32[64,128]{1,0:T(8,128)S(1)}, u32[]{:S(2)}, u32[]{:S(2)}) collective-permute-start(f32[64,128]{1,0:T(8,128)S(1)} %select_select_fusion.refs_7_.mine_ref), channel_id=1, source_target_pairs={{0,4},{4,0},{8,12},{12,8},{16,20},{20,16},{24,28},{28,24},{1,5},{5... | collective-permute-start | bytes 98312 | tf_op jit(solution)/shard_map/ppermute | solution.py:151

commit v10 on v7

--- a/solution.py
+++ b/solution.py
@@ -91,9 +91,10 @@
         loads.append((near[part], targets_ref.at[pl.ds(0, rows), cols]))
     wait_all(start_all(loads, sems))
     kernel = jnp.exp(scale * dot(targets_ref[...], support_ref[...], NT))
-    starts = [0, rows // 2, *range(rows, targets_ref.shape[0], rows)]
-    for start, out_ref in zip(starts, outs):
-        out_ref[...] = kernel[start:start + out_ref.shape[0]]
+    pivot = outs[0].shape[1]
+    outs[0][...], outs[1][...] = kernel[:rows, :pivot], kernel[:rows, pivot:]
+    for plane, out_ref in enumerate(outs[2:]):
+        out_ref[...] = kernel[(1 + plane) * rows:(2 + plane) * rows]
 
 
 def plane_offsets(n_col, core):
@@ -117,7 +118,7 @@
 
 def mine_kernel(n_col, *refs):
     tiles, refs = [ref[...] for ref in refs[:n_col + 1]], refs[n_col + 1:]
-    tiles[1:3] = [jnp.concatenate(tiles[1:3], axis=0)]
+    tiles[1:3] = [jnp.concatenate(tiles[1:3], axis=1)]
     own_ref, panels_ref, mine_ref, out_ref = refs
     span = own_ref.shape[2]
     row, col = lax.axis_index("row"), lax.axis_index("col")
@@ -198,13 +199,13 @@
     ]
     other_far = [exchange(piece, "row", n_row, 1) for piece in mine_far]
 
-    def tile_call(body, name, counts, *operands):
+    def tile_call(body, name, widths, *operands):
         pieces = len(operands) - 1
         return list(pl.pallas_call(
             functools.partial(body, scale, n_row),
-            out_shape=[jax.ShapeDtypeStruct((count, span), jnp.float32) for count in counts],
+            out_shape=[jax.ShapeDtypeStruct((rows, width), jnp.float32) for width in widths],
             in_specs=[VMEM if operand is support else HBM for operand in operands],
-            out_specs=[VMEM] * len(counts),
+            out_specs=[VMEM] * len(widths),
             scratch_shapes=[
                 pltpu.VMEM(((1 + len(far)) * rows, features), jnp.bfloat16),
                 pltpu.SemaphoreType.DMA((pieces,)),
@@ -215,11 +216,11 @@
         )(*operands))
 
     first = tile_call(
-        mine_tile_kernel, "mine_tile_kernel", [rows] * (1 + len(far)), targets, support, mark, *mine_far
+        mine_tile_kernel, "mine_tile_kernel", [span] * (1 + len(far)), targets, support, mark, *mine_far
     )
     first[0], *other_far = together(first[0], *other_far)
     last = tile_call(
-        other_tile_kernel, "other_tile_kernel", [rows // 2] * 2 + [rows] * len(far), support, *near, *other_far
+        other_tile_kernel, "other_tile_kernel", [pivot, span - pivot] + [span] * len(far), support, *near, *other_far
     )
     made = [first[0], *last[:2], *first[1:], *last[2:]]
 
@@ -232,7 +233,7 @@
     tiles, blocks = together(tiles, blocks)
     corner = blocks[0, 0, :, :pivot].astype(jnp.float32) * (1 / PANEL_UNIT)
     heads = [tile[:, :pivot] for tile in tiles]
-    heads[1:3] = [jnp.concatenate(heads[1:3], axis=0)]
+    del heads[2]
     head = heads[0]
     for offset, value in zip(plane_offsets(n_col, row % 2)[1:], heads[1:]):
         head = jnp.where(col == offset, value, head)

time: 43.2 us -> 43.2 us (level)
  no operation moved by 1% of the time
where the time goes in v10:
time: 43.2 us; the launch traced here: 42.9 us
  starting transfers between devices  23.8 us (55%)
  waiting for transfers between devices  11.7 us (27%)
  Pallas kernels  4.12 us (10%)
  other arithmetic  2.03 us (5%)
  local copies, waits for them, and re-layouts  1.06 us (2%)
    ppermute x16, starting transfers between devices, exchange(): return lax.ppermute(value, axis, [(i, i ^ mask) for i in range(size)])  11.9 us
    ppermute x16, waiting for transfers between devices, exchange(): return lax.ppermute(value, axis, [(i, i ^ mask) for i in range(size)])  11.3 us
    ppermute x2, starting transfers between devices, shards(): lax.ppermute(tile, ('row', 'col'), [(r * n_col + c, r * n_col + (c ^ 2 *...  4.38 us
    ppermute x1, starting transfers between devices, shards(): lax.ppermute(mine, ('row', 'col'), [(r * n_col + c, r * n_col + (c ^ j +...  4.1 us
    all_to_all x1, starting transfers between devices, shards(): blocks = lax.all_to_all(small, 'col', 0, 0)  3.47 us
    pallas_call x2, Pallas kernels, tile_call(): pl.pallas_call(functools.partial(body, scale, n_row), out_shape=[jax.Shap...  2.06 us
    unnamed x10, local copies, waits for them, and re-layouts  1.06 us
    pallas_call x1, Pallas kernels, shards(): pl.pallas_call(functools.partial(other_kernel, n_col, pivot), out_shape=j...  0.98 us
  transfers between devices with their start and end apart: 20, of which 9 were waited for; matrix products, arithmetic and copies ran while one was open for 5% of the time, Pallas kernels for 7%

profile of v10, /device:TPU:0, one launch (start us, length us, event | category | flops | bytes accessed | tf_op | source)
XLA Modules:
  0.0 42.9 jit_solution(9597364664406041462)
XLA Ops:
  0.0 1.0 %copy-done.2 = bf16[64,4096]{1,0:T(8,128)(2,1)S(1)} copy-done((bf16[64,4096]{1,0:T(8,128)(2,1)S(1)}, bf16[64,4096]{1,0:T(8,128)(2,1)}, u32[]{:S(2)}) %copy-start.2) | copy-done | bytes 524312
  1.1 4.1 %collective-permute-start = (bf16[64,1024]{1,0:T(8,128)(2,1)S(1)}, bf16[64,1024]{1,0:T(8,128)(2,1)S(1)}, u32[]{:S(2)}, u32[]{:S(2)}) collective-permute-start(bf16[64,1024]{1,0:T(8,128)(2,1)S(1)} %get-tuple-element.25), channel_id=1, source_target_pairs={{0,2},{1,3},{2,0},{3,1},{4,7},{5,6},{6,5},{7,4},{8,10},{9,11},{10,... | collective-permute-start | bytes 393224 | tf_op jit(solution)/shard_map/ppermute | solution.py:177
  5.2 1.6 %collective-permute-start.8 = (bf16[64,2048]{1,0:T(8,128)(2,1)S(1)}, bf16[64,2048]{1,0:T(8,128)(2,1)S(1)}, u32[]{:S(2)}, u32[]{:S(2)}) collective-permute-start(bf16[64,2048]{1,0:T(8,128)(2,1)S(1)} %get-tuple-element.30), channel_id=1, source_target_pairs={{0,1},{1,0},{2,3},{3,2},{4,5},{5,4},{6,7},{7,6},{8,9},{9,8},{10,11... | collective-permute-start | bytes 786440 | tf_op jit(solution)/shard_map/ppermute | solution.py:147
  6.8 1.0 %multiply_convert_fusion = f16[2,128,256]{2,1,0:T(8,128)(2,1)S(1)} fusion(f32[2,128,256]{2,1,0:T(8,128)} %own_ref.1), kind=kLoop, calls=%fused_computation.2 | loop fusion | flops 131072 | bytes 393216 | tf_op jit(solution)/shard_map/convert
  7.8 0.9 %pad_maximum_fusion = f16[8,128,256]{2,1,0:T(8,128)(2,1)} fusion(f16[2,128,256]{2,1,0:T(8,128)(2,1)S(1)} %multiply_convert_fusion), kind=kLoop, calls=%fused_computation.1 | loop fusion | flops 786432 | bytes 655360 | tf_op jit(solution)/shard_map/concatenate | solution.py:182
  8.7 3.5 %all-to-all-start = ((f16[4,2,128,256]{3,2,1,0:T(8,128)(2,1)}), f16[4,2,128,256]{3,2,1,0:T(8,128)(2,1)S(1)}, u32[]{:S(2)}, u32[]{:S(2)}) async-start(f16[4,2,128,256]{3,2,1,0:T(8,128)(2,1)} %bitcast), calls=%async_computation | async-start | bytes 1048576 | tf_op jit(solution)/shard_map/all_to_all | solution.py:184
  12.2 1.6 %collective-permute-start.1 = (bf16[64,1024]{1,0:T(8,128)(2,1)S(1)}, bf16[64,1024]{1,0:T(8,128)(2,1)S(1)}, u32[]{:S(2)}, u32[]{:S(2)}) collective-permute-start(bf16[64,1024]{1,0:T(8,128)(2,1)S(1)} %collective-permute-done.refs_0_), channel_id=1, source_target_pairs={{0,8},{4,12},{8,0},{12,4},{16,24},{20,28},{24,16},{28,20},{1,9},{5... | collective-permute-start | bytes 393224 | tf_op jit(solution)/shard_map/ppermute | solution.py:147
  13.8 1.5 %collective-permute-start.2 = (bf16[64,1024]{1,0:T(8,128)(2,1)S(1)}, bf16[64,1024]{1,0:T(8,128)(2,1)S(1)}, u32[]{:S(2)}, u32[]{:S(2)}) collective-permute-start(bf16[64,1024]{1,0:T(8,128)(2,1)S(1)} %collective-permute-done.refs_0_), channel_id=1, source_target_pairs={{0,16},{4,20},{8,24},{12,28},{16,0},{20,4},{24,8},{28,12},{1,17},{... | collective-permute-start | bytes 393224 | tf_op jit(solution)/shard_map/ppermute | solution.py:147
  15.3 0.5 %collective-permute-start.3 = (bf16[64,1024]{1,0:T(8,128)(2,1)S(1)}, bf16[64,1024]{1,0:T(8,128)(2,1)S(1)}, u32[]{:S(2)}, u32[]{:S(2)}) collective-permute-start(bf16[64,1024]{1,0:T(8,128)(2,1)S(1)} %collective-permute-done.refs_0_), channel_id=1, source_target_pairs={{0,24},{4,28},{8,16},{12,20},{16,8},{20,12},{24,0},{28,4},{1,25},{... | collective-permute-start | bytes 393224 | tf_op jit(solution)/shard_map/ppermute | solution.py:147
  15.8 0.5 %collective-permute-start.4 = (bf16[64,1024]{1,0:T(8,128)(2,1)S(1)}, bf16[64,1024]{1,0:T(8,128)(2,1)S(1)}, u32[]{:S(2)}, u32[]{:S(2)}) collective-permute-start(bf16[64,1024]{1,0:T(8,128)(2,1)S(1)} %collective-permute-done.refs_0_), channel_id=1, source_target_pairs={{0,4},{4,0},{8,12},{12,8},{16,20},{20,16},{24,28},{28,24},{1,5},{5... | collective-permute-start | bytes 393224 | tf_op jit(solution)/shard_map/ppermute | solution.py:147
  16.3 2.0 %collective-permute-done.1.refs_1_ = bf16[64,1024]{1,0:T(8,128)(2,1)S(1)} collective-permute-done((bf16[64,1024]{1,0:T(8,128)(2,1)S(1)}, bf16[64,1024]{1,0:T(8,128)(2,1)S(1)}, u32[]{:S(2)}, u32[]{:S(2)}) %collective-permute-start.1) | collective-permute-done | bytes 131104 | tf_op jit(solution)/shard_map/ppermute | solution.py:147
  18.3 3.1 %collective-permute-done.2.refs_2_ = bf16[64,1024]{1,0:T(8,128)(2,1)S(1)} collective-permute-done((bf16[64,1024]{1,0:T(8,128)(2,1)S(1)}, bf16[64,1024]{1,0:T(8,128)(2,1)S(1)}, u32[]{:S(2)}, u32[]{:S(2)}) %collective-permute-start.2) | collective-permute-done | bytes 131104 | tf_op jit(solution)/shard_map/ppermute | solution.py:147
  21.5 0.5 %collective-permute-start.7 = (bf16[64,1024]{1,0:T(8,128)(2,1)S(1)}, bf16[64,1024]{1,0:T(8,128)(2,1)S(1)}, u32[]{:S(2)}, u32[]{:S(2)}) collective-permute-start(bf16[64,1024]{1,0:T(8,128)(2,1)S(1)} %collective-permute-done.3.refs_3_), channel_id=1, source_target_pairs={{0,4},{4,0},{8,12},{12,8},{16,20},{20,16},{24,28},{28,24},{1,5},{5... | collective-permute-start | bytes 393224 | tf_op jit(solution)/shard_map/ppermute | solution.py:147
  22.0 1.0 %mine_tile_kernel.1 = (f32[64,256]{1,0:T(8,128)S(1)}, f32[64,256]{1,0:T(8,128)S(1)}) custom-call(bf16[64,4096]{1,0:T(8,128)(2,1)S(1)} %copy-done.3, bf16[256,4096]{1,0:T(8,128)(2,1)S(1)} %copy-done, f32[8,128]{1,0:T(8,128)S(1)} %mark_kernel.1._, bf16[64,1024]{1,0:T(8,128)(2,1)S(1)} %collective-permute-done.refs_0_, ...), custom_call_target="tpu_custom_call" | custom-call | flops 1000000 | tf_op jit(solution)/shard_map/mine_tile_kernel/pallas_call | solution.py:204
  23.0 2.8 %collective-permute-start.12 = (f32[64,256]{1,0:T(8,128)S(1)}, f32[64,256]{1,0:T(8,128)S(1)}, u32[]{:S(2)}, u32[]{:S(2)}) collective-permute-start(f32[64,256]{1,0:T(8,128)S(1)} %get-tuple-element.37), channel_id=1, source_target_pairs={{0,2},{1,3},{2,0},{3,1},{4,7},{5,6},{6,5},{7,4},{8,10},{9,11},{10,... | collective-permute-start | bytes 196616 | tf_op jit(solution)/shard_map/ppermute | solution.py:230
  25.9 1.0 %other_tile_kernel.1 = (f32[64,128]{1,0:T(8,128)S(1)}, f32[64,128]{1,0:T(8,128)S(1)}, f32[64,256]{1,0:T(8,128)S(1)}) custom-call(bf16[256,4096]{1,0:T(8,128)(2,1)S(1)} %copy-done, bf16[64,2048]{1,0:T(8,128)(2,1)S(1)} %collective-permute-done.8.refs_0_, bf16[64,2048]{1,0:T(8,128)(2,1)S(1)} %collective-permute-done.9.refs_1_, ...), custom_call_target="tpu_custom_call" | custom-call | flops 1000000 | tf_op jit(solution)/shard_map/other_tile_kernel/pallas_call | solution.py:204
  26.9 1.6 %collective-permute-start.13 = (f32[64,256]{1,0:T(8,128)S(1)}, f32[64,256]{1,0:T(8,128)S(1)}, u32[]{:S(2)}, u32[]{:S(2)}) collective-permute-start(f32[64,256]{1,0:T(8,128)S(1)} %get-tuple-element.38), channel_id=1, source_target_pairs={{0,3},{1,2},{2,1},{3,0},{4,6},{5,7},{6,4},{7,5},{8,11},{9,10},{10,... | collective-permute-start | bytes 196616 | tf_op jit(solution)/shard_map/ppermute | solution.py:230
  28.5 2.0 %collective-permute-start.11 = (f32[64,128]{1,0:T(8,128)S(1)}, f32[64,128]{1,0:T(8,128)S(1)}, u32[]{:S(2)}, u32[]{:S(2)}) collective-permute-start(f32[64,128]{1,0:T(8,128)S(1)} %get-tuple-element.36), channel_id=1, source_target_pairs={{0,1},{1,0},{2,3},{3,2},{4,5},{5,4},{6,7},{7,6},{8,9},{9,8},{10,11... | collective-permute-start | bytes 98312 | tf_op jit(solution)/shard_map/ppermute | solution.py:147
  30.5 2.1 %collective-permute-done.10.refs_1_ = f32[64,128]{1,0:T(8,128)S(1)} collective-permute-done((f32[64,128]{1,0:T(8,128)S(1)}, f32[64,128]{1,0:T(8,128)S(1)}, u32[]{:S(2)}, u32[]{:S(2)}) %collective-permute-start.10) | collective-permute-done | bytes 32800 | tf_op jit(solution)/shard_map/ppermute | solution.py:147
  32.6 0.7 %collective-permute-done.11.refs_2_ = f32[64,128]{1,0:T(8,128)S(1)} collective-permute-done((f32[64,128]{1,0:T(8,128)S(1)}, f32[64,128]{1,0:T(8,128)S(1)}, u32[]{:S(2)}, u32[]{:S(2)}) %collective-permute-start.11) | collective-permute-done | bytes 32800 | tf_op jit(solution)/shard_map/ppermute | solution.py:147
  33.3 0.4 collective-permute-done.13.refs_4_
  33.8 0.2 base_kernel.1.base_ref
  34.0 0.4 mix_kernel.1.mix_ref
  34.4 0.6 %collective-permute-done.14.other_ref = f32[64,128]{1,0:T(8,128)S(1)} collective-permute-done((f32[64,128]{1,0:T(8,128)S(1)}, f32[64,128]{1,0:T(8,128)S(1)}, u32[]{:S(2)}, u32[]{:S(2)}) %collective-permute-start.14) | collective-permute-done | bytes 32800 | tf_op jit(solution)/shard_map/ppermute | solution.py:147
  35.2 0.7 %collective-permute-start.15 = (f32[64,128]{1,0:T(8,128)S(1)}, f32[64,128]{1,0:T(8,128)S(1)}, u32[]{:S(2)}, u32[]{:S(2)}) collective-permute-start(f32[64,128]{1,0:T(8,128)S(1)} %head_kernel.1), channel_id=1, source_target_pairs={{0,24},{4,28},{8,16},{12,20},{16,8},{20,12},{24,0},{28,4},{1,25},{... | collective-permute-start | bytes 98312 | tf_op jit(solution)/shard_map/ppermute | solution.py:147
  35.9 0.9 %collective-permute-start.16 = (f32[64,128]{1,0:T(8,128)S(1)}, f32[64,128]{1,0:T(8,128)S(1)}, u32[]{:S(2)}, u32[]{:S(2)}) collective-permute-start(f32[64,128]{1,0:T(8,128)S(1)} %head_kernel.1), channel_id=1, source_target_pairs={{0,16},{4,20},{8,24},{12,28},{16,0},{20,4},{24,8},{28,12},{1,17},{... | collective-permute-start | bytes 98312 | tf_op jit(solution)/shard_map/ppermute | solution.py:147
  36.8 2.0 %collective-permute-start.17 = (f32[64,128]{1,0:T(8,128)S(1)}, f32[64,128]{1,0:T(8,128)S(1)}, u32[]{:S(2)}, u32[]{:S(2)}) collective-permute-start(f32[64,128]{1,0:T(8,128)S(1)} %head_kernel.1), channel_id=1, source_target_pairs={{0,8},{4,12},{8,0},{12,4},{16,24},{20,28},{24,16},{28,20},{1,9},{5... | collective-permute-start | bytes 98312 | tf_op jit(solution)/shard_map/ppermute | solution.py:147
  38.7 1.6 %collective-permute-done.15 = f32[64,128]{1,0:T(8,128)S(1)} collective-permute-done((f32[64,128]{1,0:T(8,128)S(1)}, f32[64,128]{1,0:T(8,128)S(1)}, u32[]{:S(2)}, u32[]{:S(2)}) %collective-permute-start.15) | collective-permute-done | bytes 32800 | tf_op jit(solution)/shard_map/ppermute | solution.py:147
  40.3 0.3 collective-permute-done.17
  40.9 0.3 mine_kernel.1.part_ref
  41.2 0.8 %collective-permute-done.18.other_ref = f32[64,128]{1,0:T(8,128)S(1)} collective-permute-done((f32[64,128]{1,0:T(8,128)S(1)}, f32[64,128]{1,0:T(8,128)S(1)}, u32[]{:S(2)}, u32[]{:S(2)}) %collective-permute-start.18) | collective-permute-done | bytes 32800 | tf_op jit(solution)/shard_map/ppermute | solution.py:147
  42.0 1.0 %other_kernel.1 = f32[64,1024]{1,0:T(8,128)} custom-call(f32[64,1024]{1,0:T(8,128)S(1)} %mine_kernel.1.part_ref, f32[2,128,256]{2,1,0:T(8,128)S(1)} %copy-done.1, f32[4,2,128,256]{3,2,1,0:T(8,128)S(1)} %convert_multiply_fusion.refs_6_.panels_ref, f32[64,128]{1,0:T(8,128)S(1)} %select_select_fusion.refs_7_.mine_ref, ...), custom_call_target="tpu_custom_call" | custom-call | flops 1000000 | tf_op jit(solution)/shard_map/other_kernel/pallas_call | solution.py:282
  (33 shorter events, 0.6 us)
Async XLA Ops:
  0.0 1.0 %copy-start.2 = (bf16[64,4096]{1,0:T(8,128)(2,1)S(1)}, bf16[64,4096]{1,0:T(8,128)(2,1)}, u32[]{:S(2)}) copy-start(bf16[64,4096]{1,0:T(8,128)(2,1)} %own_hbm.1) | copy-start | bytes 1572868
  1.0 11.1 %copy-start.4 = (f32[2,128,128]{2,1,0:T(8,128)S(1)}, f32[2,128,128]{2,1,0:T(8,128)}, u32[]{:S(2)}) copy-start(f32[2,128,128]{2,1,0:T(8,128)} %inverse_ref.3) | copy-start | bytes 393220
  1.1 11.1 %collective-permute-start = (bf16[64,1024]{1,0:T(8,128)(2,1)S(1)}, bf16[64,1024]{1,0:T(8,128)(2,1)S(1)}, u32[]{:S(2)}, u32[]{:S(2)}) collective-permute-start(bf16[64,1024]{1,0:T(8,128)(2,1)S(1)} %get-tuple-element.25), channel_id=1, source_target_pairs={{0,2},{1,3},{2,0},{3,1},{4,7},{5,6},{6,5},{7,4},{8,10},{9,11},{10,... | collective-permute-start | bytes 393224 | tf_op jit(solution)/shard_map/ppermute | solution.py:177
  5.2 10.6 %collective-permute-start.8 = (bf16[64,2048]{1,0:T(8,128)(2,1)S(1)}, bf16[64,2048]{1,0:T(8,128)(2,1)S(1)}, u32[]{:S(2)}, u32[]{:S(2)}) collective-permute-start(bf16[64,2048]{1,0:T(8,128)(2,1)S(1)} %get-tuple-element.30), channel_id=1, source_target_pairs={{0,1},{1,0},{2,3},{3,2},{4,5},{5,4},{6,7},{7,6},{8,9},{9,8},{10,11... | collective-permute-start | bytes 786440 | tf_op jit(solution)/shard_map/ppermute | solution.py:147
  8.7 25.0 %all-to-all-start = ((f16[4,2,128,256]{3,2,1,0:T(8,128)(2,1)}), f16[4,2,128,256]{3,2,1,0:T(8,128)(2,1)S(1)}, u32[]{:S(2)}, u32[]{:S(2)}) async-start(f16[4,2,128,256]{3,2,1,0:T(8,128)(2,1)} %bitcast), calls=%async_computation | async-start | bytes 1048576 | tf_op jit(solution)/shard_map/all_to_all | solution.py:184
  12.2 9.8 %copy-start = (bf16[256,4096]{1,0:T(8,128)(2,1)S(1)}, bf16[256,4096]{1,0:T(8,128)(2,1)}, u32[]{:S(2)}) copy-start(bf16[256,4096]{1,0:T(8,128)(2,1)} %support_ref.3) | copy-start | bytes 6291460
  12.2 9.8 %copy-start.3 = (bf16[64,4096]{1,0:T(8,128)(2,1)S(1)}, bf16[64,4096]{1,0:T(8,128)(2,1)}, u32[]{:S(2)}) copy-start(bf16[64,4096]{1,0:T(8,128)(2,1)} %own_hbm.1) | copy-start | bytes 1572868
  12.2 6.1 %collective-permute-start.1 = (bf16[64,1024]{1,0:T(8,128)(2,1)S(1)}, bf16[64,1024]{1,0:T(8,128)(2,1)S(1)}, u32[]{:S(2)}, u32[]{:S(2)}) collective-permute-start(bf16[64,1024]{1,0:T(8,128)(2,1)S(1)} %collective-permute-done.refs_0_), channel_id=1, source_target_pairs={{0,8},{4,12},{8,0},{12,4},{16,24},{20,28},{24,16},{28,20},{1,9},{5... | collective-permute-start | bytes 393224 | tf_op jit(solution)/shard_map/ppermute | solution.py:147
  13.8 7.7 %collective-permute-start.2 = (bf16[64,1024]{1,0:T(8,128)(2,1)S(1)}, bf16[64,1024]{1,0:T(8,128)(2,1)S(1)}, u32[]{:S(2)}, u32[]{:S(2)}) collective-permute-start(bf16[64,1024]{1,0:T(8,128)(2,1)S(1)} %collective-permute-done.refs_0_), channel_id=1, source_target_pairs={{0,16},{4,20},{8,24},{12,28},{16,0},{20,4},{24,8},{28,12},{1,17},{... | collective-permute-start | bytes 393224 | tf_op jit(solution)/shard_map/ppermute | solution.py:147
  15.3 6.2 %collective-permute-start.3 = (bf16[64,1024]{1,0:T(8,128)(2,1)S(1)}, bf16[64,1024]{1,0:T(8,128)(2,1)S(1)}, u32[]{:S(2)}, u32[]{:S(2)}) collective-permute-start(bf16[64,1024]{1,0:T(8,128)(2,1)S(1)} %collective-permute-done.refs_0_), channel_id=1, source_target_pairs={{0,24},{4,28},{8,16},{12,20},{16,8},{20,12},{24,0},{28,4},{1,25},{... | collective-permute-start | bytes 393224 | tf_op jit(solution)/shard_map/ppermute | solution.py:147
  15.8 10.1 %collective-permute-start.9 = (bf16[64,2048]{1,0:T(8,128)(2,1)S(1)}, bf16[64,2048]{1,0:T(8,128)(2,1)S(1)}, u32[]{:S(2)}, u32[]{:S(2)}) collective-permute-start(bf16[64,2048]{1,0:T(8,128)(2,1)S(1)} %collective-permute-done.8.refs_0_), channel_id=1, source_target_pairs={{0,4},{4,0},{8,12},{12,8},{16,20},{20,16},{24,28},{28,24},{1,5},{5... | collective-permute-start | bytes 786440 | tf_op jit(solution)/shard_map/ppermute | solution.py:147
  15.8 7.2 %collective-permute-start.4 = (bf16[64,1024]{1,0:T(8,128)(2,1)S(1)}, bf16[64,1024]{1,0:T(8,128)(2,1)S(1)}, u32[]{:S(2)}, u32[]{:S(2)}) collective-permute-start(bf16[64,1024]{1,0:T(8,128)(2,1)S(1)} %collective-permute-done.refs_0_), channel_id=1, source_target_pairs={{0,4},{4,0},{8,12},{12,8},{16,20},{20,16},{24,28},{28,24},{1,5},{5... | collective-permute-start | bytes 393224 | tf_op jit(solution)/shard_map/ppermute | solution.py:147
  18.3 7.5 %collective-permute-start.5 = (bf16[64,1024]{1,0:T(8,128)(2,1)S(1)}, bf16[64,1024]{1,0:T(8,128)(2,1)S(1)}, u32[]{:S(2)}, u32[]{:S(2)}) collective-permute-start(bf16[64,1024]{1,0:T(8,128)(2,1)S(1)} %collective-permute-done.1.refs_1_), channel_id=1, source_target_pairs={{0,4},{4,0},{8,12},{12,8},{16,20},{20,16},{24,28},{28,24},{1,5},{5... | collective-permute-start | bytes 393224 | tf_op jit(solution)/shard_map/ppermute | solution.py:147
  21.5 4.4 %collective-permute-start.6 = (bf16[64,1024]{1,0:T(8,128)(2,1)S(1)}, bf16[64,1024]{1,0:T(8,128)(2,1)S(1)}, u32[]{:S(2)}, u32[]{:S(2)}) collective-permute-start(bf16[64,1024]{1,0:T(8,128)(2,1)S(1)} %collective-permute-done.2.refs_2_), channel_id=1, source_target_pairs={{0,4},{4,0},{8,12},{12,8},{16,20},{20,16},{24,28},{28,24},{1,5},{5... | collective-permute-start | bytes 393224 | tf_op jit(solution)/shard_map/ppermute | solution.py:147
  21.5 4.4 %collective-permute-start.7 = (bf16[64,1024]{1,0:T(8,128)(2,1)S(1)}, bf16[64,1024]{1,0:T(8,128)(2,1)S(1)}, u32[]{:S(2)}, u32[]{:S(2)}) collective-permute-start(bf16[64,1024]{1,0:T(8,128)(2,1)S(1)} %collective-permute-done.3.refs_3_), channel_id=1, source_target_pairs={{0,4},{4,0},{8,12},{12,8},{16,20},{20,16},{24,28},{28,24},{1,5},{5... | collective-permute-start | bytes 393224 | tf_op jit(solution)/shard_map/ppermute | solution.py:147
  23.0 7.5 %collective-permute-start.12 = (f32[64,256]{1,0:T(8,128)S(1)}, f32[64,256]{1,0:T(8,128)S(1)}, u32[]{:S(2)}, u32[]{:S(2)}) collective-permute-start(f32[64,256]{1,0:T(8,128)S(1)} %get-tuple-element.37), channel_id=1, source_target_pairs={{0,2},{1,3},{2,0},{3,1},{4,7},{5,6},{6,5},{7,4},{8,10},{9,11},{10,... | collective-permute-start | bytes 196616 | tf_op jit(solution)/shard_map/ppermute | solution.py:230
  26.9 14.0 %copy-start.1 = (f32[2,128,256]{2,1,0:T(8,128)S(1)}, f32[2,128,256]{2,1,0:T(8,128)}, u32[]{:S(2)}) copy-start(f32[2,128,256]{2,1,0:T(8,128)} %own_ref.1) | copy-start | bytes 786436
  26.9 6.8 %collective-permute-start.13 = (f32[64,256]{1,0:T(8,128)S(1)}, f32[64,256]{1,0:T(8,128)S(1)}, u32[]{:S(2)}, u32[]{:S(2)}) collective-permute-start(f32[64,256]{1,0:T(8,128)S(1)} %get-tuple-element.38), channel_id=1, source_target_pairs={{0,3},{1,2},{2,1},{3,0},{4,6},{5,7},{6,4},{7,5},{8,11},{9,10},{10,... | collective-permute-start | bytes 196616 | tf_op jit(solution)/shard_map/ppermute | solution.py:230
  28.5 4.1 %collective-permute-start.10 = (f32[64,128]{1,0:T(8,128)S(1)}, f32[64,128]{1,0:T(8,128)S(1)}, u32[]{:S(2)}, u32[]{:S(2)}) collective-permute-start(f32[64,128]{1,0:T(8,128)S(1)} %get-tuple-element.35), channel_id=1, source_target_pairs={{0,1},{1,0},{2,3},{3,2},{4,5},{5,4},{6,7},{7,6},{8,9},{9,8},{10,11... | collective-permute-start | bytes 98312 | tf_op jit(solution)/shard_map/ppermute | solution.py:147
  28.5 4.8 %collective-permute-start.11 = (f32[64,128]{1,0:T(8,128)S(1)}, f32[64,128]{1,0:T(8,128)S(1)}, u32[]{:S(2)}, u32[]{:S(2)}) collective-permute-start(f32[64,128]{1,0:T(8,128)S(1)} %get-tuple-element.36), channel_id=1, source_target_pairs={{0,1},{1,0},{2,3},{3,2},{4,5},{5,4},{6,7},{7,6},{8,9},{9,8},{10,11... | collective-permute-start | bytes 98312 | tf_op jit(solution)/shard_map/ppermute | solution.py:147
  33.7 1.3 %collective-permute-start.14 = (f32[64,128]{1,0:T(8,128)S(1)}, f32[64,128]{1,0:T(8,128)S(1)}, u32[]{:S(2)}, u32[]{:S(2)}) collective-permute-start(f32[64,128]{1,0:T(8,128)S(1)} %select_select_fusion.1.mine_ref), channel_id=1, source_target_pairs={{0,4},{4,0},{8,12},{12,8},{16,20},{20,16},{24,28},{28,24},{1,5},{5... | collective-permute-start | bytes 98312 | tf_op jit(solution)/shard_map/ppermute | solution.py:147
  35.2 5.2 %collective-permute-start.15 = (f32[64,128]{1,0:T(8,128)S(1)}, f32[64,128]{1,0:T(8,128)S(1)}, u32[]{:S(2)}, u32[]{:S(2)}) collective-permute-start(f32[64,128]{1,0:T(8,128)S(1)} %head_kernel.1), channel_id=1, source_target_pairs={{0,24},{4,28},{8,16},{12,20},{16,8},{20,12},{24,0},{28,4},{1,25},{... | collective-permute-start | bytes 98312 | tf_op jit(solution)/shard_map/ppermute | solution.py:147
  35.9 4.5 %collective-permute-start.16 = (f32[64,128]{1,0:T(8,128)S(1)}, f32[64,128]{1,0:T(8,128)S(1)}, u32[]{:S(2)}, u32[]{:S(2)}) collective-permute-start(f32[64,128]{1,0:T(8,128)S(1)} %head_kernel.1), channel_id=1, source_target_pairs={{0,16},{4,20},{8,24},{12,28},{16,0},{20,4},{24,8},{28,12},{1,17},{... | collective-permute-start | bytes 98312 | tf_op jit(solution)/shard_map/ppermute | solution.py:147
  36.8 3.9 %collective-permute-start.17 = (f32[64,128]{1,0:T(8,128)S(1)}, f32[64,128]{1,0:T(8,128)S(1)}, u32[]{:S(2)}, u32[]{:S(2)}) collective-permute-start(f32[64,128]{1,0:T(8,128)S(1)} %head_kernel.1), channel_id=1, source_target_pairs={{0,8},{4,12},{8,0},{12,4},{16,24},{20,28},{24,16},{28,20},{1,9},{5... | collective-permute-start | bytes 98312 | tf_op jit(solution)/shard_map/ppermute | solution.py:147
  40.7 1.3 %collective-permute-start.18 = (f32[64,128]{1,0:T(8,128)S(1)}, f32[64,128]{1,0:T(8,128)S(1)}, u32[]{:S(2)}, u32[]{:S(2)}) collective-permute-start(f32[64,128]{1,0:T(8,128)S(1)} %select_select_fusion.refs_7_.mine_ref), channel_id=1, source_target_pairs={{0,4},{4,0},{8,12},{12,8},{16,20},{20,16},{24,28},{28,24},{1,5},{5... | collective-permute-start | bytes 98312 | tf_op jit(solution)/shard_map/ppermute | solution.py:147
